TPU v7x, 32 devices: a whole 2x2x4 slice. The times are simulated.
32 devices in a mesh: dp: 8 (over y, x, core), ffn: 4 (over z).
Axes of the slice: x: 2, y: 2, z: 4, core: 2. Of those that a mesh axis runs over, the one named last changes fastest.
Arguments:
- block_input: bfloat16 [32768, 1024], P(('dp', 'ffn')), may hold values from -6 to 6
- cotangent: bfloat16 [32768, 1024], P(('dp', 'ffn')), may hold values from -6 to 6
- w_qkv: float32 [1024, 3072], P(None, ('dp', 'ffn')), may hold values from -0.1875 to 0.1875
- w_out: float32 [1024, 1024], P(None, ('dp', 'ffn')), may hold values from -0.5 to 0.5
- w_up: float32 [1024, 4096], P(None, ('dp', 'ffn')), may hold values from -0.1875 to 0.1875
- w_down: float32 [4096, 1024], P(('dp', 'ffn')), may hold values from -0.09375 to 0.09375
- vectors: float32 [8, 1024], P(None, ('dp', 'ffn')), may hold values from -0.6 to 1.6
- b_up: float32 [4096], P(('dp', 'ffn')), may hold values from -1.8 to 1.8
- qkv_left: float32 [1024, 1024], P(('dp', 'ffn')), may hold values from -100663296 to 402653184
- qkv_right: float32 [3072, 3072], P(('dp', 'ffn')), may hold values from -33554432 to 134217728
- out_left: float32 [1024, 1024], P(('dp', 'ffn')), may hold values from -5368709 to 21474836
- out_right: float32 [1024, 1024], P(('dp', 'ffn')), may hold values from -5368709 to 21474836
- up_left: float32 [1024, 1024], P(('dp', 'ffn')), may hold values from -12079596 to 48318382
- up_right: float32 [4096, 4096], P(('dp', 'ffn')), may hold values from -3019899 to 12079596
- down_left: float32 [4096, 4096], P(('dp', 'ffn')), may hold values from -14176748 to 5.670699e+07
- down_right: float32 [1024, 1024], P(('dp', 'ffn')), may hold values from -5.670699e+07 to 2.2682796e+08
- qkv_left_root: float32 [1024, 1024], P(('dp', 'ffn')), may hold values from -0.009983486 to 0.039933944
- qkv_right_root: float32 [3072, 3072], P(('dp', 'ffn')), may hold values from -0.0131390065 to 0.052556026
- out_left_root: float32 [1024, 1024], P(('dp', 'ffn')), may hold values from -0.020774593 to 0.083098373
- out_right_root: float32 [1024, 1024], P(('dp', 'ffn')), may hold values from -0.020774593 to 0.083098373
- up_left_root: float32 [1024, 1024], P(('dp', 'ffn')), may hold values from -0.016962384 to 0.06784954
- up_right_root: float32 [4096, 4096], P(('dp', 'ffn')), may hold values from -0.023988434122900557 to 0.09595374
- down_left_root: float32 [4096, 4096], P(('dp', 'ffn')), may hold values from -0.016296932 to 0.06518773
- down_right_root: float32 [1024, 1024], P(('dp', 'ffn')), may hold values from -0.011523671 to 0.046094684
- vector_stat: float32 [8, 1024], P(None, ('dp', 'ffn')), may hold values from 16384 to 65536
- b_up_stat: float32 [4096], P(('dp', 'ffn')), may hold values from 2949.12 to 11796.48
Outputs:
- block_output: bfloat16 [32768, 1024], P(('dp', 'ffn'))
- input_grad: bfloat16 [32768, 1024], P(('dp', 'ffn'))
- qkv_grad: float32 [1024, 3072], P(None, ('dp', 'ffn'))
- out_grad: float32 [1024, 1024], P(None, ('dp', 'ffn'))
- up_grad: float32 [1024, 4096], P(None, ('dp', 'ffn'))
- down_grad: float32 [4096, 1024], P(('dp', 'ffn'))
- vector_grad: float32 [8, 1024], P(None, ('dp', 'ffn'))
- b_up_grad: float32 [4096], P(('dp', 'ffn'))
- new_qkv_left: float32 [1024, 1024], P(('dp', 'ffn'))
- new_qkv_right: float32 [3072, 3072], P(('dp', 'ffn'))
- new_out_left: float32 [1024, 1024], P(('dp', 'ffn'))
- new_out_right: float32 [1024, 1024], P(('dp', 'ffn'))
- new_up_left: float32 [1024, 1024], P(('dp', 'ffn'))
- new_up_right: float32 [4096, 4096], P(('dp', 'ffn'))
- new_down_left: float32 [4096, 4096], P(('dp', 'ffn'))
- new_down_right: float32 [1024, 1024], P(('dp', 'ffn'))
- new_vector_stat: float32 [8, 1024], P(None, ('dp', 'ffn'))
- new_b_up_stat: float32 [4096], P(('dp', 'ffn'))
- new_w_qkv: float32 [1024, 3072], P(None, ('dp', 'ffn'))
- new_w_out: float32 [1024, 1024], P(None, ('dp', 'ffn'))
- new_w_up: float32 [1024, 4096], P(None, ('dp', 'ffn'))
- new_w_down: float32 [4096, 1024], P(('dp', 'ffn'))
- new_vectors: float32 [8, 1024], P(None, ('dp', 'ffn'))
- new_b_up: float32 [4096], P(('dp', 'ffn'))
All inputs are finite; a program needn't handle non-finite values.
Results may differ from a plain program's by a relative error of at most 0.025.
Values may be sent and summed in bfloat16 or wider, within the bound.
A program may use at most 448 MiB of HBM per device.

v0:
```python
import jax
import jax.numpy as jnp
from jax import lax
from jax.sharding import PartitionSpec as P

D = 1024
HEADS = 8
HEAD_DIM = 128


norm_epsilon = 1e-05
decay_rate = 0.5
matrix_rate = 0.5
vector_rate = 0.1
masked_score = -1e30


def layer_norm(values, gain, shift):
    center = values - jnp.mean(values, axis=-1, keepdims=True)
    inverse = lax.rsqrt(jnp.mean(center * center, axis=-1, keepdims=True) + norm_epsilon)
    normed = center * inverse
    return (normed * gain + shift, normed, inverse)


def norm_backward(grad, normed, inverse, gain):
    scaled = grad * gain
    inner = (
        scaled
        - jnp.mean(scaled, axis=-1, keepdims=True)
        - normed * jnp.mean(scaled * normed, axis=-1, keepdims=True)
    )
    return (inner * inverse, jnp.sum(grad * normed, axis=0), jnp.sum(grad, axis=0))


def gelu_slope(pre):
    return (
        0.5 * (1.0 + lax.erf(pre * 0.7071067811865476))
        + pre * jnp.exp(-0.5 * pre * pre) * 0.3989422804014327
    )


def alibi_scores(query_block, keys, start):
    raw = jnp.einsum("qhd,khd->hqk", query_block, keys, preferred_element_type=jnp.float32)
    shape = (query_block.shape[0], keys.shape[0])
    rows = start + lax.broadcasted_iota(jnp.int32, shape, 0)
    cols = lax.broadcasted_iota(jnp.int32, shape, 1)
    slopes = 2.0 ** (-8.0 * (jnp.arange(HEADS).astype(jnp.float32) + 1.0) / HEADS)
    distance = (rows - cols).astype(jnp.float32)
    scores = raw * HEAD_DIM ** (-0.5) - slopes[:, None, None] * distance[None]
    return jnp.where((cols <= rows)[None], scores, masked_score)


def contract_rows(left, right):
    return lax.dot_general(
        left, right, (((0,), (0,)), ((), ())), preferred_element_type=jnp.float32
    )


def owned_block(full, group_index):
    return lax.dynamic_index_in_dim(full, group_index, 0, keepdims=False)[0]


def shards(
    block_input,
    cotangent,
    w_qkv,
    w_out,
    w_up,
    w_down,
    vectors,
    b_up,
    qkv_left,
    qkv_right,
    out_left,
    out_right,
    up_left,
    up_right,
    down_left,
    down_right,
    qkv_left_root,
    qkv_right_root,
    out_left_root,
    out_right_root,
    up_left_root,
    up_right_root,
    down_left_root,
    down_right_root,
    vector_stat,
    b_up_stat,
):
    groups = lax.axis_size("dp")
    splits = lax.axis_size("ffn")
    group_index = lax.axis_index("dp")
    tokens_here = block_input.shape[0]
    qkv_full, out_full, vector_low, qkv_mroot, out_mroot, up_mroot, down_mroot = (
        lax.all_gather(w_qkv.astype(jnp.bfloat16), ("dp", "ffn"), axis=1, tiled=True),
        lax.all_gather(w_out.astype(jnp.bfloat16), ("dp", "ffn"), axis=1, tiled=True),
        lax.all_gather(vectors.astype(jnp.bfloat16), ("dp", "ffn"), axis=1, tiled=True),
        lax.all_gather(qkv_left_root.astype(jnp.bfloat16), ("dp", "ffn"), axis=0, tiled=True),
        lax.all_gather(out_left_root.astype(jnp.bfloat16), ("dp", "ffn"), axis=0, tiled=True),
        lax.all_gather(up_left_root.astype(jnp.bfloat16), ("dp", "ffn"), axis=0, tiled=True),
        lax.all_gather(down_right_root.astype(jnp.bfloat16), ("dp", "ffn"), axis=0, tiled=True),
    )
    up_cols, up_bias, down_rows = (
        lax.all_gather(w_up.astype(jnp.bfloat16), "dp", axis=1, tiled=True),
        lax.all_gather(b_up.astype(jnp.bfloat16), "dp", axis=0, tiled=True),
        lax.all_gather(w_down.astype(jnp.bfloat16), "dp", axis=0, tiled=True),
    )
    vector_rows = vector_low.astype(jnp.float32)
    inputs = block_input.astype(jnp.float32)
    normed_one, unit_one, inverse_one = layer_norm(inputs, vector_rows[0], vector_rows[1])
    acts_one = normed_one.astype(jnp.bfloat16)
    qkv_bias = jnp.concatenate([vector_rows[2], jnp.zeros_like(vector_rows[2]), vector_rows[3]])
    projected = (jnp.dot(acts_one, qkv_full, preferred_element_type=jnp.float32) + qkv_bias).astype(
        jnp.bfloat16
    )
    queries = projected[:, :D].reshape(tokens_here, HEADS, HEAD_DIM)
    keys = projected[:, D : 2 * D].reshape(tokens_here, HEADS, HEAD_DIM)
    values = projected[:, 2 * D :].reshape(tokens_here, HEADS, HEAD_DIM)
    block = min(512, tokens_here)
    blocks = tokens_here // block
    starts = jnp.arange(blocks, dtype=jnp.int32) * block
    query_blocks = queries.reshape(blocks, block, HEADS, HEAD_DIM)

    def attend_block(item):
        scores = alibi_scores(item[0], keys, item[1])
        highest = jnp.max(scores, axis=-1, keepdims=True)
        weights = jnp.exp(scores - highest)
        totals = jnp.sum(weights, axis=-1, keepdims=True)
        probs = (weights / totals).astype(jnp.bfloat16)
        mixed = jnp.einsum("hqk,khd->qhd", probs, values, preferred_element_type=jnp.float32)
        return (mixed, highest + jnp.log(totals))

    mixed, logsum = lax.map(attend_block, (query_blocks, starts))
    mixed_low = mixed.reshape(tokens_here, D).astype(jnp.bfloat16)
    attended = jnp.dot(mixed_low, out_full, preferred_element_type=jnp.float32) + vector_rows[4]
    residual = inputs + attended
    normed_two, unit_two, inverse_two = layer_norm(residual, vector_rows[5], vector_rows[6])
    acts_two = normed_two.astype(jnp.bfloat16)
    cot_float = cotangent.astype(jnp.float32)
    gathered = lax.all_gather(acts_two, "ffn", axis=0, tiled=True)
    pre = jnp.dot(gathered, up_cols, preferred_element_type=jnp.float32) + up_bias.astype(
        jnp.float32
    )
    hidden = jax.nn.gelu(pre, approximate=False).astype(jnp.bfloat16)
    branch = lax.psum_scatter(
        jnp.dot(hidden, down_rows, preferred_element_type=jnp.float32).astype(jnp.bfloat16),
        "ffn",
        scatter_dimension=0,
        tiled=True,
    ).astype(jnp.float32)
    cot_group = lax.all_gather(cotangent, "ffn", axis=0, tiled=True)
    down_t = contract_rows(hidden, cot_group)
    slope_low = (
        jnp.dot(cot_group, down_rows.T, preferred_element_type=jnp.float32) * gelu_slope(pre)
    ).astype(jnp.bfloat16)
    up_t = contract_rows(slope_low, gathered)
    bias_grad = jnp.sum(slope_low, axis=0, dtype=jnp.float32)
    back_two = lax.psum_scatter(
        jnp.dot(slope_low, up_cols.T, preferred_element_type=jnp.float32).astype(jnp.bfloat16),
        "ffn",
        scatter_dimension=0,
        tiled=True,
    ).astype(jnp.float32)
    block_output = (residual + branch + vector_rows[7]).astype(jnp.bfloat16)
    norm_two_back, gain_two_grad, shift_two_grad = norm_backward(
        back_two, unit_two, inverse_two, vector_rows[5]
    )
    residual_grad = cot_float + norm_two_back
    branch_low = residual_grad.astype(jnp.bfloat16)
    out_t = contract_rows(branch_low, mixed_low)
    out_bias_grad = jnp.sum(branch_low, axis=0, dtype=jnp.float32)
    mixed_grad = jnp.dot(branch_low, out_full.T, preferred_element_type=jnp.float32).astype(
        jnp.bfloat16
    )
    mixed_blocks = mixed_grad.reshape(blocks, block, HEADS, HEAD_DIM)
    scale = HEAD_DIM ** (-0.5)

    def attend_back(carry, item):
        key_grad, value_grad = carry
        query_block, upstream, log_total, start = item
        scores = alibi_scores(query_block, keys, start)
        probs = jnp.exp(scores - log_total)
        prob_grad = jnp.einsum("qhd,khd->hqk", upstream, values, preferred_element_type=jnp.float32)
        centered = jnp.sum(probs * prob_grad, axis=-1, keepdims=True)
        score_grad = (probs * (prob_grad - centered)).astype(jnp.bfloat16)
        query_grad = (
            jnp.einsum("hqk,khd->qhd", score_grad, keys, preferred_element_type=jnp.float32) * scale
        )
        key_grad = (
            key_grad
            + jnp.einsum(
                "hqk,qhd->khd", score_grad, query_block, preferred_element_type=jnp.float32
            )
            * scale
        )
        value_grad = value_grad + jnp.einsum(
            "hqk,qhd->khd", probs.astype(jnp.bfloat16), upstream, preferred_element_type=jnp.float32
        )
        return ((key_grad, value_grad), query_grad)

    zero_grads = jnp.zeros((tokens_here, HEADS, HEAD_DIM), jnp.float32)
    (key_grad, value_grad), query_grad = lax.scan(
        attend_back, (zero_grads, zero_grads), (query_blocks, mixed_blocks, logsum, starts)
    )
    projected_grad = jnp.concatenate(
        [
            query_grad.reshape(tokens_here, D),
            key_grad.reshape(tokens_here, D),
            value_grad.reshape(tokens_here, D),
        ],
        axis=1,
    ).astype(jnp.bfloat16)
    qkv_t = contract_rows(projected_grad, acts_one)
    projected_sums = jnp.sum(projected_grad, axis=0, dtype=jnp.float32)
    back_one = jnp.dot(projected_grad, qkv_full.T, preferred_element_type=jnp.float32)
    norm_one_back, gain_one_grad, shift_one_grad = norm_backward(
        back_one, unit_one, inverse_one, vector_rows[0]
    )
    input_grad = (residual_grad + norm_one_back).astype(jnp.bfloat16)
    vector_part = jnp.stack(
        [
            gain_one_grad,
            shift_one_grad,
            projected_sums[:D],
            projected_sums[2 * D :],
            out_bias_grad,
            gain_two_grad,
            shift_two_grad,
            jnp.sum(cot_float, axis=0),
        ]
    )
    qkv_s, out_s, vector_s = (
        lax.psum_scatter(
            qkv_t.reshape(groups, splits, -1, D).astype(jnp.bfloat16),
            "ffn",
            scatter_dimension=1,
            tiled=True,
        ).astype(jnp.float32),
        lax.psum_scatter(
            out_t.reshape(groups, splits, -1, D).astype(jnp.bfloat16),
            "ffn",
            scatter_dimension=1,
            tiled=True,
        ).astype(jnp.float32),
        lax.psum_scatter(
            vector_part.reshape(8, groups, splits, -1).astype(jnp.bfloat16),
            "ffn",
            scatter_dimension=2,
            tiled=True,
        ).astype(jnp.float32),
    )
    up_s = up_t.reshape(groups, 1, -1, D)
    down_s = down_t.reshape(groups, 1, -1, D)
    bias_s = bias_grad.reshape(groups, 1, -1)
    qkv_g, out_g, vector_g, up_g, down_g, bias_g = (
        lax.psum(qkv_s.astype(jnp.bfloat16), "dp").astype(jnp.float32),
        lax.psum(out_s.astype(jnp.bfloat16), "dp").astype(jnp.float32),
        lax.psum(vector_s.astype(jnp.bfloat16), "dp").astype(jnp.float32),
        lax.psum(up_s.astype(jnp.bfloat16), "dp").astype(jnp.float32),
        lax.psum(down_s.astype(jnp.bfloat16), "dp").astype(jnp.float32),
        lax.psum(bias_s.astype(jnp.bfloat16), "dp").astype(jnp.float32),
    )
    vector_grad = lax.dynamic_index_in_dim(vector_g, group_index, 1, keepdims=False)[:, 0]
    b_up_grad = owned_block(bias_g, group_index)
    grads_full = [qkv_g, out_g, up_g, down_g]
    grads_owned = [owned_block(item, group_index) for item in grads_full]
    lows = [item.astype(jnp.bfloat16) for item in grads_full]
    flats = [item.reshape(-1, D) for item in lows]
    rows_owned = D // (groups * splits)
    begin = group_index * (splits * rows_owned)
    square_rows = lax.psum_scatter(
        jnp.stack(
            [
                contract_rows(
                    lax.dynamic_slice_in_dim(flat, begin, rows_owned * lax.axis_size("ffn"), 1),
                    flat,
                )
                for flat in flats
            ],
            axis=1,
        ).astype(jnp.bfloat16),
        "ffn",
        scatter_dimension=0,
        tiled=True,
    ).astype(jnp.float32)
    owned_lows = [owned_block(item, group_index) for item in lows]
    n_roots = [qkv_right_root, out_right_root, up_right_root, down_left_root]
    root_blocks = [
        root.astype(jnp.bfloat16).reshape(root.shape[0], groups, splits, -1) for root in n_roots
    ]
    start_state = tuple(
        (
            (
                jnp.zeros((item.shape[0], groups, splits, item.shape[0]), jnp.float32),
                jnp.zeros((item.shape[0], D), jnp.float32),
            )
            for item in owned_lows
        )
    )
    pieces = (
        lax.all_gather(lows[0], "ffn", axis=1, tiled=True),
        lax.all_gather(lows[1], "ffn", axis=1, tiled=True),
        lax.all_gather(lows[2], "ffn", axis=1, tiled=True),
        lax.all_gather(lows[3], "ffn", axis=1, tiled=True),
    )
    renewed = []
    for owned, rooted, piece, state in zip(owned_lows, root_blocks, pieces, start_state):
        add_square = jnp.einsum("om,pfem->opfe", owned, piece, preferred_element_type=jnp.float32)
        add_product = jnp.einsum("opfe,pfem->om", rooted, piece, preferred_element_type=jnp.float32)
        renewed.append((add_square, add_product))
    folded = tuple(renewed)
    m_stats = [qkv_left, out_left, up_left, down_right]
    n_stats = [qkv_right, out_right, up_right, down_left]
    m_roots = [qkv_mroot, out_mroot, up_mroot, down_mroot]
    new_m = []
    new_n = []
    steps = []
    for index in range(4):
        square, product = folded[index]
        new_n.append(
            decay_rate * n_stats[index] + (1.0 - decay_rate) * square.reshape(square.shape[0], -1)
        )
        new_m.append(decay_rate * m_stats[index] + (1.0 - decay_rate) * square_rows[:, index, :])
        steps.append(
            jnp.dot(
                product.astype(jnp.bfloat16), m_roots[index].T, preferred_element_type=jnp.float32
            )
        )
    new_w_qkv = w_qkv - matrix_rate * steps[0].T
    new_w_out = w_out - matrix_rate * steps[1].T
    new_w_up = w_up - matrix_rate * steps[2].T
    new_w_down = w_down - matrix_rate * steps[3]
    new_vector_stat = decay_rate * vector_stat + (1.0 - decay_rate) * vector_grad * vector_grad
    new_vectors = vectors - vector_rate * vector_grad * lax.rsqrt(new_vector_stat)
    new_b_up_stat = decay_rate * b_up_stat + (1.0 - decay_rate) * b_up_grad * b_up_grad
    new_b_up = b_up - vector_rate * b_up_grad * lax.rsqrt(new_b_up_stat)
    return (
        block_output,
        input_grad,
        grads_owned[0].T,
        grads_owned[1].T,
        grads_owned[2].T,
        grads_owned[3],
        vector_grad,
        b_up_grad,
        new_m[0],
        new_n[0],
        new_m[1],
        new_n[1],
        new_m[2],
        new_n[2],
        new_n[3],
        new_m[3],
        new_vector_stat,
        new_b_up_stat,
        new_w_qkv,
        new_w_out,
        new_w_up,
        new_w_down,
        new_vectors,
        new_b_up,
    )


def solution(mesh):
    return jax.shard_map(
        shards,
        mesh=mesh,
        in_specs=(
            P(("dp", "ffn"), None),
            P(("dp", "ffn"), None),
            P(None, ("dp", "ffn")),
            P(None, ("dp", "ffn")),
            P(None, ("dp", "ffn")),
            P(("dp", "ffn"), None),
            P(None, ("dp", "ffn")),
            P(("dp", "ffn")),
            P(("dp", "ffn"), None),
            P(("dp", "ffn"), None),
            P(("dp", "ffn"), None),
            P(("dp", "ffn"), None),
            P(("dp", "ffn"), None),
            P(("dp", "ffn"), None),
            P(("dp", "ffn"), None),
            P(("dp", "ffn"), None),
            P(("dp", "ffn"), None),
            P(("dp", "ffn"), None),
            P(("dp", "ffn"), None),
            P(("dp", "ffn"), None),
            P(("dp", "ffn"), None),
            P(("dp", "ffn"), None),
            P(("dp", "ffn"), None),
            P(("dp", "ffn"), None),
            P(None, ("dp", "ffn")),
            P(("dp", "ffn")),
        ),
        out_specs=(
            P(("dp", "ffn"), None),
            P(("dp", "ffn"), None),
            P(None, ("dp", "ffn")),
            P(None, ("dp", "ffn")),
            P(None, ("dp", "ffn")),
            P(("dp", "ffn"), None),
            P(None, ("dp", "ffn")),
            P(("dp", "ffn")),
            P(("dp", "ffn"), None),
            P(("dp", "ffn"), None),
            P(("dp", "ffn"), None),
            P(("dp", "ffn"), None),
            P(("dp", "ffn"), None),
            P(("dp", "ffn"), None),
            P(("dp", "ffn"), None),
            P(("dp", "ffn"), None),
            P(None, ("dp", "ffn")),
            P(("dp", "ffn")),
            P(None, ("dp", "ffn")),
            P(None, ("dp", "ffn")),
            P(None, ("dp", "ffn")),
            P(("dp", "ffn"), None),
            P(None, ("dp", "ffn")),
            P(("dp", "ffn")),
        ),
        check_vma=False,
    )
```

profile of v0, /device:TPU:0, one launch (start us, length us, event | category | flops | bytes accessed | tf_op | source)
XLA Modules:
  0.0 1983.3 jit_solution(4317241003396165425)
XLA Ops:
  13.2 71.1 %all-gather = bf16[32,32,8]{1,2,0:T(8,128)(2,1)S(1)} all-gather(bf16[1,32,8]{1,2,0:T(8,128)(2,1)S(1)} %convert_bitcast_fusion.5), channel_id=1, replica_groups=mesh['dp'=8,'ffn'=4] {'dp','ffn'}, dimensions={0}, use_global_device_ids=true | all-gather | bytes 16896 | tf_op jit(solution)/shard_map/all_gather | solution.py:98
  89.0 10.4 add_convert_fusion
  107.8 38.4 %while.31 = (s32[]{:T(128)}, bf16[2,512,8,128]{3,1,2,0:T(8,128)(2,1)}, f32[2,8,512,1]{2,1,3,0:T(8,128)S(1)}, s32[2]{0:T(128)S(1)}, bf16[2,512,8,128]{3,1,2,0:T(8...) while((s32[]{:T(128)}, bf16[2,512,8,128]{3,1,2,0:T(8,128)(2,1)}, ...), condition=%wide.region_5.6_spmd, body=%wide.region_2.5_spmd.sunk | while | flops 2190995968 | bytes 79829240 | solution.py:134
  111.5 6.3 fusion.196
  130.4 6.3 fusion.196
  162.2 7.7 all-gather.1
  171.9 151.7 %all-gather.21.cloned.1.call-done = bf16[4096,1024]{0,1:T(8,128)(2,1)} async-done(((bf16[1024,1024]{0,1:T(8,128)(2,1)}), bf16[4096,1024]{0,1:T(8,128)(2,1)}) %all-gather.21.cloned.1.call-update) | async-done | bytes 8388624 | tf_op jit(solution)/shard_map/all_gather | solution.py:141
  323.5 48.5 %fusion.18 = (bf16[4096,1024]{1,0:T(8,128)(2,1)}, f32[4096,1024]{1,0:T(8,128)}) fusion(f32[1024]{0:T(1024)S(1)} %bitcast.349, bf16[4096,1024]{0,1:T(8,128)(2,1)} %all-gather.21.cloned.1.call-done, bf16[1024,1024]{1,0:T(8,128)(2,1)} %all-gather.23.cloned.1.call-done), kind=kOutput, calls=%fused_computation.40 | convolution fusion | flops 8866758656 | bytes 35655680 | tf_op jit(solution)/shard_map/dot_general | solution.py:142
  372.1 131.0 %all-gather.27.cloned.1.call-done = bf16[4096,1024]{1,0:T(8,128)(2,1)} async-done(((bf16[1024,1024]{1,0:T(8,128)(2,1)}), bf16[4096,1024]{1,0:T(8,128)(2,1)}) %all-gather.27.cloned.1.call-update) | async-done | bytes 8388624 | tf_op jit(solution)/shard_map/all_gather | solution.py:152
  503.1 19.3 fusion.140
  525.6 11.0 convolution_convert_fusion
  545.3 134.1 %reduce-scatter.11.cloned.1.call-done = bf16[1024,1024]{0,1:T(8,128)(2,1)} async-done(((bf16[4096,1024]{0,1:T(8,128)(2,1)}), bf16[1024,1024]{0,1:T(8,128)(2,1)}) %reduce-scatter.11.cloned.1.call-update) | async-done | bytes 2097168 | tf_op jit(solution)/shard_map/reduce_scatter | solution.py:159
  697.7 124.7 %while.32 = (s32[]{:T(128)}, f32[1024,8,128]{0,2,1:T(8,128)}, f32[1024,8,128]{0,2,1:T(8,128)}, bf16[2,512,8,128]{3,1,2,0:T(8,128)(2,1)}, bf16[2,512,8,128]{3,1,2...) while((s32[]{:T(128)}, f32[1024,8,128]{0,2,1:T(8,128)}, ...), condition=%wide.region_14.15_spmd.clone, body=%wide.region_12.14_spmd.clone.sunk | while | flops 5422182912 | bytes 280058176 | solution.py:203
  701.3 8.2 fusion.205
  709.5 14.7 multiply_reduce_fusion.4
  724.2 15.2 multiply_convert_fusion.2
  746.5 7.6 bitcast_dynamic-update-slice_fusion.8
  761.4 8.2 fusion.205
  769.6 14.7 multiply_reduce_fusion.4
  784.3 15.1 multiply_convert_fusion.2
  802.7 5.9 bitcast_add_fusion.5
  808.6 7.4 bitcast_dynamic-update-slice_fusion.8
  816.0 6.3 bitcast_add_fusion.4
  840.5 10.1 convolution_convert_fusion.2
  855.2 14.9 convolution_convert_fusion.4
  870.1 14.8 convolution_convert_fusion.3
  887.5 78.1 %reduce-scatter.13.cloned.1.call-done = bf16[8,1,96,1024]{3,2,0,1:T(8,128)(2,1)} async-done(((bf16[8,4,96,1024]{3,2,0,1:T(8,128)(2,1)}), bf16[8,1,96,1024]{3,2,0,1:T(8,128)(2,1)}) %reduce-scatter.13.cloned.1.call-update) | async-done | bytes 1572880 | tf_op jit(solution)/shard_map/reduce_scatter | solution.py:234
  965.6 15.4 convolution_convert_fusion.1
  983.4 12.2 fusion.139
  1009.5 66.4 %all-reduce.8.cloned.1.call-done = (bf16[8,1,96,1024]{3,2,0,1:T(8,128)(2,1)}, bf16[8,1,32,1024]{3,2,1,0:T(8,128)(2,1)}, bf16[8,1,128,1024]{3,2,1,0:T(8,128)(2,1)}, bf16[8,1,128,1024]{3,2,1,0:T(8,128)(2,1)}) async-done(((bf16[8,1,96,1024]{3,2,0,1:T(8,128)(2,1)}, bf16[8,1,32,1024]{3,2,1,0:T(8,128)(2,1)}, bf16[8,1,128,1024]{3,2,1,0:T(8,128)(2,1)}, bf16[8,1,128,1024]{3,2,1,0:T(8,128)(2,1)}), ...) | async-done | bytes 6291472 | tf_op jit(solution)/shard_map/psum | solution.py:257
  1101.2 121.7 %reduce-scatter.9.cloned.1.call-done = bf16[1024,1024]{0,1:T(8,128)(2,1)} async-done(((bf16[4096,1024]{0,1:T(8,128)(2,1)}), bf16[1024,1024]{0,1:T(8,128)(2,1)}) %reduce-scatter.9.cloned.1.call-update) | async-done | bytes 2097168 | tf_op jit(solution)/shard_map/reduce_scatter | solution.py:146
  1223.0 8.4 fusion.49
  1238.1 7.3 reduce-scatter.15.cloned.1.call-done
  1245.4 23.7 %all-reduce.1 = (bf16[8,8,1,32]{3,1,0,2:T(8,128)(2,1)S(1)}, bf16[8,1,128]{2,0,1:T(8,128)(2,1)S(1)}) all-reduce(bf16[8,8,1,32]{3,1,0,2:T(8,128)(2,1)} %reduce-scatter.15.cloned.1.call-done, bf16[8,1,128]{2,0,1:T(8,128)(2,1)S(1)} %bitcast.351), channel_id=1, replica_groups=mesh['dp'=8,'ffn'=4] {'dp'}, use_global_device_ids=true, to_apply=%region_31.32 | all-reduce | flops 3072 | bytes 12288 | tf_op jit(solution)/shard_map/psum | solution.py:259
  1279.1 40.5 %all-gather.31.cloned.1.call-done = bf16[8,4,32,1024]{3,2,0,1:T(8,128)(2,1)} async-done(((bf16[8,1,32,1024]{3,2,0,1:T(8,128)(2,1)}), bf16[8,4,32,1024]{3,2,0,1:T(8,128)(2,1)}) %all-gather.31.cloned.1.call-update) | async-done | bytes 2097168 | tf_op jit(solution)/shard_map/all_gather | solution.py:303
  1323.9 54.4 %all-gather.39.cloned.1.call-done = bf16[1024,1024]{1,0:T(8,128)(2,1)} async-done(((bf16[32,1024]{1,0:T(8,128)(2,1)}), bf16[1024,1024]{1,0:T(8,128)(2,1)}) %all-gather.39.cloned.1.call-update) | async-done | bytes 2097168 | tf_op jit(solution)/shard_map/all_gather | solution.py:100
  1381.9 112.1 %all-gather.29.cloned.1.call-done = bf16[8,4,96,1024]{3,2,0,1:T(8,128)(2,1)} async-done(((bf16[8,1,96,1024]{3,2,0,1:T(8,128)(2,1)}), bf16[8,4,96,1024]{3,2,0,1:T(8,128)(2,1)}) %all-gather.29.cloned.1.call-update) | async-done | bytes 6291472 | tf_op jit(solution)/shard_map/all_gather | solution.py:302
  1501.6 50.4 %all-gather.37.cloned.1.call-done = bf16[1024,1024]{1,0:T(8,128)(2,1)} async-done(((bf16[32,1024]{1,0:T(8,128)(2,1)}), bf16[1024,1024]{1,0:T(8,128)(2,1)}) %all-gather.37.cloned.1.call-update) | async-done | bytes 2097168 | tf_op jit(solution)/shard_map/all_gather | solution.py:99
  1552.0 6.3 fusion.74
  1558.4 51.8 %all-gather.41.cloned.1.call-done = bf16[1024,1024]{1,0:T(8,128)(2,1)} async-done(((bf16[32,1024]{1,0:T(8,128)(2,1)}), bf16[1024,1024]{1,0:T(8,128)(2,1)}) %all-gather.41.cloned.1.call-update) | async-done | bytes 2097168 | tf_op jit(solution)/shard_map/all_gather | solution.py:101
  1610.2 150.1 %all-gather.33.cloned.1.call-done = bf16[8,4,128,1024]{3,2,0,1:T(8,128)(2,1)} async-done(((bf16[8,1,128,1024]{3,2,0,1:T(8,128)(2,1)}), bf16[8,4,128,1024]{3,2,0,1:T(8,128)(2,1)}) %all-gather.33.cloned.1.call-update) | async-done | bytes 8388624 | tf_op jit(solution)/shard_map/all_gather | solution.py:304
  1760.3 8.1 fusion.70
  1769.4 9.0 copy.283
  1778.4 131.2 %all-gather.35.cloned.1.call-done = bf16[8,4,128,1024]{3,2,0,1:T(8,128)(2,1)} async-done(((bf16[8,1,128,1024]{3,2,0,1:T(8,128)(2,1)}), bf16[8,4,128,1024]{3,2,0,1:T(8,128)(2,1)}) %all-gather.35.cloned.1.call-update) | async-done | bytes 8388624 | tf_op jit(solution)/shard_map/all_gather | solution.py:305
  1909.6 8.3 copy.285
  1917.9 8.1 fusion.41
  1931.3 36.1 %all-gather.43.cloned.1.call-done = bf16[1024,1024]{1,0:T(8,128)(2,1)} async-done(((bf16[32,1024]{1,0:T(8,128)(2,1)}), bf16[1024,1024]{1,0:T(8,128)(2,1)}) %all-gather.43.cloned.1.call-update) | async-done | bytes 2097168 | tf_op jit(solution)/shard_map/all_gather | solution.py:102
  1967.4 8.9 fusion.68
  (369 shorter events, 217.6 us)
Async XLA Ops:
  7.2 81.8 %all-gather.17.cloned.1.call-start = ((), (), s32[]{:S(2)}) async-start(), calls=%async_computation.5 | async-start | bytes 6488064 | tf_op jit(solution)/shard_map/all_gather | solution.py:96
  9.0 142.3 %all-gather.19.cloned.1.call-start = ((), (), s32[]{:S(2)}) async-start(), calls=%async_computation.6 | async-start | bytes 2162688 | tf_op jit(solution)/shard_map/all_gather | solution.py:97
  10.6 161.3 %all-gather.23.cloned.1.call-start = ((), (), s32[]{:S(2)}) async-start(), calls=%async_computation.8 | async-start | bytes 2359296 | tf_op jit(solution)/shard_map/all_gather | solution.py:105
  12.4 311.1 %all-gather.21.cloned.1.call-start = ((), (), s32[]{:S(2)}) async-start(), calls=%async_computation.7 | async-start | bytes 10485760 | tf_op jit(solution)/shard_map/all_gather | solution.py:141
  160.7 211.4 %all-gather.25.cloned.1.call-start = ((), (), s32[]{:S(2)}) async-start(), calls=%async_computation.9 | async-start | bytes 2359296 | tf_op jit(solution)/shard_map/all_gather | solution.py:107
  161.5 341.5 %all-gather.27.cloned.1.call-start = ((), (), s32[]{:S(2)}) async-start(), calls=%async_computation.11 | async-start | bytes 10485760 | tf_op jit(solution)/shard_map/all_gather | solution.py:152
  162.1 517.3 %reduce-scatter.11.cloned.1.call-start = ((), (), s32[]{:S(2)}) async-start(), calls=%async_computation.12 | async-start | bytes 10485760 | tf_op jit(solution)/shard_map/reduce_scatter | solution.py:159
  536.5 348.4 %all-reduce.6.cloned.1.call-start = ((), (), s32[]{:S(2)}) async-start(), calls=%async_computation.24 | async-start | bytes 4194304
  538.1 141.3 %copy-start.33 = (f32[1024]{0:T(1024)S(1)}, f32[1024]{0:T(1024)}, u32[]{:S(2)}) copy-start(f32[1024]{0:T(1024)} %copy-done.32) | copy-start | bytes 12292
  538.1 141.3 %copy-start.46 = (f32[1,1024]{1,0:T(1,128)S(1)}, f32[1,1024]{1,0:T(1,128)}, u32[]{:S(2)}) copy-start(f32[1,1024]{1,0:T(1,128)} %get-tuple-element.635) | copy-start | bytes 12292
  538.1 141.3 %copy-start.49 = (f32[1024]{0:T(1024)S(1)}, f32[1024]{0:T(1024)}, u32[]{:S(2)}) copy-start(f32[1024]{0:T(1024)} %copy-done.48) | copy-start | bytes 12292
  540.9 143.7 %copy-start.12 = (bf16[1024,1024]{0,1:T(8,128)(2,1)S(1)}, bf16[1024,1024]{0,1:T(8,128)(2,1)}, u32[]{:S(2)}) copy-start(bf16[1024,1024]{0,1:T(8,128)(2,1)} %copy.264) | copy-start | bytes 6291460
  695.9 269.6 %reduce-scatter.13.cloned.1.call-start = ((), (), s32[]{:S(2)}) async-start(), calls=%async_computation.13 | async-start | bytes 7864320 | tf_op jit(solution)/shard_map/reduce_scatter | solution.py:234
  854.0 221.9 %all-reduce.8.cloned.1.call-start = ((), (), s32[]{:S(2)}) async-start(), calls=%async_computation.25 | async-start | bytes 12582912 | tf_op jit(solution)/shard_map/psum | solution.py:257
  965.6 257.3 %reduce-scatter.9.cloned.1.call-start = ((), (), s32[]{:S(2)}) async-start(), calls=%async_computation.10 | async-start | bytes 10485760 | tf_op jit(solution)/shard_map/reduce_scatter | solution.py:146
  981.0 264.3 %reduce-scatter.15.cloned.1.call-start = ((), (), s32[]{:S(2)}) async-start(), calls=%async_computation.14 | async-start | bytes 81920 | tf_op jit(solution)/shard_map/reduce_scatter | solution.py:246
  1009.4 267.8 %reduce-scatter.17.cloned.1.call-start = ((), (), s32[]{:S(2)}) async-start(), calls=%async_computation.15 | async-start | bytes 1310720 | tf_op jit(solution)/shard_map/reduce_scatter | solution.py:272
  1084.8 234.9 %all-gather.31.cloned.1.call-start = ((), (), s32[]{:S(2)}) async-start(), calls=%async_computation.17 | async-start | bytes 2621440 | tf_op jit(solution)/shard_map/all_gather | solution.py:303
  1085.4 292.9 %all-gather.39.cloned.1.call-start = ((), (), s32[]{:S(2)}) async-start(), calls=%async_computation.21 | async-start | bytes 2162688 | tf_op jit(solution)/shard_map/all_gather | solution.py:100
  1086.1 407.8 %all-gather.29.cloned.1.call-start = ((), (), s32[]{:S(2)}) async-start(), calls=%async_computation.16 | async-start | bytes 7864320 | tf_op jit(solution)/shard_map/all_gather | solution.py:302
  1086.7 465.3 %all-gather.37.cloned.1.call-start = ((), (), s32[]{:S(2)}) async-start(), calls=%async_computation.20 | async-start | bytes 2162688 | tf_op jit(solution)/shard_map/all_gather | solution.py:99
  1087.4 522.8 %all-gather.41.cloned.1.call-start = ((), (), s32[]{:S(2)}) async-start(), calls=%async_computation.22 | async-start | bytes 2162688 | tf_op jit(solution)/shard_map/all_gather | solution.py:101
  1088.2 672.1 %all-gather.33.cloned.1.call-start = ((), (), s32[]{:S(2)}) async-start(), calls=%async_computation.18 | async-start | bytes 10485760 | tf_op jit(solution)/shard_map/all_gather | solution.py:304
  1088.9 820.7 %all-gather.35.cloned.1.call-start = ((), (), s32[]{:S(2)}) async-start(), calls=%async_computation.19 | async-start | bytes 10485760 | tf_op jit(solution)/shard_map/all_gather | solution.py:305
  1089.5 877.9 %all-gather.43.cloned.1.call-start = ((), (), s32[]{:S(2)}) async-start(), calls=%async_computation.23 | async-start | bytes 2162688 | tf_op jit(solution)/shard_map/all_gather | solution.py:102
  1096.3 126.6 %copy-start.34 = (f32[1024]{0:T(1024)S(1)}, f32[1024]{0:T(1024)}, u32[]{:S(2)}) copy-start(f32[1024]{0:T(1024)} %copy-done.32) | copy-start | bytes 12292
  1096.3 126.6 %copy-start.47 = (f32[1,1024]{1,0:T(1,128)S(1)}, f32[1,1024]{1,0:T(1,128)}, u32[]{:S(2)}) copy-start(f32[1,1024]{1,0:T(1,128)} %get-tuple-element.635) | copy-start | bytes 12292
  1096.3 126.6 %copy-start.50 = (f32[1024]{0:T(1024)S(1)}, f32[1024]{0:T(1024)}, u32[]{:S(2)}) copy-start(f32[1024]{0:T(1024)} %copy-done.48) | copy-start | bytes 12292
  1096.3 126.6 %copy-start.58 = (f32[1024]{0:T(1024)S(1)}, f32[1024]{0:T(1024)}, u32[]{:S(2)}) copy-start(f32[1024]{0:T(1024)} %copy-done.57) | copy-start | bytes 12292
  1096.4 126.6 %copy-start.60 = (f32[1024]{0:T(1024)S(1)}, f32[1024]{0:T(1024)}, u32[]{:S(2)}) copy-start(f32[1024]{0:T(1024)} %copy-done.59) | copy-start | bytes 12292
  1096.4 126.6 %copy-start.64 = (f32[1,1024]{1,0:T(1,128)S(1)}, f32[1,1024]{1,0:T(1,128)}, u32[]{:S(2)}) copy-start(f32[1,1024]{1,0:T(1,128)} %get-tuple-element.633) | copy-start | bytes 12292
  1231.3 38.3 %copy-start.62 = (f32[8,32]{1,0:T(8,128)S(1)}, f32[8,32]{1,0:T(8,128)}, u32[]{:S(2)}) copy-start(f32[8,32]{1,0:T(8,128)} %param.36) | copy-start | bytes 3076
  1235.5 42.8 %copy-start.35 = (f32[32,1024]{1,0:T(8,128)S(1)}, f32[32,1024]{1,0:T(8,128)}, u32[]{:S(2)}) copy-start(f32[32,1024]{1,0:T(8,128)} %param.45) | copy-start | bytes 393220
  1235.5 42.8 %copy-start.36 = (f32[32,1024]{1,0:T(8,128)S(1)}, f32[32,1024]{1,0:T(8,128)}, u32[]{:S(2)}) copy-start(f32[32,1024]{1,0:T(8,128)} %param.42) | copy-start | bytes 393220
  1235.5 42.8 %copy-start.37 = (f32[32,1024]{1,0:T(8,128)S(1)}, f32[32,1024]{1,0:T(8,128)}, u32[]{:S(2)}) copy-start(f32[32,1024]{1,0:T(8,128)} %param.40) | copy-start | bytes 393220
  1235.5 42.8 %copy-start.38 = (f32[32,1024]{1,0:T(8,128)S(1)}, f32[32,1024]{1,0:T(8,128)}, u32[]{:S(2)}) copy-start(f32[32,1024]{1,0:T(8,128)} %param.38) | copy-start | bytes 393220
  1269.1 52.5 %copy-start.63 = (f32[8,1,1,32]{3,1,0,2:T(1,128)}, f32[8,1,1,32]{3,1,0,2:T(1,128)S(1)}, u32[]{:S(2)}) copy-start(f32[8,1,1,32]{3,1,0,2:T(1,128)S(1)} %dynamic-slice_convert_fusion) | copy-start | bytes 3076
  1274.5 47.1 %copy-start.44 = (f32[32,1024]{1,0:T(8,128)S(1)}, f32[32,1024]{1,0:T(8,128)}, u32[]{:S(2)}) copy-start(f32[32,1024]{1,0:T(8,128)} %param.41) | copy-start | bytes 393220
  1278.3 100.0 %copy-start.26 = (f32[1024,32]{0,1:T(8,128)S(1)}, f32[1024,32]{0,1:T(8,128)}, u32[]{:S(2)}) copy-start(f32[1024,32]{0,1:T(8,128)} %param.33) | copy-start | bytes 393220
  1319.7 58.6 %copy-start.13 = (bf16[8,4,32,1024]{3,2,0,1:T(8,128)(2,1)S(1)}, bf16[8,4,32,1024]{3,2,0,1:T(8,128)(2,1)}, u32[]{:S(2)}) copy-start(bf16[8,4,32,1024]{3,2,0,1:T(8,128)(2,1)} %all-gather.31.cloned.1.call-done) | copy-start | bytes 6291460
  1381.9 115.6 %copy-start.23 = (f32[96,3072]{1,0:T(8,128)S(1)}, f32[96,3072]{1,0:T(8,128)}, u32[]{:S(2)}) copy-start(f32[96,3072]{1,0:T(8,128)} %param.39) | copy-start | bytes 3538948
  1497.5 54.6 %copy-start.17 = (bf16[96,8,4,96]{3,2,1,0:T(4,128)(2,1)S(1)}, bf16[96,8,4,96]{3,2,1,0:T(4,128)(2,1)}, u32[]{:S(2)}) copy-start(bf16[96,8,4,96]{3,2,1,0:T(4,128)(2,1)} %reshape.347) | copy-start | bytes 1769476
  1497.5 54.6 %copy-start.22 = (f32[1024,96]{0,1:T(8,128)S(1)}, f32[1024,96]{0,1:T(8,128)}, u32[]{:S(2)}) copy-start(f32[1024,96]{0,1:T(8,128)} %param.32) | copy-start | bytes 1179652
  1501.6 258.7 %copy-start.25 = (bf16[128,8,4,128]{3,2,1,0:T(4,128)(2,1)S(1)}, bf16[128,8,4,128]{3,2,1,0:T(4,128)(2,1)}, u32[]{:S(2)}) copy-start(bf16[128,8,4,128]{3,2,1,0:T(4,128)(2,1)} %reshape.349) | copy-start | bytes 3145732
  1501.6 258.7 %copy-start.29 = (f32[1024,128]{0,1:T(8,128)S(1)}, f32[1024,128]{0,1:T(8,128)}, u32[]{:S(2)}) copy-start(f32[1024,128]{0,1:T(8,128)} %copy.290) | copy-start | bytes 1572868
  1778.4 139.5 %copy-start.18 = (f32[128,4096]{1,0:T(8,128)S(1)}, f32[128,4096]{1,0:T(8,128)}, u32[]{:S(2)}) copy-start(f32[128,4096]{1,0:T(8,128)} %param.44) | copy-start | bytes 6291460
  1926.0 41.4 %copy-start.24 = (bf16[128,8,4,128]{3,2,1,0:T(4,128)(2,1)S(1)}, bf16[128,8,4,128]{3,2,1,0:T(4,128)(2,1)}, u32[]{:S(2)}) copy-start(bf16[128,8,4,128]{3,2,1,0:T(4,128)(2,1)} %reshape.350) | copy-start | bytes 3145732
  1926.0 41.4 %copy-start.28 = (f32[128,1024]{1,0:T(8,128)S(1)}, f32[128,1024]{1,0:T(8,128)}, u32[]{:S(2)}) copy-start(f32[128,1024]{1,0:T(8,128)} %param.35) | copy-start | bytes 1572868
  (61 other events, 457.6 us)
Sparse Core Ops, SparseCore 0:
  11.5 71.7 all-gather.16
  86.8 55.5 all-gather.18
  144.8 27.0 all-gather.22
  173.9 149.6 all-gather.20
  325.8 26.0 all-gather.24
  353.4 149.6 all-gather.26
  536.7 142.6 reduce-scatter.10
  696.0 87.2 all-reduce.5
  854.1 111.3 reduce-scatter.12
  970.6 105.3 all-reduce.7
  1078.3 144.5 reduce-scatter.8
  1225.6 19.7 reduce-scatter.14
  1248.3 25.2 reduce-scatter.16
  1275.1 44.5 all-gather.30
  1323.0 55.2 all-gather.38
  1379.7 114.1 all-gather.28
  1497.3 54.6 all-gather.36
  1554.8 55.3 all-gather.40
  1611.8 148.4 all-gather.32
  1761.7 147.8 all-gather.34
  1912.5 54.7 all-gather.42
where the time goes:
time: 1990 us; the launch traced here: 1980 us
  waiting for transfers between devices  1320 us (66%)
  matrix products  324 us (16%)
  local copies, waits for them, and re-layouts  111 us (6%)
  other arithmetic  105 us (5%)
  blocking collectives  102 us (5%)
    all_gather x1, waiting for transfers between devices, shards(): gathered = lax.all_gather(acts_two, 'ffn', axis=0, tiled=True)  152 us
    all_gather x1, waiting for transfers between devices, shards(): lax.all_gather(lows[2], 'ffn', axis=1, tiled=True)  150 us
    reduce_scatter x1, waiting for transfers between devices, shards(): lax.psum_scatter(jnp.dot(slope_low, up_cols.T, preferred_element_type=jnp...  134 us
    all_gather x1, waiting for transfers between devices, shards(): lax.all_gather(lows[3], 'ffn', axis=1, tiled=True)  131 us
    all_gather x1, waiting for transfers between devices, shards(): cot_group = lax.all_gather(cotangent, 'ffn', axis=0, tiled=True)  131 us
    reduce_scatter x1, waiting for transfers between devices, shards(): lax.psum_scatter(jnp.dot(hidden, down_rows, preferred_element_type=jnp.fl...  122 us
    all_gather x1, waiting for transfers between devices, shards(): lax.all_gather(lows[0], 'ffn', axis=1, tiled=True)  112 us
    reduce_scatter x1, waiting for transfers between devices, shards(): lax.psum_scatter(qkv_t.reshape(groups, splits, -1, D).astype(jnp.bfloat16...  78.1 us
  transfers between devices with their start and end apart: 21, of which 16 were waited for; matrix products, arithmetic and copies ran while one was open for 24% of the time, Pallas kernels for 0%

commit v1 on v0

v1 whole, which is shorter than its diff:
```python
import functools

import jax
import jax.numpy as jnp
from jax import lax
from jax.experimental import pallas as pl
from jax.experimental.pallas import tpu as pltpu
from jax.sharding import PartitionSpec as P

D = 1024
HEADS = 8
HEAD_DIM = 128
MESH = pl.DeviceIdType.MESH
ALL = ("dp", "ffn")
BF = jnp.bfloat16
F32 = jnp.float32
MIB = 2**20

norm_epsilon = 1e-05
decay_rate = 0.5
matrix_rate = 0.5
vector_rate = 0.1
masked_score = -1e30


def layer_norm(values, gain, shift):
    center = values - jnp.mean(values, axis=-1, keepdims=True)
    inverse = lax.rsqrt(jnp.mean(center * center, axis=-1, keepdims=True) + norm_epsilon)
    normed = center * inverse
    return (normed * gain + shift, normed, inverse)


def norm_backward(grad, normed, inverse, gain):
    scaled = grad * gain
    inner = (
        scaled
        - jnp.mean(scaled, axis=-1, keepdims=True)
        - normed * jnp.mean(scaled * normed, axis=-1, keepdims=True)
    )
    return (inner * inverse, jnp.sum(grad * normed, axis=0), jnp.sum(grad, axis=0))


def dot_nt(left, right):
    return lax.dot_general(left, right, (((1,), (1,)), ((), ())), preferred_element_type=F32)


def dot_tn(left, right):
    return lax.dot_general(left, right, (((0,), (0,)), ((), ())), preferred_element_type=F32)


def dot_nn(left, right):
    return jnp.dot(left, right, preferred_element_type=F32)


def coords():
    dp = lax.axis_index("dp")
    return dp // 2, dp % 2, lax.axis_index("ffn")


def flip(value, mask):
    result = value
    bit = 1
    while bit <= mask:
        if mask & bit:
            result = result + bit - 2 * bit * ((result // bit) % 2)
        bit *= 2
    return result


def greet():
    p, c, z = coords()
    barrier = pltpu.get_barrier_semaphore()
    peers = [(flip(p, 1) * 2 + c, z), (flip(p, 2) * 2 + c, z), (p * 2 + 1 - c, z)]
    peers += [(p * 2 + c, flip(z, k)) for k in (1, 2, 3)]
    for peer in peers:
        pl.semaphore_signal(barrier, inc=1, device_id=peer, device_id_type=MESH)
    pl.semaphore_wait(barrier, len(peers))


FIRST = (1, 2)
SECOND = (2, 1)
GATHER_COPIES = 31
REDUCE_COPIES = 31


def gather_steps(shard, out, send, recv, local_sem):
    p, c, z = coords()
    half_rows = shard.shape[0] // 2
    copies = {}
    local = pltpu.make_async_copy(shard, out.at[p, c, z], local_sem)

    def post(name, src, dst, device):
        at = len(copies)
        copies[name] = pltpu.make_async_remote_copy(
            src, dst, send.at[at], recv.at[at], device_id=device, device_id_type=MESH
        )
        copies[name].start()

    def half(ref, h):
        return ref.at[pl.ds(h * half_rows, half_rows)]

    def spread(k):
        for name, turn in (("first", FIRST), ("second", SECOND)):
            for h in (0, 1):
                dst = half(out.at[p, c, flip(z, k)], h)
                src = dst if k else half(shard, h)
                post((name, k, h), src, dst, (flip(p, turn[h]) * 2 + c, z))

    def begin():
        local.start()
        for k in (1, 2, 3):
            post(("z", k), shard, out.at[p, c, z], (p * 2 + c, flip(z, k)))
        spread(0)

    def landed(k):
        copies["z", k].wait_recv()
        spread(k)

    def forward(k):
        for h in (0, 1):
            copies["first", k, h].wait_recv()
            piece = half(out.at[flip(p, FIRST[h]), c, flip(z, k)], h)
            post(("relay", k, h), piece, piece, (flip(p, SECOND[h]) * 2 + c, z))

    def share(k):
        for h in (0, 1):
            copies["second", k, h].wait_recv()
            copies["relay", k, h].wait_recv()
        if k == 0:
            local.wait()
        piece = out.at[:, c, flip(z, k)]
        post(("core", k), piece, piece, (p * 2 + 1 - c, z))

    def finish():
        for k in range(4):
            copies["core", k].wait_recv()
        for copy in copies.values():
            copy.wait_send()

    plan = [begin, (landed, 1), (forward, 0), (landed, 2), (forward, 1), (share, 0), (landed, 3)]
    plan += [(forward, 2), (share, 1), (forward, 3), (share, 2), (share, 3), finish]
    return plan


def reduce_steps(parts, out, held, from_core, from_second, from_first, from_z, send, recv, load):
    p, c, z = coords()
    half_rows = parts.shape[-2] // 2
    copies = {}
    loads = {}
    order = (1, 2, 3, 0)

    def post(name, src, dst, device):
        at = len(copies)
        copies[name] = pltpu.make_async_remote_copy(
            src, dst, send.at[at], recv.at[at], device_id=device, device_id_type=MESH
        )
        copies[name].start()

    def half(h):
        return pl.ds(h * half_rows, half_rows)

    def begin():
        for k in order:
            post(("core", k), parts.at[:, 1 - c, flip(z, k)], from_core.at[k], (p * 2 + 1 - c, z))
            loads[k] = pltpu.make_async_copy(
                parts.at[:, c, flip(z, k)], held.at[k], load.at[k]
            )
            loads[k].start()

    def add(dst, *sources):
        total = dst[...].astype(F32)
        for source in sources:
            total = total + source[...].astype(F32)
        dst[...] = total.astype(BF)

    def cores(k):
        loads[k].wait()
        copies["core", k].wait_recv()
        for j in range(4):
            add(held.at[k, j], from_core.at[k, j])
        for h in (0, 1):
            for j, q in ((1, flip(p, 3)), (0, flip(p, SECOND[h]))):
                post(
                    ("second", k, h, j),
                    held.at[k, q, half(h)],
                    from_second.at[k, h, j],
                    (flip(p, SECOND[h]) * 2 + c, z),
                )

    def second(k):
        for h in (0, 1):
            copies["second", k, h, 1].wait_recv()
            q = flip(p, FIRST[h])
            add(held.at[k, q, half(h)], from_second.at[k, h, 1])
            post(("first", k, h), held.at[k, q, half(h)], from_first.at[k, h], (q * 2 + c, z))

    def first(k):
        for h in (0, 1):
            copies["second", k, h, 0].wait_recv()
            copies["first", k, h].wait_recv()
            add(held.at[k, p, half(h)], from_second.at[k, h, 0], from_first.at[k, h])
        if k:
            post(("z", k), held.at[k, p], from_z.at[k - 1], (p * 2 + c, flip(z, k)))

    def finish():
        for k in (1, 2, 3):
            copies["z", k].wait_recv()
        total = held[0, p].astype(F32)
        for k in range(3):
            total = total + from_z[k].astype(F32)
        out[...] = total
        for copy in copies.values():
            copy.wait_send()

    plan = [begin, (cores, 1), (cores, 2), (second, 1), (cores, 3), (second, 2), (first, 1)]
    plan += [(cores, 0), (second, 3), (first, 2), (second, 0), (first, 3), (first, 0), finish]
    return plan


def run_step(step):
    if isinstance(step, tuple):
        step[0](step[1])
    else:
        step()


def interleave(plans, offset):
    total = max(len(plan) + offset * g for g, plan in enumerate(plans))
    merged = []
    for t in range(total):
        for g, plan in enumerate(plans):
            at = t - offset * g
            if 0 <= at < len(plan):
                merged.append(plan[at])
    return merged


def gather_kernel(count, *refs):
    ins, outs = refs[:count], refs[count : 2 * count]
    send, recv, local = refs[2 * count :]
    greet()
    plans = [
        gather_steps(ins[g], outs[g], send.at[g], recv.at[g], local.at[g]) for g in range(count)
    ]
    for step in interleave(plans, 7):
        run_step(step)


def reduce_kernel(count, *refs):
    ins, outs = refs[:count], refs[count : 2 * count]
    scratch = refs[2 * count :]
    greet()
    plans = [reduce_steps(ins[g], outs[g], *scratch[8 * g : 8 * g + 8]) for g in range(count)]
    for step in interleave(plans, 7):
        run_step(step)


def reduce_scratch(rows, width):
    return [
        pltpu.VMEM((4, 4, rows, width), BF),
        pltpu.VMEM((4, 4, rows, width), BF),
        pltpu.VMEM((4, 2, 2, rows // 2, width), BF),
        pltpu.VMEM((4, 2, rows // 2, width), BF),
        pltpu.VMEM((3, rows, width), BF),
        pltpu.SemaphoreType.DMA((REDUCE_COPIES,)),
        pltpu.SemaphoreType.DMA((REDUCE_COPIES,)),
        pltpu.SemaphoreType.DMA((4,)),
    ]


def fits_grid(rows):
    return (
        lax.axis_size("dp") == 8 and lax.axis_size("ffn") == 4 and all(r % 32 == 0 for r in rows)
    )


def gather_all(shards, collective_id):
    if not fits_grid([item.shape[0] for item in shards]):
        return [lax.all_gather(item, ALL, axis=0, tiled=True) for item in shards]
    count = len(shards)
    anywhere = pl.BlockSpec(memory_space=pl.ANY)
    outs = pl.pallas_call(
        functools.partial(gather_kernel, count),
        out_shape=tuple(jax.ShapeDtypeStruct((4, 2, 4) + item.shape, BF) for item in shards),
        in_specs=[anywhere] * count,
        out_specs=(anywhere,) * count,
        scratch_shapes=[
            pltpu.SemaphoreType.DMA((count, GATHER_COPIES)),
            pltpu.SemaphoreType.DMA((count, GATHER_COPIES)),
            pltpu.SemaphoreType.DMA((count,)),
        ],
        compiler_params=pltpu.CompilerParams(collective_id=collective_id, has_side_effects=True),
    )(*shards)
    return [item.reshape(-1, item.shape[-1]) for item in outs]


def reduce_all(parts, collective_id):
    devices = lax.axis_size("dp") * lax.axis_size("ffn")
    rows = [item.shape[0] // devices for item in parts]
    if not fits_grid(rows):
        return [
            lax.psum_scatter(item.astype(BF), ALL, scatter_dimension=0, tiled=True).astype(F32)
            for item in parts
        ]
    count = len(parts)
    scratch = []
    for item, r in zip(parts, rows):
        scratch += reduce_scratch(r, item.shape[-1])
    outs = pl.pallas_call(
        functools.partial(reduce_kernel, count),
        out_shape=tuple(
            jax.ShapeDtypeStruct((r, item.shape[-1]), F32) for item, r in zip(parts, rows)
        ),
        in_specs=[pl.BlockSpec(memory_space=pl.ANY)] * count,
        out_specs=(pl.BlockSpec(memory_space=pltpu.VMEM),) * count,
        scratch_shapes=scratch,
        compiler_params=pltpu.CompilerParams(
            collective_id=collective_id, has_side_effects=True, vmem_limit_bytes=56 * MIB
        ),
    )(*[item.reshape(4, 2, 4, r, item.shape[-1]) for item, r in zip(parts, rows)])
    return list(outs)


QUERY_BLOCK = 256


def scores_t(query, keys, slope, start, rows):
    raw = dot_nt(keys, query)
    at_key = lax.broadcasted_iota(jnp.int32, (rows, 1), 0).astype(F32)
    return raw * HEAD_DIM ** (-0.5) + at_key * slope


def mask_t(scores, start, rows, width):
    at_key = lax.broadcasted_iota(jnp.int32, (rows, width), 0)
    at_query = lax.broadcasted_iota(jnp.int32, (rows, width), 1) + start
    return jnp.where(at_key <= at_query, scores, masked_score)


def head_slope(head):
    level = head.astype(F32) + 1.0
    return jnp.exp2(jnp.full((1, 1), -8.0 / HEADS, F32) * level)


def attend_kernel(q_ref, k_ref, v_ref, o_ref, lse_ref):
    slope = head_slope(pl.program_id(0))
    length = q_ref.shape[0]
    values_t = v_ref[...].astype(F32).T.astype(BF)
    for start in range(0, length, QUERY_BLOCK):
        rows = start + QUERY_BLOCK
        scores = scores_t(q_ref[start:rows, :], k_ref[:rows, :], slope, start, rows)
        scores = mask_t(scores, start, rows, QUERY_BLOCK)
        highest = jnp.max(scores, axis=0, keepdims=True)
        weights = jnp.exp(scores - highest)
        totals = jnp.sum(weights, axis=0, keepdims=True)
        mixed = dot_nn(values_t[:, :rows], weights.astype(BF)) / totals
        o_ref[start:rows, :] = mixed.T.astype(BF)
        lse_ref[0, :, start:rows] = highest + jnp.log(totals)


def attend(projected):
    tokens = projected.shape[0]
    column = lambda offset: pl.BlockSpec((tokens, HEAD_DIM), lambda h: (0, offset + h))
    return pl.pallas_call(
        attend_kernel,
        grid=(HEADS,),
        out_shape=(
            jax.ShapeDtypeStruct((tokens, D), BF),
            jax.ShapeDtypeStruct((HEADS, 1, tokens), F32),
        ),
        in_specs=[column(0), column(HEADS), column(2 * HEADS)],
        out_specs=(column(0), pl.BlockSpec((1, 1, tokens), lambda h: (h, 0, 0))),
        compiler_params=pltpu.CompilerParams(vmem_limit_bytes=48 * MIB),
    )(projected, projected, projected)


def attend_back_kernel(q_ref, k_ref, v_ref, do_ref, lse_ref, out_ref, dk, dv):
    slope = head_slope(pl.program_id(0))
    length = q_ref.shape[0]
    scale = HEAD_DIM ** (-0.5)
    keys_t = k_ref[...].astype(F32).T.astype(BF)
    for start in reversed(range(0, length, QUERY_BLOCK)):
        rows = start + QUERY_BLOCK
        query = q_ref[start:rows, :]
        upstream = do_ref[start:rows, :]
        scores = scores_t(query, k_ref[:rows, :], slope, start, rows)
        scores = mask_t(scores, start, rows, QUERY_BLOCK)
        probs = jnp.exp(scores - lse_ref[0, :, start:rows])
        prob_grad = dot_nt(v_ref[:rows, :], upstream)
        weighted = probs * prob_grad
        centered = jnp.sum(weighted, axis=0, keepdims=True)
        score_grad = (weighted - probs * centered).astype(BF)
        out_ref[0, start:rows, :] = (dot_nn(keys_t[:, :rows], score_grad) * scale).T.astype(BF)
        key_part = dot_nn(score_grad, query)
        value_part = dot_nn(probs.astype(BF), upstream)
        if rows == length:
            dk[...] = key_part
            dv[...] = value_part
        else:
            dk[:rows, :] += key_part
            dv[:rows, :] += value_part
    out_ref[1] = (dk[...] * scale).astype(BF)
    out_ref[2] = dv[...].astype(BF)


def attend_back(projected, upstream, lse):
    tokens = projected.shape[0]
    column = lambda offset: pl.BlockSpec((tokens, HEAD_DIM), lambda h: (0, offset + h))
    return pl.pallas_call(
        attend_back_kernel,
        grid=(HEADS,),
        out_shape=jax.ShapeDtypeStruct((3, tokens, D), BF),
        in_specs=[
            column(0),
            column(HEADS),
            column(2 * HEADS),
            column(0),
            pl.BlockSpec((1, 1, tokens), lambda h: (h, 0, 0)),
        ],
        out_specs=pl.BlockSpec((3, tokens, HEAD_DIM), lambda h: (0, 0, h)),
        scratch_shapes=[pltpu.VMEM((tokens, HEAD_DIM), F32), pltpu.VMEM((tokens, HEAD_DIM), F32)],
        compiler_params=pltpu.CompilerParams(vmem_limit_bytes=48 * MIB),
    )(projected, projected, projected, upstream, lse)


def gelu_pair(pre):
    half = 0.5 * (1.0 + lax.erf(pre * 0.7071067811865476))
    slope = half + pre * jnp.exp(-0.5 * pre * pre) * 0.3989422804014327
    return pre * half, slope


def hidden_kernel(acts_ref, up_ref, bias_ref, hidden_ref, slope_ref):
    pre = dot_nt(acts_ref[...], up_ref[...]) + bias_ref[...]
    hidden, slope = gelu_pair(pre)
    hidden_ref[...] = hidden.astype(BF)
    slope_ref[...] = slope.astype(BF)


def hidden_units(acts, up_full, bias):
    tokens = acts.shape[0]
    units = up_full.shape[0]
    block = 512
    column = pl.BlockSpec((tokens, block), lambda n: (0, n))
    return pl.pallas_call(
        hidden_kernel,
        grid=(units // block,),
        out_shape=(jax.ShapeDtypeStruct((tokens, units), BF),) * 2,
        in_specs=[
            pl.BlockSpec((tokens, D), lambda n: (0, 0)),
            pl.BlockSpec((block, D), lambda n: (n, 0)),
            pl.BlockSpec((1, block), lambda n: (0, n)),
        ],
        out_specs=(column, column),
        compiler_params=pltpu.CompilerParams(vmem_limit_bytes=48 * MIB),
    )(acts, up_full, bias.reshape(1, -1))


SMALL_ROWS = 32
SMALL_WIDTH = 128


def pack_small(vector_part, bias_part):
    owners = vector_part.shape[0]
    flat = jnp.concatenate([vector_part.reshape(owners, -1), bias_part.reshape(owners, -1)], axis=1)
    room = SMALL_ROWS * SMALL_WIDTH
    flat = jnp.pad(flat, ((0, 0), (0, room - flat.shape[1])))
    return flat.reshape(owners * SMALL_ROWS, SMALL_WIDTH)


def unpack_small(packed, columns, units):
    owners = packed.shape[0] // SMALL_ROWS
    flat = packed.reshape(owners, -1)
    vector_part = flat[:, : 8 * columns].reshape(owners, 8, columns)
    bias_part = flat[:, 8 * columns : 8 * columns + units]
    return vector_part, bias_part


def shards(
    block_input,
    cotangent,
    w_qkv,
    w_out,
    w_up,
    w_down,
    vectors,
    b_up,
    qkv_left,
    qkv_right,
    out_left,
    out_right,
    up_left,
    up_right,
    down_left,
    down_right,
    qkv_left_root,
    qkv_right_root,
    out_left_root,
    out_right_root,
    up_left_root,
    up_right_root,
    down_left_root,
    down_right_root,
    vector_stat,
    b_up_stat,
):
    owners = lax.axis_size("dp") * lax.axis_size("ffn")
    me = lax.axis_index("dp") * lax.axis_size("ffn") + lax.axis_index("ffn")
    columns = vectors.shape[1]
    units = b_up.shape[0]
    small = pack_small(vectors[None], b_up[None]).astype(BF)
    small_full, qkv_full, out_full, up_full, down_full = gather_all(
        [
            small,
            w_qkv.T.astype(BF),
            w_out.T.astype(BF),
            w_up.T.astype(BF),
            w_down.astype(BF),
        ],
        1,
    )
    vector_low, bias_low = unpack_small(small_full, columns, units)
    vector_rows = vector_low.transpose(1, 0, 2).reshape(8, D).astype(F32)
    up_bias = bias_low.reshape(-1).astype(F32)
    inputs = block_input.astype(F32)
    normed_one, unit_one, inverse_one = layer_norm(inputs, vector_rows[0], vector_rows[1])
    acts_one = normed_one.astype(BF)
    qkv_bias = jnp.concatenate([vector_rows[2], jnp.zeros_like(vector_rows[2]), vector_rows[3]])
    projected = (dot_nt(acts_one, qkv_full) + qkv_bias).astype(BF)
    mixed_low, logsum = attend(projected)
    residual = inputs + dot_nt(mixed_low, out_full) + vector_rows[4]
    normed_two, unit_two, inverse_two = layer_norm(residual, vector_rows[5], vector_rows[6])
    acts_two = normed_two.astype(BF)
    cot_float = cotangent.astype(F32)
    hidden, slope = hidden_units(acts_two, up_full, up_bias)
    block_output = (residual + dot_nn(hidden, down_full) + vector_rows[7]).astype(BF)
    down_t = dot_tn(hidden, cotangent).astype(BF)
    slope_low = (dot_nt(cotangent, down_full) * slope.astype(F32)).astype(BF)
    up_t = dot_tn(slope_low, acts_two).astype(BF)
    bias_grad = jnp.sum(slope_low, axis=0, dtype=F32)
    back_two = dot_nn(slope_low, up_full)
    down_g, up_g = reduce_all([down_t, up_t], 2)
    norm_two_back, gain_two_grad, shift_two_grad = norm_backward(
        back_two, unit_two, inverse_two, vector_rows[5]
    )
    residual_grad = cot_float + norm_two_back
    branch_low = residual_grad.astype(BF)
    out_t = dot_tn(branch_low, mixed_low).astype(BF)
    out_bias_grad = jnp.sum(branch_low, axis=0, dtype=F32)
    mixed_grad = dot_nn(branch_low, out_full).astype(BF)
    projected_grad = attend_back(projected, mixed_grad, logsum)
    qkv_t = jnp.concatenate([dot_tn(projected_grad[i], acts_one) for i in range(3)], 0).astype(BF)
    projected_sums = jnp.sum(projected_grad, axis=1, dtype=F32)
    back_one = sum(dot_nn(projected_grad[i], qkv_full[i * D : (i + 1) * D]) for i in range(3))
    norm_one_back, gain_one_grad, shift_one_grad = norm_backward(
        back_one, unit_one, inverse_one, vector_rows[0]
    )
    input_grad = (residual_grad + norm_one_back).astype(BF)
    vector_part = jnp.stack(
        [
            gain_one_grad,
            shift_one_grad,
            projected_sums[0],
            projected_sums[2],
            out_bias_grad,
            gain_two_grad,
            shift_two_grad,
            jnp.sum(cot_float, axis=0),
        ]
    )
    small_part = pack_small(
        vector_part.reshape(8, owners, columns).transpose(1, 0, 2), bias_grad.reshape(owners, units)
    )
    qkv_g, out_g, small_g = reduce_all([qkv_t, out_t, small_part.astype(BF)], 3)
    vector_grad, b_up_grad = unpack_small(small_g, columns, units)
    vector_grad, b_up_grad = vector_grad[0], b_up_grad[0]
    grads = [qkv_g, out_g, up_g, down_g]
    lows = [item.astype(BF) for item in grads]
    m_roots = [qkv_left_root, out_left_root, up_left_root, down_right_root]
    gathered = gather_all(lows + [root.astype(BF) for root in m_roots], 4)
    grads_full, roots_full = gathered[:4], gathered[4:]
    n_roots = [qkv_right_root, out_right_root, up_right_root, down_left_root]
    m_stats = [qkv_left, out_left, up_left, down_right]
    n_stats = [qkv_right, out_right, up_right, down_left]
    rows_owned = m_stats[0].shape[0]
    new_m, new_n, steps = [], [], []
    for low, full, root, n_root, m_stat, n_stat in zip(
        lows, grads_full, roots_full, n_roots, m_stats, n_stats
    ):
        new_n.append(decay_rate * n_stat + (1.0 - decay_rate) * dot_nt(low, full))
        mine = lax.dynamic_slice_in_dim(full, me * rows_owned, rows_owned, 1)
        new_m.append(decay_rate * m_stat + (1.0 - decay_rate) * dot_tn(mine, full))
        product = dot_nn(n_root.astype(BF), full)
        steps.append(dot_nt(product.astype(BF), root))
    new_w_qkv = w_qkv - matrix_rate * steps[0].T
    new_w_out = w_out - matrix_rate * steps[1].T
    new_w_up = w_up - matrix_rate * steps[2].T
    new_w_down = w_down - matrix_rate * steps[3]
    new_vector_stat = decay_rate * vector_stat + (1.0 - decay_rate) * vector_grad * vector_grad
    new_vectors = vectors - vector_rate * vector_grad * lax.rsqrt(new_vector_stat)
    new_b_up_stat = decay_rate * b_up_stat + (1.0 - decay_rate) * b_up_grad * b_up_grad
    new_b_up = b_up - vector_rate * b_up_grad * lax.rsqrt(new_b_up_stat)
    return (
        block_output,
        input_grad,
        grads[0].T,
        grads[1].T,
        grads[2].T,
        grads[3],
        vector_grad,
        b_up_grad,
        new_m[0],
        new_n[0],
        new_m[1],
        new_n[1],
        new_m[2],
        new_n[2],
        new_n[3],
        new_m[3],
        new_vector_stat,
        new_b_up_stat,
        new_w_qkv,
        new_w_out,
        new_w_up,
        new_w_down,
        new_vectors,
        new_b_up,
    )


def solution(mesh):
    return jax.shard_map(
        shards,
        mesh=mesh,
        in_specs=(
            P(("dp", "ffn"), None),
            P(("dp", "ffn"), None),
            P(None, ("dp", "ffn")),
            P(None, ("dp", "ffn")),
            P(None, ("dp", "ffn")),
            P(("dp", "ffn"), None),
            P(None, ("dp", "ffn")),
            P(("dp", "ffn")),
            P(("dp", "ffn"), None),
            P(("dp", "ffn"), None),
            P(("dp", "ffn"), None),
            P(("dp", "ffn"), None),
            P(("dp", "ffn"), None),
            P(("dp", "ffn"), None),
            P(("dp", "ffn"), None),
            P(("dp", "ffn"), None),
            P(("dp", "ffn"), None),
            P(("dp", "ffn"), None),
            P(("dp", "ffn"), None),
            P(("dp", "ffn"), None),
            P(("dp", "ffn"), None),
            P(("dp", "ffn"), None),
            P(("dp", "ffn"), None),
            P(("dp", "ffn"), None),
            P(None, ("dp", "ffn")),
            P(("dp", "ffn")),
        ),
        out_specs=(
            P(("dp", "ffn"), None),
            P(("dp", "ffn"), None),
            P(None, ("dp", "ffn")),
            P(None, ("dp", "ffn")),
            P(None, ("dp", "ffn")),
            P(("dp", "ffn"), None),
            P(None, ("dp", "ffn")),
            P(("dp", "ffn")),
            P(("dp", "ffn"), None),
            P(("dp", "ffn"), None),
            P(("dp", "ffn"), None),
            P(("dp", "ffn"), None),
            P(("dp", "ffn"), None),
            P(("dp", "ffn"), None),
            P(("dp", "ffn"), None),
            P(("dp", "ffn"), None),
            P(None, ("dp", "ffn")),
            P(("dp", "ffn")),
            P(None, ("dp", "ffn")),
            P(None, ("dp", "ffn")),
            P(None, ("dp", "ffn")),
            P(("dp", "ffn"), None),
            P(None, ("dp", "ffn")),
            P(("dp", "ffn")),
        ),
        check_vma=False,
    )
```

time: 1990 us -> 751 us (0.38)
  waiting for transfers between devices: 1320 us -> 0 us
  Pallas kernels: 0 us -> 502 us
  matrix products: 324 us -> 185 us
  blocking collectives: 102 us -> 0 us
  local copies, waits for them, and re-layouts: 111 us -> 9.83 us
  other arithmetic: 105 us -> 48.7 us
    all_gather x14 -> x0, waiting for transfers between devices: 911 us -> none  [the longest x1 152 us: shards(): gathered = lax.all_gather(acts_two, 'ffn', axis=0, tiled=True)]
    pallas_call x0 -> x7, Pallas kernels: none -> 502 us  [the longest x2 301 us: gather_all(): pl.pallas_call(functools.partial(gather_kernel, count), out_shape=tuple((...]
    reduce_scatter x5 -> x0, waiting for transfers between devices: 341 us -> none  [the longest x1 134 us: shards(): lax.psum_scatter(jnp.dot(slope_low, up_cols.T, preferred_element_type=jnp...]
    dot_general x38 -> x27, matrix products: 324 us -> 185 us  [the longest x11 80.6 us: dot_nt(): lax.dot_general(left, right, (((1,), (1,)), ((), ())), preferred_element_...]
    all_gather x2 -> x0, blocking collectives: 78.8 us -> none  [the longest x1 71.1 us: shards(): lax.all_gather(vectors.astype(jnp.bfloat16), ('dp', 'ffn'), axis=1, tiled...]
    psum x1 -> x0, waiting for transfers between devices: 66.4 us -> none  [shards(): lax.psum(qkv_s.astype(jnp.bfloat16), 'dp').astype(jnp.float32)]
    convert_element_type x24 -> x15, other arithmetic: 58.3 us -> 15.3 us  [the longest x4 6.89 us: shards(): lows = [item.astype(BF) for item in grads]]
    unnamed x172 -> x118, local copies, waits for them, and re-layouts: 32.1 us -> 7.16 us
  transfers between devices with their start and end apart: 21 -> 0, of which waited for: 16 -> 0; matrix products, arithmetic and copies ran while one was open for 24% -> 0% of each run, Pallas kernels for 0% -> 0%
where the time goes in v1:
time: 751 us; the launch traced here: 746 us
  Pallas kernels  502 us (67%)
  matrix products  185 us (25%)
  other arithmetic  48.7 us (6%)
  local copies, waits for them, and re-layouts  9.83 us (1%)
    pallas_call x2, Pallas kernels, gather_all(): pl.pallas_call(functools.partial(gather_kernel, count), out_shape=tuple((...  301 us
    pallas_call x2, Pallas kernels, reduce_all(): pl.pallas_call(functools.partial(reduce_kernel, count), out_shape=tuple((...  141 us
    dot_general x11, matrix products, dot_nt(): lax.dot_general(left, right, (((1,), (1,)), ((), ())), preferred_element_...  80.6 us
    dot_general x10, matrix products, dot_tn(): lax.dot_general(left, right, (((0,), (0,)), ((), ())), preferred_element_...  58.7 us
    dot_general x6, matrix products, dot_nn(): return jnp.dot(left, right, preferred_element_type=F32)  45.4 us
    pallas_call x1, Pallas kernels, attend_back(): pl.pallas_call(attend_back_kernel, grid=(HEADS,), out_shape=jax.ShapeDtyp...  24.5 us
    pallas_call x1, Pallas kernels, hidden_units(): pl.pallas_call(hidden_kernel, grid=(units // block,), out_shape=(jax.Shap...  18.7 us
    pallas_call x1, Pallas kernels, attend(): pl.pallas_call(attend_kernel, grid=(HEADS,), out_shape=(jax.ShapeDtypeStr...  16.7 us

profile of v1, /device:TPU:0, one launch (start us, length us, event | category | flops | bytes accessed | tf_op | source)
XLA Modules:
  0.0 746.4 jit_solution(1674715298614128558)
XLA Ops:
  2.3 2.1 convert_reduce_fusion
  4.4 2.3 fusion.17
  11.2 0.8 copy.56
  12.8 128.6 %shard_map.433 = (bf16[4,2,4,32,128]{4,3,2,1,0:T(8,128)(2,1)}, bf16[4,2,4,96,1024]{4,3,2,1,0:T(8,128)(2,1)}, bf16[4,2,4,32,1024]{4,3,2,1,0:T(8,128)(2,1)}, bf16[...) custom-call(bf16[32,128]{1,0:T(8,128)(2,1)} %bitcast.138, bf16[96,1024]{1,0:T(8,128)(2,1)} %convert_bitcast_fusion.1.refs_1_, ...), custom_call_target="tpu_custom_call" | custom-call | tf_op jit(solution)/shard_map/pallas_call | solution.py:282
  141.4 1.1 copy.64
  143.5 12.0 %add_convert_fusion.q_ref.k_ref.v_ref = bf16[1024,3072]{1,0:T(8,128)(2,1)} fusion(f32[3072]{0:T(1024)S(1)} %pad_maximum_fusion.1, bf16[3072,1024]{1,0:T(8,128)(2,1)} %bitcast.144, bf16[1024,1024]{1,0:T(8,128)(2,1)S(1)} %copy-done.4, f32[1024]{0:T(1024)S(1)} %add.134, f32[1024]{0:T(1024)S(1)} %mul.201, f32[1024]{0:T(1024)S(1)} %add_rsqrt_fusion.1, ...), kind=kOutput, calls=%fused_computation.2 | convolution fusion | flops 6455033856 | bytes 14708736 | tf_op jit(solution)/shard_map/dot_general | solution.py:44
  155.5 16.7 %shard_map.434 = (bf16[1024,1024]{1,0:T(8,128)(2,1)S(1)}, f32[8,1,1024]{2,1,0:T(1,128)S(1)}) custom-call(bf16[1024,3072]{1,0:T(8,128)(2,1)} %add_convert_fusion.q_ref.k_ref.v_ref, bf16[1024,3072]{1,0:T(8,128)(2,1)} %add_convert_fusion.q_ref.k_ref.v_ref, bf16[1024,3072]{1,0:T(8,128)(2,1)} %add_convert_fusion.q_ref.k_ref.v_ref), custom_call_target="tpu_custom_call" | custom-call | tf_op jit(solution)/shard_map/pallas_call | solution.py:363
  172.3 2.5 fusion.71
  176.1 18.7 %shard_map.435 = (bf16[1024,4096]{1,0:T(8,128)(2,1)}, bf16[1024,4096]{1,0:T(8,128)(2,1)}) custom-call(bf16[1024,1024]{1,0:T(8,128)(2,1)S(1)} %add_convert_fusion.2.acts_ref, bf16[4096,1024]{1,0:T(8,128)(2,1)} %bitcast.119, f32[1,4096]{1,0:T(1,128)S(1)} %bitcast.101), custom_call_target="tpu_custom_call" | custom-call | tf_op jit(solution)/shard_map/pallas_call | solution.py:443
  194.8 15.4 %fusion.72 = (bf16[4096]{0:T(1024)(128)(2,1)S(1)}, bf16[1024,4096]{1,0:T(8,128)(2,1)}) fusion(bf16[1024,4096]{1,0:T(8,128)(2,1)} %get-tuple-element.53, bf16[4096,1024]{1,0:T(8,128)(2,1)} %bitcast.142, bf16[1024,1024]{1,0:T(8,128)(2,1)S(1)} %copy-done.13), kind=kOutput, calls=%fused_computation.144 | convolution fusion | flops 8606707712 | bytes 27271168 | tf_op jit(solution)/shard_map/dot_general | solution.py:44
  210.2 14.6 %add_convert_fusion.1 = bf16[1024,1024]{1,0:T(8,128)(2,1)} fusion(f32[1024,1024]{1,0:T(8,128)S(1)} %get-tuple-element.167, f32[1024]{0:T(1024)S(1)} %add.148, bf16[1024,4096]{1,0:T(8,128)(2,1)} %get-tuple-element.51, bf16[4096,1024]{1,0:T(8,128)(2,1)} %bitcast.143), kind=kOutput, calls=%fused_computation.33 | convolution fusion | flops 8593080320 | bytes 23072768 | tf_op jit(solution)/shard_map/dot_general | solution.py:52
  224.9 15.9 %multiply_reduce_fusion = (bf16[1024]{0:T(1024)(128)(2,1)S(1)}, f32[1024]{0:T(1024)S(1)}, f32[1024]{0:T(1024)S(1)}, bf16[1024]{0:T(1024)(128)(2,1)S(1)}, f32[1024,1024]{1,0:T(8,128)}) fusion(f32[1024,1024]{1,0:T(8,128)S(1)} %get-tuple-element.167, f32[1024]{0:T(1024)S(1)} %add_rsqrt_fusion, f32[1024]{0:T(1024)S(1)} %broadcast_multiply_fusion.4, ...), kind=kOutput, calls=%fused_computation.29 | convolution fusion | flops 8599367680 | bytes 25190400 | tf_op jit(solution)/shard_map/dot_general | solution.py:52
  240.8 11.7 %convolution_convert_fusion.1 = bf16[4096,1024]{1,0:T(8,128)(2,1)} fusion(bf16[1024,4096]{1,0:T(8,128)(2,1)S(1)} %copy-done.43, bf16[1024,1024]{1,0:T(8,128)(2,1)S(1)} %copy-done.13), kind=kOutput, calls=%fused_computation.4 | convolution fusion | flops 8594128896 | bytes 18874368 | tf_op jit(solution)/shard_map/dot_general | solution.py:48
  252.6 6.7 convert_reduce_fusion.1
  259.3 3.7 convolution_convert_fusion.2
  263.0 2.3 convolution_convert_fusion.6.do_ref
  265.4 24.5 %shard_map.436 = bf16[3,1024,1024]{2,1,0:T(8,128)(2,1)} custom-call(bf16[1024,3072]{1,0:T(8,128)(2,1)} %add_convert_fusion.q_ref.k_ref.v_ref, bf16[1024,3072]{1,0:T(8,128)(2,1)} %add_convert_fusion.q_ref.k_ref.v_ref, bf16[1024,3072]{1,0:T(8,128)(2,1)} %add_convert_fusion.q_ref.k_ref.v_ref, bf16[1024,1024]{1,0:T(8,128)(2,1)S(1)} %convolution_convert_fusion.6.do_ref, ...), custom_call_target="tpu_custom_call" | custom-call | tf_op jit(solution)/shard_map/pallas_call | solution.py:408
  290.0 4.5 reduce
  294.7 5.1 convolution_convert_fusion.3
  299.9 2.8 convolution_convert_fusion.4
  302.7 2.8 convolution_convert_fusion.5
  305.6 13.4 %pad_maximum_fusion = bf16[3072,1024]{1,0:T(8,128)(2,1)} fusion(bf16[1024,1024]{1,0:T(8,128)(2,1)S(1)} %convolution_convert_fusion.3, bf16[1024,1024]{1,0:T(8,128)(2,1)S(1)} %convolution_convert_fusion.4, bf16[1024,1024]{1,0:T(8,128)(2,1)S(1)} %convolution_convert_fusion.5), kind=kLoop, calls=%fused_computation.5 | loop fusion | flops 18874368 | bytes 12582912 | tf_op jit(solution)/shard_map/concatenate | solution.py:550
  319.0 2.3 fusion.20
  321.3 4.4 fusion.22
  325.8 5.8 fusion.16
  331.6 3.1 fusion.15
  335.8 57.4 %shard_map.437 = (f32[96,1024]{1,0:T(8,128)}, f32[32,1024]{1,0:T(8,128)}, f32[32,128]{1,0:T(8,128)}) custom-call(bf16[4,2,4,96,1024]{4,3,2,1,0:T(8,128)(2,1)} %bitcast.115, bf16[4,2,4,32,1024]{4,3,2,1,0:T(8,128)(2,1)} %bitcast.126, bf16[4,2,4,32,128]{4,3,2,1,0:T(8,128)(2,1)} %bitcast.131), custom_call_target="tpu_custom_call" | custom-call | tf_op jit(solution)/shard_map/pallas_call | solution.py:309
  393.9 1.2 multiply_subtract_fusion.1
  395.8 1.5 convert_element_type.194.refs_1_
  397.4 1.7 convert_element_type.193.refs_0_
  399.1 14.8 %convolution_convert_fusion = bf16[4096,1024]{1,0:T(8,128)(2,1)} fusion(bf16[1024,4096]{1,0:T(8,128)(2,1)} %get-tuple-element.171, bf16[1024,1024]{1,0:T(8,128)(2,1)S(1)} %add_convert_fusion.2.acts_ref), kind=kOutput, calls=%fused_computation.3 | convolution fusion | flops 8594128896 | bytes 18874368 | tf_op jit(solution)/shard_map/dot_general | solution.py:48
  413.9 83.4 %shard_map.438 = (f32[128,1024]{1,0:T(8,128)}, f32[128,1024]{1,0:T(8,128)}) custom-call(bf16[4,2,4,128,1024]{4,3,2,1,0:T(8,128)(2,1)} %bitcast.121, bf16[4,2,4,128,1024]{4,3,2,1,0:T(8,128)(2,1)} %bitcast.122), custom_call_target="tpu_custom_call" | custom-call | tf_op jit(solution)/shard_map/pallas_call | solution.py:309
  497.3 1.9 convert_element_type.195.refs_2_
  499.1 1.8 convert_element_type.196.refs_3_
  500.9 2.0 copy.59
  503.0 172.4 %shard_map.439 = (bf16[4,2,4,96,1024]{4,3,2,1,0:T(8,128)(2,1)}, bf16[4,2,4,32,1024]{4,3,2,1,0:T(8,128)(2,1)}, bf16[4,2,4,128,1024]{4,3,2,1,0:T(8,128)(2,1)}, bf1...) custom-call(bf16[96,1024]{1,0:T(8,128)(2,1)} %convert_element_type.1, ...), custom_call_target="tpu_custom_call" | custom-call | tf_op jit(solution)/shard_map/pallas_call | solution.py:282
  675.4 6.0 fusion.30
  681.4 4.1 fusion.33
  685.5 3.0 fusion.36
  688.5 3.1 fusion.31
  691.6 5.6 fusion.32
  697.3 3.1 fusion.19
  700.4 2.6 fusion.35
  703.0 9.4 %fusion.29 = f32[1024,128]{1,0:T(8,128)} fusion(f32[1024,128]{1,0:T(8,128)S(1)} %copy-done.15, bf16[1024,1024]{1,0:T(8,128)(2,1)} %bitcast.128, bf16[4096,1024]{1,0:T(8,128)(2,1)} %bitcast.105, f32[128,4096]{1,0:T(8,128)} %param.47), kind=kOutput, calls=%fused_computation.58 | convolution fusion | flops 1343094784 | bytes 13631488 | tf_op jit(solution)/shard_map/dot_general | solution.py:44
  712.4 7.6 %fusion.8 = f32[128,4096]{1,0:T(8,128)} fusion(f32[128,4096]{1,0:T(8,128)S(1)} %copy-done.10, bf16[128,1024]{1,0:T(8,128)(2,1)S(1)} %copy-done.9, bf16[4096,1024]{1,0:T(8,128)(2,1)} %bitcast.106), kind=kOutput, calls=%fused_computation.18 | convolution fusion | flops 1074790400 | bytes 12845056 | tf_op jit(solution)/shard_map/dot_general | solution.py:44
  720.1 6.4 fusion.34
  726.5 9.8 %fusion.28 = f32[128,1024]{1,0:T(8,128)} fusion(f32[128,1024]{1,0:T(8,128)S(1)} %copy-done.17, bf16[1024,1024]{1,0:T(8,128)(2,1)} %bitcast.127, bf16[4096,1024]{1,0:T(8,128)(2,1)} %bitcast.103, f32[128,4096]{1,0:T(8,128)} %param.48), kind=kOutput, calls=%fused_computation.56 | convolution fusion | flops 1343094784 | bytes 13631488 | tf_op jit(solution)/shard_map/dot_general | solution.py:44
  736.3 7.7 %fusion.7 = f32[128,4096]{1,0:T(8,128)} fusion(f32[128,4096]{1,0:T(8,128)S(1)} %copy-done.11, bf16[128,1024]{1,0:T(8,128)(2,1)S(1)} %copy-done.8, bf16[4096,1024]{1,0:T(8,128)(2,1)} %bitcast.104), kind=kOutput, calls=%fused_computation.16 | convolution fusion | flops 1074790400 | bytes 12845056 | tf_op jit(solution)/shard_map/dot_general | solution.py:44
  (168 shorter events, 14.6 us)
Async XLA Ops:
  0.7 11.4 %copy-start.16 = (f32[128,1024]{1,0:T(8,128)S(1)}, f32[128,1024]{1,0:T(8,128)}, u32[]{:S(2)}) copy-start(f32[128,1024]{1,0:T(8,128)} %param.31) | copy-start | bytes 1572868
  0.7 10.5 %copy-start.14 = (f32[1024,128]{1,0:T(8,128)S(1)}, f32[1024,128]{1,0:T(8,128)}, u32[]{:S(2)}) copy-start(f32[1024,128]{1,0:T(8,128)} %param.30) | copy-start | bytes 1572868
  0.7 9.8 %copy-start.19 = (f32[1024,96]{0,1:T(8,128)S(1)}, f32[1024,96]{0,1:T(8,128)}, u32[]{:S(2)}) copy-start(f32[1024,96]{0,1:T(8,128)} %param.28) | copy-start | bytes 1179652
  2.2 5.1 copy-start.33
  2.2 5.7 copy-start.34
  2.2 6.3 copy-start.35
  2.2 7.0 copy-start.36
  2.3 7.6 %copy-start.25 = (f32[1024,32]{0,1:T(8,128)S(1)}, f32[1024,32]{0,1:T(8,128)}, u32[]{:S(2)}) copy-start(f32[1024,32]{0,1:T(8,128)} %param.29) | copy-start | bytes 393220
  2.3 141.2 %copy-start.4 = (bf16[1024,1024]{1,0:T(8,128)(2,1)S(1)}, bf16[1024,1024]{1,0:T(8,128)(2,1)}, u32[]{:S(2)}) copy-start(bf16[1024,1024]{1,0:T(8,128)(2,1)} %param.26) | copy-start | bytes 6291460
  155.5 16.8 %copy-start.44 = (bf16[4,2,4,32,1024]{4,3,2,1,0:T(8,128)(2,1)S(1)}, bf16[4,2,4,32,1024]{4,3,2,1,0:T(8,128)(2,1)}, u32[]{:S(2)}) copy-start(bf16[4,2,4,32,1024]{4,3,2,1,0:T(8,128)(2,1)} %get-tuple-element.49) | copy-start | bytes 6291460
  174.8 50.1 %copy-start.2 = (f32[1024,1024]{1,0:T(8,128)}, f32[1024,1024]{1,0:T(8,128)S(1)}, u32[]{:S(2)}) copy-start(f32[1024,1024]{1,0:T(8,128)S(1)} %get-tuple-element.167) | copy-start | bytes 12582916
  176.1 18.7 %copy-start.13 = (bf16[1024,1024]{1,0:T(8,128)(2,1)S(1)}, bf16[1024,1024]{1,0:T(8,128)(2,1)}, u32[]{:S(2)}) copy-start(bf16[1024,1024]{1,0:T(8,128)(2,1)} %param.27) | copy-start | bytes 6291460
  224.9 15.9 %copy-start.43 = (bf16[1024,4096]{1,0:T(8,128)(2,1)S(1)}, bf16[1024,4096]{1,0:T(8,128)(2,1)}, u32[]{:S(2)}) copy-start(bf16[1024,4096]{1,0:T(8,128)(2,1)} %get-tuple-element.51) | copy-start | bytes 25165828
  252.6 6.7 copy-start.1
  259.3 3.7 copy-start.6
  259.3 3.7 copy-start.45
  294.7 5.1 copy-start.3
  294.7 5.1 copy-start.5
  299.8 19.1 %slice-start.4 = ((s8[6291456]{0:T(1024)(128)(4,1)}), s8[4194304]{0:T(1024)(128)(4,1)S(1)}, s32[]{:S(2)}) async-start(s8[6291456]{0:T(1024)(128)(4,1)} %bitcast.145), calls=%async_computation.4 | async-start | bytes 8388608
  302.7 16.3 %slice-start.5 = ((s8[6291456]{0:T(1024)(128)(4,1)}), s8[2097152]{0:T(1024)(128)(4,1)S(1)}, s32[]{:S(2)}) async-start(s8[6291456]{0:T(1024)(128)(4,1)} %bitcast.145), calls=%async_computation.5 | async-start | bytes 4194304
  325.8 5.8 copy-start.7
  335.8 58.1 %copy-start.41 = (f32[128]{0:T(128)S(1)}, f32[128]{0:T(128)}, u32[]{:S(2)}) copy-start(f32[128]{0:T(128)} %param.33) | copy-start | bytes 1540
  335.8 58.1 %copy-start.42 = (f32[128]{0:T(128)S(1)}, f32[128]{0:T(128)}, u32[]{:S(2)}) copy-start(f32[128]{0:T(128)} %param.51) | copy-start | bytes 1540
  335.8 59.4 %copy-start.39 = (f32[8,32]{1,0:T(8,128)S(1)}, f32[8,32]{1,0:T(8,128)}, u32[]{:S(2)}) copy-start(f32[8,32]{1,0:T(8,128)} %param.32) | copy-start | bytes 3076
  335.8 59.4 %copy-start.40 = (f32[8,32]{1,0:T(8,128)S(1)}, f32[8,32]{1,0:T(8,128)}, u32[]{:S(2)}) copy-start(f32[8,32]{1,0:T(8,128)} %param.50) | copy-start | bytes 3076
  395.2 18.6 %copy-start.38 = (f32[8,32]{1,0:T(8,128)}, f32[8,32]{1,0:T(8,128)S(1)}, u32[]{:S(2)}) copy-start(f32[8,32]{1,0:T(8,128)S(1)} %squeeze_reshape.3) | copy-start | bytes 3076
  413.9 261.5 %copy-start.20 = (f32[1024,96]{0,1:T(8,128)S(1)}, f32[1024,96]{0,1:T(8,128)}, u32[]{:S(2)}) copy-start(f32[1024,96]{0,1:T(8,128)} %param.28) | copy-start | bytes 1179652
  497.3 178.1 %copy-start.22 = (f32[96,3072]{1,0:T(8,128)S(1)}, f32[96,3072]{1,0:T(8,128)}, u32[]{:S(2)}) copy-start(f32[96,3072]{1,0:T(8,128)} %param.43) | copy-start | bytes 3538948
  675.3 6.0 copy-start.26
  675.4 6.0 copy-start.30
  681.3 4.2 copy-start.24
  681.4 4.2 copy-start.31
  681.4 7.2 copy-start.32
  681.4 10.3 %copy-start.37 = (f32[32,1024]{1,0:T(8,128)S(1)}, f32[32,1024]{1,0:T(8,128)}, u32[]{:S(2)}) copy-start(f32[32,1024]{1,0:T(8,128)} %param.34) | copy-start | bytes 393220
  681.4 15.8 %slice-start.2 = ((s8[6291456]{0:T(1024)(128)(4,1)}), s8[2097152]{0:T(1024)(128)(4,1)S(1)}, s32[]{:S(2)}) async-start(s8[6291456]{0:T(1024)(128)(4,1)} %bitcast.112), calls=%async_computation.2 | async-start | bytes 4194304
  688.5 8.7 %slice-start.3 = ((s8[6291456]{0:T(1024)(128)(4,1)}), s8[4194304]{0:T(1024)(128)(4,1)S(1)}, s32[]{:S(2)}) async-start(s8[6291456]{0:T(1024)(128)(4,1)} %bitcast.112), calls=%async_computation.3 | async-start | bytes 8388608
  688.5 8.7 %copy-start.18 = (bf16[96,1024]{1,0:T(8,128)(2,1)S(1)}, bf16[96,1024]{1,0:T(8,128)(2,1)}, u32[]{:S(2)}) copy-start(bf16[96,1024]{1,0:T(8,128)(2,1)} %convert_element_type.193.refs_0_) | copy-start | bytes 589828
  688.5 8.7 %copy-start.23 = (f32[96,3072]{1,0:T(8,128)S(1)}, f32[96,3072]{1,0:T(8,128)}, u32[]{:S(2)}) copy-start(f32[96,3072]{1,0:T(8,128)} %param.35) | copy-start | bytes 3538948
  691.6 8.7 %slice-start = ((s8[8388608]{0:T(1024)(128)(4,1)}), s8[4194304]{0:T(1024)(128)(4,1)S(1)}, s32[]{:S(2)}) async-start(s8[8388608]{0:T(1024)(128)(4,1)} %bitcast.107), calls=%async_computation | async-start | bytes 8388608
  703.0 9.4 %copy-start.9 = (bf16[128,1024]{1,0:T(8,128)(2,1)S(1)}, bf16[128,1024]{1,0:T(8,128)(2,1)}, u32[]{:S(2)}) copy-start(bf16[128,1024]{1,0:T(8,128)(2,1)} %convert_element_type.195.refs_2_) | copy-start | bytes 786436
  703.0 9.4 %copy-start.10 = (f32[128,4096]{1,0:T(8,128)S(1)}, f32[128,4096]{1,0:T(8,128)}, u32[]{:S(2)}) copy-start(f32[128,4096]{1,0:T(8,128)} %param.39) | copy-start | bytes 6291460
  712.4 7.6 %copy-start.29 = (f32[32,1024]{1,0:T(8,128)S(1)}, f32[32,1024]{1,0:T(8,128)}, u32[]{:S(2)}) copy-start(f32[32,1024]{1,0:T(8,128)} %param.41) | copy-start | bytes 393220
  720.1 6.4 copy-start.17
  726.5 9.8 %copy-start.8 = (bf16[128,1024]{1,0:T(8,128)(2,1)S(1)}, bf16[128,1024]{1,0:T(8,128)(2,1)}, u32[]{:S(2)}) copy-start(bf16[128,1024]{1,0:T(8,128)(2,1)} %convert_element_type.196.refs_3_) | copy-start | bytes 786436
  726.5 9.8 %copy-start.11 = (f32[128,4096]{1,0:T(8,128)S(1)}, f32[128,4096]{1,0:T(8,128)}, u32[]{:S(2)}) copy-start(f32[128,4096]{1,0:T(8,128)} %param.40) | copy-start | bytes 6291460
  736.3 7.7 %copy-start.21 = (f32[96,1024]{1,0:T(8,128)S(1)}, f32[96,1024]{1,0:T(8,128)}, u32[]{:S(2)}) copy-start(f32[96,1024]{1,0:T(8,128)} %get-tuple-element.55) | copy-start | bytes 1179652
  736.3 8.4 %copy-start.27 = (f32[32,1024]{1,0:T(8,128)S(1)}, f32[32,1024]{1,0:T(8,128)}, u32[]{:S(2)}) copy-start(f32[32,1024]{1,0:T(8,128)} %get-tuple-element.56) | copy-start | bytes 393220
  736.3 9.1 %copy-start.12 = (f32[128,1024]{1,0:T(8,128)S(1)}, f32[128,1024]{1,0:T(8,128)}, u32[]{:S(2)}) copy-start(f32[128,1024]{1,0:T(8,128)} %get-tuple-element.203) | copy-start | bytes 1572868
  (4 other events, 11.4 us)

commit v2 on v1

v2 whole, which is shorter than its diff:
```python
import functools

import jax
import jax.numpy as jnp
from jax import lax
from jax.experimental import pallas as pl
from jax.experimental.pallas import tpu as pltpu
from jax.sharding import PartitionSpec as P

D = 1024
HEADS = 8
HEAD_DIM = 128
MESH = pl.DeviceIdType.MESH
ALL = ("dp", "ffn")
BF = jnp.bfloat16
F32 = jnp.float32
MIB = 2**20

norm_epsilon = 1e-05
decay_rate = 0.5
matrix_rate = 0.5
vector_rate = 0.1
masked_score = -1e30


def layer_norm(values, gain, shift):
    center = values - jnp.mean(values, axis=-1, keepdims=True)
    inverse = lax.rsqrt(jnp.mean(center * center, axis=-1, keepdims=True) + norm_epsilon)
    normed = center * inverse
    return (normed * gain + shift, normed, inverse)


def norm_backward(grad, normed, inverse, gain):
    scaled = grad * gain
    inner = (
        scaled
        - jnp.mean(scaled, axis=-1, keepdims=True)
        - normed * jnp.mean(scaled * normed, axis=-1, keepdims=True)
    )
    return (inner * inverse, jnp.sum(grad * normed, axis=0), jnp.sum(grad, axis=0))


def dot_nt(left, right):
    return lax.dot_general(left, right, (((1,), (1,)), ((), ())), preferred_element_type=F32)


def dot_tn(left, right):
    return lax.dot_general(left, right, (((0,), (0,)), ((), ())), preferred_element_type=F32)


def dot_nn(left, right):
    return jnp.dot(left, right, preferred_element_type=F32)


def coords():
    dp = lax.axis_index("dp")
    return dp // 2, dp % 2, lax.axis_index("ffn")


def flip(value, mask):
    result = value
    bit = 1
    while bit <= mask:
        if mask & bit:
            result = result + bit - 2 * bit * ((result // bit) % 2)
        bit *= 2
    return result


def greet():
    p, c, z = coords()
    barrier = pltpu.get_barrier_semaphore()
    peers = [(flip(p, 1) * 2 + c, z), (flip(p, 2) * 2 + c, z), (p * 2 + 1 - c, z)]
    peers += [(p * 2 + c, flip(z, k)) for k in (1, 2, 3)]
    for peer in peers:
        pl.semaphore_signal(barrier, inc=1, device_id=peer, device_id_type=MESH)
    pl.semaphore_wait(barrier, len(peers))


FIRST = (1, 2)
SECOND = (2, 1)


class Copies:
    def __init__(self, send, recv):
        self.send, self.recv, self.made = send, recv, {}

    def copy(self, name):
        at, make = self.made[name]
        src, dst, device = make()
        return pltpu.make_async_remote_copy(
            src, dst, self.send.at[at], self.recv.at[at], device_id=device, device_id_type=MESH
        )

    def post(self, name, make):
        self.made[name] = (len(self.made), make)
        self.copy(name).start()

    def got(self, name):
        self.copy(name).wait_recv()

    def sent(self):
        for name in self.made:
            self.copy(name).wait_send()


def gather_plan(place, shard, out, send, recv, local_sem):
    p, c, z = place
    half_rows = shard.shape[0] // 2
    copies = Copies(send, recv)

    def local():
        return pltpu.make_async_copy(shard, out.at[p, c, z], local_sem)

    def half(ref, h):
        return ref.at[pl.ds(h * half_rows, half_rows)]

    def along_z(k):
        copies.post(("z", k), lambda: (shard, out.at[p, c, z], (p * 2 + c, flip(z, k))))

    def spread(k):
        for name, turn in (("first", FIRST), ("second", SECOND)):
            for h in (0, 1):

                def make(h=h, turn=turn):
                    dst = half(out.at[p, c, flip(z, k)], h)
                    return (dst if k else half(shard, h)), dst, (flip(p, turn[h]) * 2 + c, z)

                copies.post((name, k, h), make)

    def begin():
        along_z(1)
        spread(0)
        local().start()

    def landed(k):
        copies.got(("z", k))
        if k < 3:
            along_z(k + 1)
        spread(k)

    def forward(k):
        for h in (0, 1):
            copies.got(("first", k, h))

            def make(h=h):
                piece = half(out.at[flip(p, FIRST[h]), c, flip(z, k)], h)
                return piece, piece, (flip(p, SECOND[h]) * 2 + c, z)

            copies.post(("relay", k, h), make)

    def share(k):
        for h in (0, 1):
            copies.got(("second", k, h))
            copies.got(("relay", k, h))
        if k == 0:
            local().wait()

        def make():
            piece = out.at[:, c, flip(z, k)]
            return piece, piece, (p * 2 + 1 - c, z)

        copies.post(("core", k), make)

    def finish():
        for k in range(4):
            copies.got(("core", k))
        copies.sent()

    do = functools.partial
    plan = [begin, do(landed, 1), do(forward, 0), do(landed, 2), do(forward, 1), do(share, 0)]
    plan += [do(landed, 3), do(forward, 2), do(share, 1), do(forward, 3), do(share, 2)]
    return plan + [do(share, 3), finish]


def reduce_plan(
    place, parts, out, held, from_core, from_second, from_first, from_z, send, recv, load
):
    p, c, z = place
    half_rows = parts.shape[-2] // 2
    copies = Copies(send, recv)
    order = (3, 2, 1, 0)

    def half(h):
        return pl.ds(h * half_rows, half_rows)

    def local(k):
        return pltpu.make_async_copy(parts.at[:, c, flip(z, k)], held.at[k], load.at[k])

    def to_core(k):
        copies.post(
            ("core", k),
            lambda: (parts.at[:, 1 - c, flip(z, k)], from_core.at[k], (p * 2 + 1 - c, z)),
        )
        local(k).start()

    def add(dst, *sources):
        total = dst[...].astype(F32)
        for source in sources:
            total = total + source[...].astype(F32)
        dst[...] = total.astype(BF)

    def begin():
        to_core(order[0])

    def cores(k):
        local(k).wait()
        copies.got(("core", k))
        if k:
            to_core(order[order.index(k) + 1])
        for h in (0, 1):
            for j, mask in ((1, 3), (0, SECOND[h])):
                q = flip(p, mask)
                add(held.at[k, q, half(h)], from_core.at[k, q, half(h)])
                copies.post(
                    ("second", k, h, j),
                    lambda h=h, j=j, mask=mask: (
                        held.at[k, flip(p, mask), half(h)],
                        from_second.at[k, h, j],
                        (flip(p, SECOND[h]) * 2 + c, z),
                    ),
                )
        for h in (0, 1):
            for mask in (0, FIRST[h]):
                q = flip(p, mask)
                add(held.at[k, q, half(h)], from_core.at[k, q, half(h)])

    def second(k):
        for h in (0, 1):
            copies.got(("second", k, h, 1))
            add(held.at[k, flip(p, FIRST[h]), half(h)], from_second.at[k, h, 1])
            copies.post(
                ("first", k, h),
                lambda h=h: (
                    held.at[k, flip(p, FIRST[h]), half(h)],
                    from_first.at[k, h],
                    (flip(p, FIRST[h]) * 2 + c, z),
                ),
            )

    def first(k):
        for h in (0, 1):
            copies.got(("second", k, h, 0))
            copies.got(("first", k, h))
            add(held.at[k, p, half(h)], from_second.at[k, h, 0], from_first.at[k, h])
        if k:
            copies.post(
                ("z", k), lambda: (held.at[k, p], from_z.at[k - 1], (p * 2 + c, flip(z, k)))
            )

    def finish():
        for k in (3, 2, 1):
            copies.got(("z", k))
        total = held[0, p].astype(F32)
        for k in range(3):
            total = total + from_z[k].astype(F32)
        out[...] = total
        copies.sent()

    do = functools.partial
    plan = [begin, do(cores, 3), do(cores, 2), do(second, 3), do(cores, 1), do(second, 2)]
    plan += [do(first, 3), do(cores, 0), do(second, 1), do(first, 2), do(second, 0)]
    return plan + [do(first, 1), do(first, 0), finish]


def merge_plans(plans, offset):
    total = max(len(plan) + offset * g for g, plan in enumerate(plans))
    merged = []
    for t in range(total):
        for g, plan in enumerate(plans):
            at = t - offset * g
            if 0 <= at < len(plan):
                merged.append(plan[at])
    return merged


ANYWHERE = pl.BlockSpec(memory_space=pl.ANY)
COPIES = 31


class Gather:
    def __init__(self, shard):
        self.array = shard
        self.rows, self.width = shard.shape
        self.shape = jax.ShapeDtypeStruct((4, 2, 4, self.rows, self.width), BF)
        self.spec = ANYWHERE
        sems = pltpu.SemaphoreType.DMA((COPIES,))
        self.scratch = [sems, sems, pltpu.SemaphoreType.DMA]
        self.plan = gather_plan

    def finish(self, out):
        return out.reshape(-1, self.width)

    def plainly(self):
        return lax.all_gather(self.array, ALL, axis=0, tiled=True)


class Reduce:
    def __init__(self, parts):
        devices = lax.axis_size("dp") * lax.axis_size("ffn")
        self.parts = parts
        self.rows, width = parts.shape[0] // devices, parts.shape[1]
        self.shape = jax.ShapeDtypeStruct((self.rows, width), F32)
        self.spec = pl.BlockSpec((self.rows, width), lambda *_: (0, 0))
        sems = pltpu.SemaphoreType.DMA((COPIES,))
        rows = self.rows
        self.scratch = [
            pltpu.VMEM((4, 4, rows, width), BF),
            pltpu.VMEM((4, 4, rows, width), BF),
            pltpu.VMEM((4, 2, 2, rows // 2, width), BF),
            pltpu.VMEM((4, 2, rows // 2, width), BF),
            pltpu.VMEM((3, rows, width), BF),
            sems,
            sems,
            pltpu.SemaphoreType.DMA((4,)),
        ]
        self.plan = reduce_plan

    @property
    def array(self):
        return self.parts.reshape(4, 2, 4, self.rows, self.parts.shape[1])

    def finish(self, out):
        return out

    def plainly(self):
        return lax.psum_scatter(self.parts, ALL, scatter_dimension=0, tiled=True).astype(F32)


def on_fast_grid():
    return lax.axis_size("dp") == 8 and lax.axis_size("ffn") == 4


def fused_call(body, steps, ins, outs, scratch, jobs, collective_id, spread=None):
    plainly = not (on_fast_grid() and all(job.rows % 32 == 0 for job in jobs))
    run = [] if plainly else jobs
    counts = [len(ins), len(run), len(outs), len(run), len(scratch)]

    def kernel(*refs):
        groups = []
        at = 0
        for count in counts:
            groups.append(refs[at : at + count])
            at += count
        own_in, job_in, own_out, job_out, own_scratch = groups
        t = pl.program_id(0)
        if run:
            place = coords()
            plans = []
            for job, src, dst in zip(run, job_in, job_out):
                plans.append(job.plan(place, src, dst, *refs[at : at + len(job.scratch)]))
                at += len(job.scratch)
            merged = merge_plans(plans, 7)
            stops = spread or steps
            for step in range(steps):
                now = [m for i, m in enumerate(merged[:-1]) if i * stops // len(merged) == step]
                if step == 0:
                    now = [greet] + now
                if now:

                    @pl.when(t == step)
                    def _(now=now):
                        for each in now:
                            each()

        if body is not None:
            body(t, *own_in, *own_out, *own_scratch)
        if run:

            @pl.when(t == steps - 1)
            def _():
                merged[-1]()

    all_scratch = list(scratch)
    for job in run:
        all_scratch += job.scratch
    extra = dict(collective_id=collective_id, has_side_effects=True) if run else {}
    results = pl.pallas_call(
        kernel,
        grid=(steps,),
        out_shape=tuple(o[0] for o in outs) + tuple(job.shape for job in run),
        in_specs=[i[1] for i in ins] + [ANYWHERE] * len(run),
        out_specs=tuple(o[1] for o in outs) + tuple(job.spec for job in run),
        scratch_shapes=all_scratch,
        compiler_params=pltpu.CompilerParams(vmem_limit_bytes=60 * MIB, **extra),
    )(*[i[0] for i in ins], *[job.array for job in run])
    own = list(results[: len(outs)])
    if plainly:
        return own, [job.plainly() for job in jobs]
    return own, [job.finish(out) for job, out in zip(jobs, results[len(outs) :])]


def transfer(jobs, collective_id):
    if not (on_fast_grid() and all(job.rows % 32 == 0 for job in jobs)):
        return [job.plainly() for job in jobs]
    return fused_call(None, 1, [], [], [], jobs, collective_id)[1]


def whole(array):
    rank = len(array.shape)
    spec = pl.BlockSpec(array.shape, lambda t: (0,) * rank, pipeline_mode=pl.Buffered(1))
    return array, spec


def block(array, shape, at):
    return array, pl.BlockSpec(shape, at)


def result(shape, dtype, tile=None, at=None):
    rank = len(shape)
    if tile is None:
        return jax.ShapeDtypeStruct(shape, dtype), pl.BlockSpec(shape, lambda t: (0,) * rank)
    return jax.ShapeDtypeStruct(shape, dtype), pl.BlockSpec(tile, at)


def chunks(rows, size, body):
    @pl.loop(0, rows // size)
    def _(i):
        body(pl.ds(pl.multiple_of(i * size, size), size))


QUERY_BLOCK = 256
CHUNK = 128
UNITS = 512


def head_slope(head):
    level = head.astype(F32) + 1.0
    return jnp.exp2(jnp.full((1, 1), -8.0 / HEADS, F32) * level)


def scores_t(query, keys, slope, start, rows):
    at_key = lax.broadcasted_iota(jnp.int32, (rows, 1), 0).astype(F32)
    scores = dot_nt(keys, query) * HEAD_DIM ** (-0.5) + at_key * slope
    at_key = lax.broadcasted_iota(jnp.int32, (rows, QUERY_BLOCK), 0)
    at_query = lax.broadcasted_iota(jnp.int32, (rows, QUERY_BLOCK), 1) + start
    return jnp.where(at_key <= at_query, scores, masked_score)


def attend_body(t, x, vec, wq, wk, wv, head_vec, qkv, mixed, lse, acts):
    length = x.shape[0]

    @pl.when(t == 0)
    def _():
        def norm(rows):
            normed = layer_norm(x[rows, :].astype(F32), vec[0:1, :], vec[1:2, :])[0]
            acts[rows, :] = normed.astype(BF)

        chunks(length, CHUNK, norm)

    weights = jnp.concatenate([wq[...], wk[...], wv[...]], axis=0)
    projected = dot_nt(acts[...], weights)
    qkv[0] = (projected[:, :HEAD_DIM] + head_vec[2:3, :]).astype(BF)
    qkv[1] = projected[:, HEAD_DIM : 2 * HEAD_DIM].astype(BF)
    values = projected[:, 2 * HEAD_DIM :] + head_vec[3:4, :]
    qkv[2] = values.astype(BF)
    values_t = values.T.astype(BF)
    slope = head_slope(t)
    for start in range(0, length, QUERY_BLOCK):
        rows = start + QUERY_BLOCK
        scores = scores_t(qkv[0, start:rows, :], qkv[1, :rows, :], slope, start, rows)
        highest = jnp.max(scores, axis=0, keepdims=True)
        weights = jnp.exp(scores - highest)
        totals = jnp.sum(weights, axis=0, keepdims=True)
        mix = dot_nn(values_t[:, :rows], weights.astype(BF)) / totals
        mixed[start:rows, :] = mix.T.astype(BF)
        lse[0, :, start:rows] = highest + jnp.log(totals)


def attend(x, vec, qkv_full, jobs, collective_id):
    tokens = x.shape[0]
    head_rows = lambda part: block(
        qkv_full, (HEAD_DIM, D), lambda h: (part * HEADS + h, 0)
    )
    return fused_call(
        attend_body,
        HEADS,
        [
            whole(x),
            whole(vec),
            head_rows(0),
            head_rows(1),
            head_rows(2),
            block(vec, (8, HEAD_DIM), lambda h: (0, h)),
        ],
        [
            result((3, tokens, D), BF, (3, tokens, HEAD_DIM), lambda h: (0, 0, h)),
            result((tokens, D), BF, (tokens, HEAD_DIM), lambda h: (0, h)),
            result((HEADS, 1, tokens), F32, (1, 1, tokens), lambda h: (h, 0, 0)),
            result((tokens, D), BF),
        ],
        [],
        jobs,
        collective_id,
    )


def gelu_pair(pre):
    half = 0.5 * (1.0 + lax.erf(pre * 0.7071067811865476))
    slope = half + pre * jnp.exp(-0.5 * pre * pre) * 0.3989422804014327
    return pre * half, slope


def hidden_body(t, x, mixed, out_w, vec, dy, up, bias, residual, acts, hidden, slope, down_t):
    tokens = x.shape[0]

    @pl.when(t == 0)
    def _():
        def enter(rows):
            attended = dot_nt(mixed[rows, :], out_w[...]) + vec[4:5, :]
            here = x[rows, :].astype(F32) + attended
            residual[rows, :] = here
            acts[rows, :] = layer_norm(here, vec[5:6, :], vec[6:7, :])[0].astype(BF)

        chunks(tokens, 2 * CHUNK, enter)

    for start in range(0, tokens, 256):
        rows = slice(start, start + 256)
        pre = dot_nt(acts[rows, :], up[...]) + bias[...]
        value, steep = gelu_pair(pre)
        hidden[rows, :] = value.astype(BF)
        slope[rows, :] = steep.astype(BF)
    down_t[...] = dot_tn(hidden[...], dy[...]).astype(BF)


def hidden_forward(x, mixed, out_full, vec, dy, up_full, bias, jobs, collective_id):
    tokens = x.shape[0]
    units = up_full.shape[0]
    return fused_call(
        hidden_body,
        units // UNITS,
        [
            whole(x),
            whole(mixed),
            whole(out_full),
            whole(vec),
            whole(dy),
            block(up_full, (UNITS, D), lambda n: (n, 0)),
            block(bias, (1, UNITS), lambda n: (0, n)),
        ],
        [
            result((tokens, D), F32),
            result((tokens, D), BF),
            result((tokens, units), BF, (tokens, UNITS), lambda n: (0, n)),
            result((tokens, units), BF, (tokens, UNITS), lambda n: (0, n)),
            result((units, D), BF, (UNITS, D), lambda n: (n, 0)),
        ],
        [],
        jobs,
        collective_id,
    )


def hidden_back_body(
    t, dy, acts, residual, hidden, slope, down, up, vec, out, up_t, bias_sum, dh, dh_low, sums, total, back, du
):
    tokens = dy.shape[0]
    last = pl.num_programs(0) - 1

    def accumulate(into, value):
        @pl.when(t == 0)
        def _():
            into[...] = value

        @pl.when(t > 0)
        def _():
            into[...] += value

    accumulate(total, dot_nn(hidden[...], down[...]))
    du[...] = (dot_nt(dy[...], down[...]) * slope[...].astype(F32)).astype(BF)
    bias_sum[...] = jnp.sum(du[...].astype(F32), axis=0, keepdims=True)
    up_t[...] = dot_tn(du[...], acts[...]).astype(BF)
    accumulate(back, dot_nn(du[...], up[...]))

    @pl.when(t == last)
    def _():
        sums[...] = jnp.zeros_like(sums)

        def leave(rows):
            here = residual[rows, :]
            out[rows, :] = (here + total[rows, :] + vec[7:8, :]).astype(BF)
            grad = back[rows, :]
            normed, inverse = layer_norm(here, 1.0, 0.0)[1:]
            change, gain, shift = norm_backward(grad, normed, inverse, vec[5:6, :])
            upstream = dy[rows, :].astype(F32)
            here = upstream + change
            dh[rows, :] = here
            low = here.astype(BF)
            dh_low[rows, :] = low
            for row, value in enumerate((jnp.sum(low.astype(F32), axis=0), gain, shift, jnp.sum(upstream, axis=0))):
                sums[4 + row : 5 + row, :] += value[None]

        chunks(tokens, CHUNK, leave)


def hidden_backward(
    dy, acts, residual, hidden, slope, down_full, up_full, vec, jobs, collective_id
):
    tokens = dy.shape[0]
    units = up_full.shape[0]
    column = lambda array: block(array, (tokens, UNITS), lambda n: (0, n))
    rows = lambda array: block(array, (UNITS, D), lambda n: (n, 0))
    return fused_call(
        hidden_back_body,
        units // UNITS,
        [
            whole(dy),
            whole(acts),
            whole(residual),
            column(hidden),
            column(slope),
            rows(down_full),
            rows(up_full),
            whole(vec),
        ],
        [
            result((tokens, D), BF),
            result((units, D), BF, (UNITS, D), lambda n: (n, 0)),
            result((1, units), F32, (1, UNITS), lambda n: (0, n)),
            result((tokens, D), F32),
            result((tokens, D), BF),
            result((8, D), F32),
        ],
        [
            pltpu.VMEM((tokens, D), F32),
            pltpu.VMEM((tokens, D), F32),
            pltpu.VMEM((tokens, UNITS), BF),
        ],
        jobs,
        collective_id,
    )


def attend_back_body(
    t, dh_low, out_w, mixed, x, dh, vec, acts, qkv, lse, wq, wk, wv, sums_in,
    out_t, qkv_t, grad_in, sums, upstream, grads, dk, dv, back,
):
    length = x.shape[0]
    last = pl.num_programs(0) - 1
    scale = HEAD_DIM ** (-0.5)

    @pl.when(t == 0)
    def _():
        def enter(rows):
            value = dot_nn(dh_low[rows, :], out_w[...]).astype(BF)
            for head in range(HEADS):
                upstream[head, rows, :] = value[:, head * HEAD_DIM : (head + 1) * HEAD_DIM]

        chunks(length, 2 * CHUNK, enter)
        out_t[...] = dot_tn(dh_low[...], mixed[...]).astype(BF)
        sums[...] = sums_in[...]

    slope = head_slope(t)
    keys_t = qkv[1].astype(F32).T.astype(BF)
    for start in reversed(range(0, length, QUERY_BLOCK)):
        rows = start + QUERY_BLOCK
        query = qkv[0, start:rows, :]
        above = upstream[t, start:rows, :]
        scores = scores_t(query, qkv[1, :rows, :], slope, start, rows)
        probs = jnp.exp(scores - lse[0, :, start:rows])
        prob_grad = dot_nt(qkv[2, :rows, :], above)
        weighted = probs * prob_grad
        centered = jnp.sum(weighted, axis=0, keepdims=True)
        score_grad = (weighted - probs * centered).astype(BF)
        query_grad = dot_nn(keys_t[:, :rows], score_grad) * scale
        grads[start:rows, :HEAD_DIM] = query_grad.T.astype(BF)
        key_part = dot_nn(score_grad, query)
        value_part = dot_nn(probs.astype(BF), above)
        if rows == length:
            dk[...] = key_part
            dv[...] = value_part
        else:
            dk[:rows, :] += key_part
            dv[:rows, :] += value_part
    grads[:, HEAD_DIM : 2 * HEAD_DIM] = (dk[...] * scale).astype(BF)
    grads[:, 2 * HEAD_DIM :] = dv[...].astype(BF)
    totals = jnp.sum(grads[...].astype(F32), axis=0, keepdims=True)
    lanes = pl.ds(pl.multiple_of(t * HEAD_DIM, HEAD_DIM), HEAD_DIM)
    sums[2:3, lanes] = totals[:, :HEAD_DIM]
    sums[3:4, lanes] = totals[:, 2 * HEAD_DIM :]
    weight_grad = dot_tn(grads[...], acts[...]).astype(BF)
    for part in range(3):
        qkv_t[part] = weight_grad[part * HEAD_DIM : (part + 1) * HEAD_DIM, :]
    weights = jnp.concatenate([wq[...], wk[...], wv[...]], axis=0)
    more = dot_nn(grads[...], weights)

    @pl.when(t == 0)
    def _():
        back[...] = more

    @pl.when(t > 0)
    def _():
        back[...] += more

    @pl.when(t == last)
    def _():
        def leave(rows):
            normed, inverse = layer_norm(x[rows, :].astype(F32), 1.0, 0.0)[1:]
            change, gain, shift = norm_backward(back[rows, :], normed, inverse, vec[0:1, :])
            grad_in[rows, :] = (dh[rows, :] + change).astype(BF)
            sums[0:1, :] += gain[None]
            sums[1:2, :] += shift[None]

        chunks(length, CHUNK, leave)


def attend_backward(
    dh_low, out_full, mixed, x, dh, vec, acts, qkv, lse, qkv_full, sums, jobs, collective_id
):
    tokens = x.shape[0]
    head_rows = lambda part: block(
        qkv_full, (HEAD_DIM, D), lambda h: (part * HEADS + h, 0)
    )
    return fused_call(
        attend_back_body,
        HEADS,
        [
            whole(dh_low),
            whole(out_full),
            whole(mixed),
            whole(x),
            whole(dh),
            whole(vec),
            whole(acts),
            block(qkv, (3, tokens, HEAD_DIM), lambda h: (0, 0, h)),
            block(lse, (1, 1, tokens), lambda h: (h, 0, 0)),
            head_rows(0),
            head_rows(1),
            head_rows(2),
            whole(sums),
        ],
        [
            result((D, D), BF),
            result((3, D, D), BF, (3, HEAD_DIM, D), lambda h: (0, h, 0)),
            result((tokens, D), BF),
            result((8, D), F32),
        ],
        [
            pltpu.VMEM((HEADS, tokens, HEAD_DIM), BF),
            pltpu.VMEM((tokens, 3 * HEAD_DIM), BF),
            pltpu.VMEM((tokens, HEAD_DIM), F32),
            pltpu.VMEM((tokens, HEAD_DIM), F32),
            pltpu.VMEM((tokens, D), F32),
        ],
        jobs,
        collective_id,
    )


def renew_body(
    t, own, full, root, n_stat, m_stat, m_root, weight, new_n, new_m, new_w, left, product
):
    last = pl.num_programs(0) - 1
    me = lax.axis_index("dp") * lax.axis_size("ffn") + lax.axis_index("ffn")
    rows_owned = m_stat.shape[0]
    share = 128 // rows_owned
    lanes = pl.ds(pl.multiple_of((me // share) * 128, 128), 128)
    here = full[...]
    new_n[...] = decay_rate * n_stat[...] + (1.0 - decay_rate) * dot_nt(own[...], here)
    left_part = dot_tn(full[:, lanes], here)
    product_part = dot_nn(root[...].astype(BF), here)

    @pl.when(t == 0)
    def _():
        left[...] = left_part
        product[...] = product_part

    @pl.when(t > 0)
    def _():
        left[...] += left_part
        product[...] += product_part

    @pl.when(t == last)
    def _():
        mine = left[pl.ds(pl.multiple_of((me % share) * rows_owned, rows_owned), rows_owned), :]
        new_m[...] = decay_rate * m_stat[...] + (1.0 - decay_rate) * mine
        step = dot_nt(product[...].astype(BF), m_root[...])
        new_w[...] = weight[...] - matrix_rate * step


def renew(own, full, n_root, n_stat, m_stat, m_root, weight, jobs, collective_id):
    rows, total = own.shape[0], full.shape[0]
    rows_owned = m_stat.shape[0]
    if not on_fast_grid():
        me = lax.axis_index("dp") * lax.axis_size("ffn") + lax.axis_index("ffn")
        new_n = decay_rate * n_stat + (1.0 - decay_rate) * dot_nt(own, full)
        mine = lax.dynamic_slice_in_dim(full, me * rows_owned, rows_owned, 1)
        new_m = decay_rate * m_stat + (1.0 - decay_rate) * dot_tn(mine, full)
        product = dot_nn(n_root.astype(BF), full)
        new_w = weight - matrix_rate * dot_nt(product.astype(BF), m_root)
        return [new_n, new_m, new_w], [job.plainly() for job in jobs]
    size = 512
    column = lambda array: block(array, (rows, size), lambda n: (0, n))
    return fused_call(
        renew_body,
        total // size,
        [
            whole(own),
            block(full, (size, D), lambda n: (n, 0)),
            column(n_root),
            column(n_stat),
            whole(m_stat),
            whole(m_root),
            whole(weight),
        ],
        [
            result((rows, total), F32, (rows, size), lambda n: (0, n)),
            result((rows_owned, D), F32),
            result((rows, D), F32),
        ],
        [pltpu.VMEM((128, D), F32), pltpu.VMEM((rows, D), F32)],
        jobs,
        collective_id,
    )


SMALL_ROWS = 32
SMALL_WIDTH = 128


def pack_small(vector_part, bias_part):
    owners = vector_part.shape[0]
    flat = jnp.concatenate([vector_part.reshape(owners, -1), bias_part.reshape(owners, -1)], axis=1)
    room = SMALL_ROWS * SMALL_WIDTH
    flat = jnp.pad(flat, ((0, 0), (0, room - flat.shape[1])))
    return flat.reshape(owners * SMALL_ROWS, SMALL_WIDTH)


def unpack_small(packed, columns, units):
    owners = packed.shape[0] // SMALL_ROWS
    flat = packed.reshape(owners, -1)
    vector_part = flat[:, : 8 * columns].reshape(owners, 8, columns)
    bias_part = flat[:, 8 * columns : 8 * columns + units]
    return vector_part, bias_part


def shards(
    block_input,
    cotangent,
    w_qkv,
    w_out,
    w_up,
    w_down,
    vectors,
    b_up,
    qkv_left,
    qkv_right,
    out_left,
    out_right,
    up_left,
    up_right,
    down_left,
    down_right,
    qkv_left_root,
    qkv_right_root,
    out_left_root,
    out_right_root,
    up_left_root,
    up_right_root,
    down_left_root,
    down_right_root,
    vector_stat,
    b_up_stat,
):
    owners = lax.axis_size("dp") * lax.axis_size("ffn")
    columns = vectors.shape[1]
    units = b_up.shape[0]
    qkv_w, out_w, up_w = w_qkv.T, w_out.T, w_up.T
    small = pack_small(vectors[None], b_up[None]).astype(BF)
    small_full, qkv_full = transfer([Gather(small), Gather(qkv_w.astype(BF))], 1)
    vector_low, bias_low = unpack_small(small_full, columns, units)
    vector_rows = vector_low.transpose(1, 0, 2).reshape(8, D).astype(F32)
    up_bias = bias_low.reshape(1, -1).astype(F32)
    (qkv, mixed, lse, acts_one), (out_full, up_full) = attend(
        block_input, vector_rows, qkv_full, [Gather(out_w.astype(BF)), Gather(up_w.astype(BF))], 2
    )
    (residual, acts_two, hidden, slope, down_t), (down_full,) = hidden_forward(
        block_input,
        mixed,
        out_full,
        vector_rows,
        cotangent,
        up_full,
        up_bias,
        [Gather(w_down.astype(BF))],
        3,
    )
    (block_output, up_t, bias_grad, dh, dh_low, sums), (down_g, qkv_mroot) = hidden_backward(
        cotangent,
        acts_two,
        residual,
        hidden,
        slope,
        down_full,
        up_full,
        vector_rows,
        [Reduce(down_t), Gather(qkv_left_root.astype(BF))],
        4,
    )
    (out_t, qkv_t, input_grad, sums), (up_g, out_mroot, up_mroot) = attend_backward(
        dh_low,
        out_full,
        mixed,
        block_input,
        dh,
        vector_rows,
        acts_one,
        qkv,
        lse,
        qkv_full,
        sums,
        [Reduce(up_t), Gather(out_left_root.astype(BF)), Gather(up_left_root.astype(BF))],
        5,
    )
    small_part = pack_small(
        sums.reshape(8, owners, columns).transpose(1, 0, 2), bias_grad.reshape(owners, units)
    ).astype(BF)
    down_low = down_g.astype(BF)
    up_low = up_g.astype(BF)
    qkv_g, out_g, small_g, down_all, down_mroot = transfer(
        [
            Reduce(qkv_t.reshape(-1, D)),
            Reduce(out_t),
            Reduce(small_part),
            Gather(down_low),
            Gather(down_right_root.astype(BF)),
        ],
        6,
    )
    qkv_low, out_low = qkv_g.astype(BF), out_g.astype(BF)
    (new_down_n, new_down_m, new_w_down), (up_all,) = renew(
        down_low,
        down_all,
        down_left_root,
        down_left,
        down_right,
        down_mroot,
        w_down,
        [Gather(up_low)],
        7,
    )
    (new_up_n, new_up_m, new_w_up), (qkv_all, out_all) = renew(
        up_low,
        up_all,
        up_right_root,
        up_right,
        up_left,
        up_mroot,
        up_w,
        [Gather(qkv_low), Gather(out_low)],
        8,
    )
    new_qkv_n, new_qkv_m, new_w_qkv = renew(
        qkv_low, qkv_all, qkv_right_root, qkv_right, qkv_left, qkv_mroot, qkv_w, [], 9
    )[0]
    new_out_n, new_out_m, new_w_out = renew(
        out_low, out_all, out_right_root, out_right, out_left, out_mroot, out_w, [], 9
    )[0]
    new_m = [new_qkv_m, new_out_m, new_up_m, new_down_m]
    new_n = [new_qkv_n, new_out_n, new_up_n, new_down_n]
    new_w_qkv, new_w_out, new_w_up = new_w_qkv.T, new_w_out.T, new_w_up.T
    grads = [qkv_g, out_g, up_g, down_g]
    vector_grad, b_up_grad = unpack_small(small_g, columns, units)
    vector_grad, b_up_grad = vector_grad[0], b_up_grad[0]
    new_vector_stat = decay_rate * vector_stat + (1.0 - decay_rate) * vector_grad * vector_grad
    new_vectors = vectors - vector_rate * vector_grad * lax.rsqrt(new_vector_stat)
    new_b_up_stat = decay_rate * b_up_stat + (1.0 - decay_rate) * b_up_grad * b_up_grad
    new_b_up = b_up - vector_rate * b_up_grad * lax.rsqrt(new_b_up_stat)
    return (
        block_output,
        input_grad,
        grads[0].T,
        grads[1].T,
        grads[2].T,
        grads[3],
        vector_grad,
        b_up_grad,
        new_m[0],
        new_n[0],
        new_m[1],
        new_n[1],
        new_m[2],
        new_n[2],
        new_n[3],
        new_m[3],
        new_vector_stat,
        new_b_up_stat,
        new_w_qkv,
        new_w_out,
        new_w_up,
        new_w_down,
        new_vectors,
        new_b_up,
    )


def solution(mesh):
    return jax.shard_map(
        shards,
        mesh=mesh,
        in_specs=(
            P(("dp", "ffn"), None),
            P(("dp", "ffn"), None),
            P(None, ("dp", "ffn")),
            P(None, ("dp", "ffn")),
            P(None, ("dp", "ffn")),
            P(("dp", "ffn"), None),
            P(None, ("dp", "ffn")),
            P(("dp", "ffn")),
            P(("dp", "ffn"), None),
            P(("dp", "ffn"), None),
            P(("dp", "ffn"), None),
            P(("dp", "ffn"), None),
            P(("dp", "ffn"), None),
            P(("dp", "ffn"), None),
            P(("dp", "ffn"), None),
            P(("dp", "ffn"), None),
            P(("dp", "ffn"), None),
            P(("dp", "ffn"), None),
            P(("dp", "ffn"), None),
            P(("dp", "ffn"), None),
            P(("dp", "ffn"), None),
            P(("dp", "ffn"), None),
            P(("dp", "ffn"), None),
            P(("dp", "ffn"), None),
            P(None, ("dp", "ffn")),
            P(("dp", "ffn")),
        ),
        out_specs=(
            P(("dp", "ffn"), None),
            P(("dp", "ffn"), None),
            P(None, ("dp", "ffn")),
            P(None, ("dp", "ffn")),
            P(None, ("dp", "ffn")),
            P(("dp", "ffn"), None),
            P(None, ("dp", "ffn")),
            P(("dp", "ffn")),
            P(("dp", "ffn"), None),
            P(("dp", "ffn"), None),
            P(("dp", "ffn"), None),
            P(("dp", "ffn"), None),
            P(("dp", "ffn"), None),
            P(("dp", "ffn"), None),
            P(("dp", "ffn"), None),
            P(("dp", "ffn"), None),
            P(None, ("dp", "ffn")),
            P(("dp", "ffn")),
            P(None, ("dp", "ffn")),
            P(None, ("dp", "ffn")),
            P(None, ("dp", "ffn")),
            P(("dp", "ffn"), None),
            P(None, ("dp", "ffn")),
            P(("dp", "ffn")),
        ),
        check_vma=False,
    )
```

time: 751 us -> 655 us (0.87)
  matrix products: 185 us -> 0 us
  Pallas kernels: 502 us -> 612 us
  other arithmetic: 48.7 us -> 14.5 us
  local copies, waits for them, and re-layouts: 9.83 us -> 18.8 us
    dot_general x27 -> x0, matrix products: 185 us -> none  [the longest x11 80.6 us: dot_nt(): lax.dot_general(left, right, (((1,), (1,)), ((), ())), preferred_element_...]
    pallas_call x7 -> x10, Pallas kernels: 502 us -> 612 us  [fused_call(): pl.pallas_call(kernel, grid=(steps,), out_shape=tuple((o[0] for o in outs...]
    reduce_sum x5 -> x0, other arithmetic: 16 us -> none  [the longest x1 6.65 us: shards(): out_bias_grad = jnp.sum(branch_low, axis=0, dtype=F32)]
    concatenate x2 -> x0, other arithmetic: 13.4 us -> none  [the longest x1 13.4 us: shards(): jnp.concatenate([dot_tn(projected_grad[i], acts_one) for i in range(3)], 0)]
    unnamed x118 -> x63, local copies, waits for them, and re-layouts: 7.16 us -> 16.9 us
where the time goes in v2:
time: 655 us; the launch traced here: 646 us
  Pallas kernels  612 us (93%)
  local copies, waits for them, and re-layouts  18.8 us (3%)
  other arithmetic  14.5 us (2%)
    pallas_call x10, Pallas kernels, fused_call(): pl.pallas_call(kernel, grid=(steps,), out_shape=tuple((o[0] for o in outs...  612 us
    unnamed x63, local copies, waits for them, and re-layouts  16.9 us

profile of v2, /device:TPU:0, one launch (start us, length us, event | category | flops | bytes accessed | tf_op | source)
XLA Modules:
  0.0 646.4 jit_solution(9416331608382548183)
XLA Ops:
  0.7 1.8 bitcast_convert_fusion.2.refs_1_
  2.4 0.7 convert.26
  3.2 0.7 convert_bitcast_fusion
  3.9 0.6 fusion.5
  4.5 50.3 %shard_map.433 = (bf16[4,2,4,32,128]{4,3,2,1,0:T(8,128)(2,1)}, bf16[4,2,4,96,1024]{4,3,2,1,0:T(8,128)(2,1)}) custom-call(bf16[32,128]{1,0:T(8,128)(2,1)} %bitcast.86, bf16[96,1024]{1,0:T(8,128)(2,1)} %bitcast_convert_fusion.2.refs_1_), custom_call_target="tpu_custom_call" | custom-call | tf_op jit(solution)/shard_map/pallas_call | solution.py:378
  54.8 1.1 copy.62
  56.0 0.7 reshape.154.refs_1_.refs_5_.refs_3_.refs_7_
  56.7 0.2 copy.55
  56.9 0.8 bitcast_convert_fusion.refs_7_
  57.7 0.6 bitcast_convert_fusion.1.refs_6_
  58.4 69.2 %shard_map.434 = (bf16[3,1024,1024]{2,1,0:T(8,128)(2,1)}, bf16[1024,1024]{1,0:T(8,128)(2,1)}, f32[8,1,1024]{2,1,0:T(1,128)}, bf16[1024,1024]{1,0:T(8,128)(2,1)},...) custom-call(bf16[1024,1024]{1,0:T(8,128)(2,1)} %refs_3_.5, ...), custom_call_target="tpu_custom_call" | custom-call | tf_op jit(solution)/shard_map/pallas_call | solution.py:378
  127.6 0.6 slice_convert_fusion.1
  128.2 0.7 convert_element_type.72.refs_7_
  128.9 60.6 %shard_map.435 = (f32[1024,1024]{1,0:T(8,128)}, bf16[1024,1024]{1,0:T(8,128)(2,1)}, bf16[1024,4096]{1,0:T(8,128)(2,1)}, bf16[1024,4096]{1,0:T(8,128)(2,1)}, bf16...) custom-call(bf16[1024,1024]{1,0:T(8,128)(2,1)} %refs_3_.5, ...), custom_call_target="tpu_custom_call" | custom-call | tf_op jit(solution)/shard_map/pallas_call | solution.py:378
  189.5 0.6 convert_element_type.73.refs_9_
  190.2 88.2 %shard_map.436 = (bf16[1024,1024]{1,0:T(8,128)(2,1)}, bf16[4096,1024]{1,0:T(8,128)(2,1)}, f32[1,4096]{1,0:T(1,128)}, f32[1024,1024]{1,0:T(8,128)}, bf16[1024,102...) custom-call(bf16[1024,1024]{1,0:T(8,128)(2,1)} %refs_0_.5, ...), custom_call_target="tpu_custom_call" | custom-call | tf_op jit(solution)/shard_map/pallas_call | solution.py:378
  278.3 0.6 convert_element_type.74.refs_14_
  279.0 0.6 convert_element_type.75.refs_15_
  279.6 109.9 %shard_map.437 = (bf16[1024,1024]{1,0:T(8,128)(2,1)}, bf16[3,1024,1024]{2,1,0:T(8,128)(2,1)}, bf16[1024,1024]{1,0:T(8,128)(2,1)}, f32[8,1024]{1,0:T(8,128)}, f32...) custom-call(bf16[1024,1024]{1,0:T(8,128)(2,1)} %get-tuple-element.85.refs_0_, ...), custom_call_target="tpu_custom_call" | custom-call | tf_op jit(solution)/shard_map/pallas_call | solution.py:378
  389.5 0.8 convert.28
  390.6 0.7 copy.60
  391.3 0.7 convert_element_type.77.refs_3_.refs_0_
  392.1 0.6 convert_element_type.78.refs_4_
  392.7 106.9 %shard_map.438 = (f32[96,1024]{1,0:T(8,128)}, f32[32,1024]{1,0:T(8,128)}, f32[32,128]{1,0:T(8,128)}, bf16[4,2,4,128,1024]{4,3,2,1,0:T(8,128)(2,1)}, bf16[4,2,4,32,1024]{4,3,2,1,0:T(8,128)(2,1)}) custom-call(bf16[4,2,4,96,1024]{4,3,2,1,0:T(8,128)(2,1)} %bitcast.63, bf16[4,2,4,32,1024]{4,3,2,1,0:T(8,128)(2,1)} %bitcast.67, ...), custom_call_target="tpu_custom_call" | custom-call | tf_op jit(solution)/shard_map/pallas_call | solution.py:378
  499.6 0.7 convert_element_type.80.refs_7_.refs_0_
  500.3 53.5 %shard_map.439 = (f32[128,4096]{1,0:T(8,128)}, f32[32,1024]{1,0:T(8,128)}, f32[128,1024]{1,0:T(8,128)}, bf16[4,2,4,128,1024]{4,3,2,1,0:T(8,128)(2,1)}) custom-call(bf16[128,1024]{1,0:T(8,128)(2,1)} %convert_element_type.77.refs_3_.refs_0_, bf16[4096,1024]{1,0:T(8,128)(2,1)} %bitcast.57, f32[128,4096]{1,0:T(8,128)} %refs_2_.4, f32[128,4096]{1,0:T(8,128)} %refs_3_.6, ...), custom_call_target="tpu_custom_call" | custom-call | tf_op jit(solution)/shard_map/pallas_call | solution.py:378
  553.8 0.7 convert_element_type.79.refs_7_.refs_0_
  554.5 0.6 convert_element_type.81.refs_8_.refs_0_
  555.2 57.7 %shard_map.440 = (f32[128,4096]{1,0:T(8,128)}, f32[32,1024]{1,0:T(8,128)}, f32[128,1024]{1,0:T(8,128)}, bf16[4,2,4,96,1024]{4,3,2,1,0:T(8,128)(2,1)}, bf16[4,2,4,32,1024]{4,3,2,1,0:T(8,128)(2,1)}) custom-call(bf16[128,1024]{1,0:T(8,128)(2,1)} %convert_element_type.80.refs_7_.refs_0_, bf16[4096,1024]{1,0:T(8,128)(2,1)} %bitcast.56, f32[128,4096]{1,0:T(8,128)} %refs_2_.5, ...), custom_call_target="tpu_custom_call" | custom-call | tf_op jit(solution)/shard_map/pallas_call | solution.py:378
  612.9 5.2 shard_map.442
  618.1 10.5 %shard_map.441 = (f32[96,3072]{1,0:T(8,128)}, f32[32,1024]{1,0:T(8,128)}, f32[96,1024]{1,0:T(8,128)}) custom-call(bf16[96,1024]{1,0:T(8,128)(2,1)} %convert_element_type.79.refs_7_.refs_0_, bf16[3072,1024]{1,0:T(8,128)(2,1)} %bitcast.64, f32[96,3072]{1,0:T(8,128)} %refs_2_.6, f32[96,3072]{1,0:T(8,128)} %refs_3_.8, f32[32,1024]{1,0:T(8,128)} %refs_4_.8, ...), custom_call_target="tpu_custom_call" | custom-call | tf_op jit(solution)/shard_map/pallas_call | solution.py:378
  628.5 2.2 copy.58
  630.7 0.7 slice_reduce_fusion
  631.5 0.6 multiply_subtract_fusion
  632.1 1.2 multiply_subtract_fusion.1
  633.3 1.0 copy.57
  634.3 1.3 copy.73
  635.6 1.0 copy-done.3
  636.6 1.3 copy.74
  638.0 0.7 copy.75
  638.7 0.7 copy.76
  639.4 0.8 copy.77
  640.2 0.7 copy.78
  640.8 1.3 copy.79
  642.1 1.0 copy-done.4
  643.2 1.3 copy.80
  644.5 0.7 copy.81
  645.2 0.8 copy.82
  (56 shorter events, 0.7 us)
Async XLA Ops:
  0.7 56.1 %copy-start.10 = (f32[1024,128]{1,0:T(8,128)S(1)}, f32[1024,128]{1,0:T(8,128)}, u32[]{:S(2)}) copy-start(f32[1024,128]{1,0:T(8,128)} %param.30) | copy-start | bytes 1572868
  0.7 57.1 %copy-start.9 = (f32[1024,32]{0,1:T(8,128)S(1)}, f32[1024,32]{0,1:T(8,128)}, u32[]{:S(2)}) copy-start(f32[1024,32]{0,1:T(8,128)} %param.29) | copy-start | bytes 393220
  56.9 70.6 %copy-start = (f32[1024,128]{0,1:T(8,128)}, f32[1024,128]{0,1:T(8,128)S(1)}, u32[]{:S(2)}) copy-start(f32[1024,128]{0,1:T(8,128)S(1)} %copy.55) | copy-start | bytes 1572868
  58.4 69.8 %copy-start.1 = (f32[128,1024]{1,0:T(8,128)S(1)}, f32[128,1024]{1,0:T(8,128)}, u32[]{:S(2)}) copy-start(f32[128,1024]{1,0:T(8,128)} %refs_6_.1) | copy-start | bytes 1572868
  128.9 60.6 %copy-start.14 = (f32[32,1024]{1,0:T(8,128)S(1)}, f32[32,1024]{1,0:T(8,128)}, u32[]{:S(2)}) copy-start(f32[32,1024]{1,0:T(8,128)} %param.42) | copy-start | bytes 393220
  190.1 88.2 %copy-start.15 = (f32[32,1024]{1,0:T(8,128)S(1)}, f32[32,1024]{1,0:T(8,128)}, u32[]{:S(2)}) copy-start(f32[32,1024]{1,0:T(8,128)} %param.44) | copy-start | bytes 393220
  190.1 88.8 %copy-start.16 = (f32[32,1024]{1,0:T(8,128)S(1)}, f32[32,1024]{1,0:T(8,128)}, u32[]{:S(2)}) copy-start(f32[32,1024]{1,0:T(8,128)} %param.46) | copy-start | bytes 393220
  279.6 110.9 %copy-start.22 = (f32[1,4096]{1,0:T(1,128)S(1)}, f32[1,4096]{1,0:T(1,128)}, u32[]{:S(2)}) copy-start(f32[1,4096]{1,0:T(1,128)} %get-tuple-element.96) | copy-start | bytes 49156
  279.6 111.7 %copy-start.6 = (f32[128,1024]{1,0:T(8,128)S(1)}, f32[128,1024]{1,0:T(8,128)}, u32[]{:S(2)}) copy-start(f32[128,1024]{1,0:T(8,128)} %get-tuple-element.204) | copy-start | bytes 1572868
  279.6 112.5 %copy-start.17 = (f32[32,1024]{1,0:T(8,128)S(1)}, f32[32,1024]{1,0:T(8,128)}, u32[]{:S(2)}) copy-start(f32[32,1024]{1,0:T(8,128)} %param.49) | copy-start | bytes 393220
  392.7 106.9 %copy-start.7 = (f32[128,1024]{1,0:T(8,128)S(1)}, f32[128,1024]{1,0:T(8,128)}, u32[]{:S(2)}) copy-start(f32[128,1024]{1,0:T(8,128)} %get-tuple-element.100) | copy-start | bytes 1572868
  500.3 53.5 %copy-start.8 = (f32[96,1024]{1,0:T(8,128)S(1)}, f32[96,1024]{1,0:T(8,128)}, u32[]{:S(2)}) copy-start(f32[96,1024]{1,0:T(8,128)} %get-tuple-element.98) | copy-start | bytes 1179652
  500.3 54.2 %copy-start.12 = (f32[32,1024]{1,0:T(8,128)S(1)}, f32[32,1024]{1,0:T(8,128)}, u32[]{:S(2)}) copy-start(f32[32,1024]{1,0:T(8,128)} %get-tuple-element.99) | copy-start | bytes 393220
  618.1 13.4 %copy-start.21 = (f32[8,32]{1,0:T(8,128)S(1)}, f32[8,32]{1,0:T(8,128)}, u32[]{:S(2)}) copy-start(f32[8,32]{1,0:T(8,128)} %param.32) | copy-start | bytes 3076
  618.1 13.4 %copy-start.23 = (f32[8,32]{1,0:T(8,128)S(1)}, f32[8,32]{1,0:T(8,128)}, u32[]{:S(2)}) copy-start(f32[8,32]{1,0:T(8,128)} %param.50) | copy-start | bytes 3076
  628.5 5.8 copy-start.2
  631.5 4.1 copy-start.20
  634.3 2.3 copy-start.3
  636.6 2.1 copy-start.13
  636.6 3.5 copy-start.19
  638.0 2.9 copy-start.5
  640.8 2.3 copy-start.4
  643.2 1.3 copy-start.18
  643.2 2.0 copy-start.11

commit v3 on v2

--- a/solution.py
+++ b/solution.py
@@ -52,11 +52,6 @@
     return jnp.dot(left, right, preferred_element_type=F32)
 
 
-def coords():
-    dp = lax.axis_index("dp")
-    return dp // 2, dp % 2, lax.axis_index("ffn")
-
-
 def flip(value, mask):
     result = value
     bit = 1
@@ -67,20 +62,6 @@
     return result
 
 
-def greet():
-    p, c, z = coords()
-    barrier = pltpu.get_barrier_semaphore()
-    peers = [(flip(p, 1) * 2 + c, z), (flip(p, 2) * 2 + c, z), (p * 2 + 1 - c, z)]
-    peers += [(p * 2 + c, flip(z, k)) for k in (1, 2, 3)]
-    for peer in peers:
-        pl.semaphore_signal(barrier, inc=1, device_id=peer, device_id_type=MESH)
-    pl.semaphore_wait(barrier, len(peers))
-
-
-FIRST = (1, 2)
-SECOND = (2, 1)
-
-
 class Copies:
     def __init__(self, send, recv):
         self.send, self.recv, self.made = send, recv, {}
@@ -92,8 +73,10 @@
             src, dst, self.send.at[at], self.recv.at[at], device_id=device, device_id_type=MESH
         )
 
-    def post(self, name, make):
+    def plan(self, name, make):
         self.made[name] = (len(self.made), make)
+
+    def post(self, name):
         self.copy(name).start()
 
     def got(self, name):
@@ -104,50 +87,96 @@
             self.copy(name).wait_send()
 
 
+class Place:
+    def __init__(self):
+        dp = lax.axis_index("dp")
+        self.y, self.x, self.c, self.z = dp // 4, (dp // 2) % 2, dp % 2, lax.axis_index("ffn")
+
+    def device(self, y=0, x=0, c=0, z=0):
+        dp = (flip(self.y, y) * 2 + flip(self.x, x)) * 2 + flip(self.c, c)
+        return dp, flip(self.z, z)
+
+    def span(self, group):
+        if len(group) == 1:
+            return pl.ds(flip(self.z, group[0]), 1)
+        if len(group) == 2:
+            return pl.ds(flip(self.z // 2, group[0] // 2) * 2, 2)
+        return pl.ds(0, 4)
+
+
+def greet(place):
+    barrier = pltpu.get_barrier_semaphore()
+    steps = [dict(y=1), dict(x=1), dict(c=1), dict(z=1), dict(z=2), dict(z=3)]
+    for step in steps:
+        pl.semaphore_signal(
+            barrier, inc=1, device_id=place.device(**step), device_id_type=MESH
+        )
+    pl.semaphore_wait(barrier, len(steps))
+
+
+def one(index):
+    return pl.ds(index, 1)
+
+
+TURNS = (("x", "y"), ("y", "x"))
+
+
 def gather_plan(place, shard, out, send, recv, local_sem):
-    p, c, z = place
+    y, x, c, z = place.y, place.x, place.c, place.z
     half_rows = shard.shape[0] // 2
     copies = Copies(send, recv)
 
-    def local():
-        return pltpu.make_async_copy(shard, out.at[p, c, z], local_sem)
-
     def half(ref, h):
         return ref.at[pl.ds(h * half_rows, half_rows)]
 
+    def local():
+        return pltpu.make_async_copy(shard, out.at[y, x, c, z], local_sem)
+
     def along_z(k):
-        copies.post(("z", k), lambda: (shard, out.at[p, c, z], (p * 2 + c, flip(z, k))))
+        return shard, out.at[y, x, c, z], place.device(z=k)
+
+    def own(turn, k, h):
+        dst = half(out.at[y, x, c, flip(z, k)], h)
+        return (dst if k else half(shard, h)), dst, place.device(**{TURNS[h][turn]: 1})
+
+    def relay(k, h):
+        block = out.at[y, 1 - x, c, flip(z, k)] if h == 0 else out.at[1 - y, x, c, flip(z, k)]
+        return half(block, h), half(block, h), place.device(**{TURNS[h][1]: 1})
+
+    def across(k):
+        piece = out.at[:, :, c, flip(z, k)]
+        return piece, piece, place.device(c=1)
+
+    do = functools.partial
+    for k in range(4):
+        if k:
+            copies.plan(("z", k), do(along_z, k))
+        for h in (0, 1):
+            copies.plan(("first", k, h), do(own, 0, k, h))
+            copies.plan(("second", k, h), do(own, 1, k, h))
+            copies.plan(("relay", k, h), do(relay, k, h))
+        copies.plan(("core", k), do(across, k))
 
     def spread(k):
-        for name, turn in (("first", FIRST), ("second", SECOND)):
+        for name in ("first", "second"):
             for h in (0, 1):
-
-                def make(h=h, turn=turn):
-                    dst = half(out.at[p, c, flip(z, k)], h)
-                    return (dst if k else half(shard, h)), dst, (flip(p, turn[h]) * 2 + c, z)
-
-                copies.post((name, k, h), make)
+                copies.post((name, k, h))
 
     def begin():
-        along_z(1)
+        copies.post(("z", 1))
         spread(0)
         local().start()
 
     def landed(k):
         copies.got(("z", k))
         if k < 3:
-            along_z(k + 1)
+            copies.post(("z", k + 1))
         spread(k)
 
     def forward(k):
         for h in (0, 1):
             copies.got(("first", k, h))
-
-            def make(h=h):
-                piece = half(out.at[flip(p, FIRST[h]), c, flip(z, k)], h)
-                return piece, piece, (flip(p, SECOND[h]) * 2 + c, z)
-
-            copies.post(("relay", k, h), make)
+            copies.post(("relay", k, h))
 
     def share(k):
         for h in (0, 1):
@@ -155,44 +184,219 @@
             copies.got(("relay", k, h))
         if k == 0:
             local().wait()
-
-        def make():
-            piece = out.at[:, c, flip(z, k)]
-            return piece, piece, (p * 2 + 1 - c, z)
-
-        copies.post(("core", k), make)
+        copies.post(("core", k))
 
     def finish():
         for k in range(4):
             copies.got(("core", k))
         copies.sent()
 
+    return [
+        (0, 0, begin),
+        (4, 1, do(forward, 0)),
+        (6, 1, do(landed, 1)),
+        (13, 2, do(share, 0)),
+        (14, 2, do(forward, 1)),
+        (18, 2, do(landed, 2)),
+        (20, 3, do(share, 1)),
+        (24, 3, do(forward, 2)),
+        (30, 2, do(landed, 3)),
+        (31, 3, do(share, 2)),
+        (35, 3, do(forward, 3)),
+        (39, 3, do(share, 3)),
+        (40, 4, finish),
+    ]
+
+
+def gather_small_plan(place, shard, out, send, recv, local_sem):
+    y, x, c, z = place.y, place.x, place.c, place.z
+    rows = shard.shape[0]
+    copies = Copies(send, recv)
+
+    def half(h):
+        return pl.ds(h * (rows // 2), rows // 2)
+
+    def local():
+        return pltpu.make_async_copy(shard, out.at[y, x, c, z], local_sem)
+
+    def along_z(k):
+        return shard, out.at[y, x, c, z], place.device(z=k)
+
+    def first(h):
+        piece = out.at[y, x, c, :, half(h)]
+        return piece, piece, place.device(**{TURNS[h][0]: 1})
+
+    def second(h):
+        piece = out.at[y, :, c, :, half(h)] if h == 0 else out.at[:, x, c, :, half(h)]
+        return piece, piece, place.device(**{TURNS[h][1]: 1})
+
+    def across():
+        piece = out.at[:, :, c]
+        return piece, piece, place.device(c=1)
+
     do = functools.partial
-    plan = [begin, do(landed, 1), do(forward, 0), do(landed, 2), do(forward, 1), do(share, 0)]
-    plan += [do(landed, 3), do(forward, 2), do(share, 1), do(forward, 3), do(share, 2)]
-    return plan + [do(share, 3), finish]
+    for k in (1, 2, 3):
+        copies.plan(("z", k), do(along_z, k))
+    for h in (0, 1):
+        copies.plan(("first", h), do(first, h))
+        copies.plan(("second", h), do(second, h))
+    copies.plan("core", across)
+
+    def begin():
+        local().start()
+        for k in (1, 2, 3):
+            copies.post(("z", k))
+
+    def start_first():
+        for k in (1, 2, 3):
+            copies.got(("z", k))
+        local().wait()
+        for h in (0, 1):
+            copies.post(("first", h))
+
+    def start_second():
+        for h in (0, 1):
+            copies.got(("first", h))
+            copies.post(("second", h))
+
+    def share():
+        for h in (0, 1):
+            copies.got(("second", h))
+        copies.post("core")
+
+    def finish():
+        copies.got("core")
+        copies.sent()
+
+    return [
+        (0, 0, begin),
+        (24, 1, start_first),
+        (36, 2, start_second),
+        (60, 3, share),
+        (62, 4, finish),
+    ]
+
+
+def gather_z_last_plan(place, shard, out, send, recv, local_sem):
+    y, x, c, z = place.y, place.x, place.c, place.z
+    rows = shard.shape[0]
+    copies = Copies(send, recv)
+
+    def half(h):
+        return pl.ds(h * (rows // 2), rows // 2)
+
+    def local():
+        return pltpu.make_async_copy(shard, out.at[y, x, c, z], local_sem)
+
+    def first(h):
+        return shard.at[half(h)], out.at[y, x, c, z, half(h)], place.device(**{TURNS[h][0]: 1})
+
+    def second(h):
+        piece = out.at[y, :, c, z, half(h)] if h == 0 else out.at[:, x, c, z, half(h)]
+        return piece, piece, place.device(**{TURNS[h][1]: 1})
+
+    def along_z(k):
+        piece = out.at[:, :, c, z]
+        return piece, piece, place.device(z=k)
+
+    def across():
+        piece = out.at[:, :, c]
+        return piece, piece, place.device(c=1)
+
+    do = functools.partial
+    for h in (0, 1):
+        copies.plan(("first", h), do(first, h))
+        copies.plan(("second", h), do(second, h))
+    for k in (1, 2, 3):
+        copies.plan(("z", k), do(along_z, k))
+    copies.plan("core", across)
+
+    def begin():
+        local().start()
+        for h in (0, 1):
+            copies.post(("first", h))
+
+    def start_second():
+        local().wait()
+        for h in (0, 1):
+            copies.got(("first", h))
+            copies.post(("second", h))
+
+    def column():
+        for h in (0, 1):
+            copies.got(("second", h))
+        for k in (1, 2, 3):
+            copies.post(("z", k))
+
+    def share():
+        for k in (1, 2, 3):
+            copies.got(("z", k))
+        copies.post("core")
+
+    def finish():
+        copies.got("core")
+        copies.sent()
+
+    return [(0, 0, begin), (3, 1, start_second), (9, 2, column), (93, 3, share), (100, 4, finish)]
 
 
 def reduce_plan(
     place, parts, out, held, from_core, from_second, from_first, from_z, send, recv, load
 ):
-    p, c, z = place
-    half_rows = parts.shape[-2] // 2
+    y, x, c, z = place.y, place.x, place.c, place.z
+    rows = parts.shape[-2]
+    whole_first = rows < 64
+    groups = [(0, 1, 2, 3)] if whole_first else [(3,), (2,), (1,), (0,)]
     copies = Copies(send, recv)
-    order = (3, 2, 1, 0)
 
     def half(h):
-        return pl.ds(h * half_rows, half_rows)
-
-    def local(k):
-        return pltpu.make_async_copy(parts.at[:, c, flip(z, k)], held.at[k], load.at[k])
-
-    def to_core(k):
-        copies.post(
-            ("core", k),
-            lambda: (parts.at[:, 1 - c, flip(z, k)], from_core.at[k], (p * 2 + 1 - c, z)),
+        return pl.ds(h * (rows // 2), rows // 2)
+
+    def local(group):
+        span = place.span(group)
+        return pltpu.make_async_copy(
+            parts.at[:, :, c, span], held.at[:, :, span], load.at[groups.index(group)]
         )
-        local(k).start()
+
+    def core_route(group):
+        span = place.span(group)
+        return parts.at[:, :, 1 - c, span], from_core.at[:, :, span], place.device(c=1)
+
+    def second_part(group, h, other):
+        at = (1 - y if other else y) if h == 0 else (1 - x if other else x)
+        if h == 0:
+            return (at, slice(None), place.span(group), half(h))
+        return (slice(None), at, place.span(group), half(h))
+
+    def second_route(group, h):
+        return (
+            held.at[second_part(group, h, True)],
+            from_second.at[h, :, place.span(group)],
+            place.device(**{TURNS[h][1]: 1}),
+        )
+
+    def first_part(group, h):
+        return (y, 1 - x, place.span(group), half(h)) if h == 0 else (1 - y, x, place.span(group), half(h))
+
+    def first_route(group, h):
+        return (
+            held.at[first_part(group, h)],
+            from_first.at[h, place.span(group)],
+            place.device(**{TURNS[h][0]: 1}),
+        )
+
+    def z_route(k):
+        return held.at[y, x, flip(z, k)], from_z.at[k - 1], place.device(z=k)
+
+    do = functools.partial
+    for group in groups:
+        copies.plan(("core", group), do(core_route, group))
+        for h in (0, 1):
+            copies.plan(("second", group, h), do(second_route, group, h))
+            copies.plan(("first", group, h), do(first_route, group, h))
+        for k in group:
+            if k:
+                copies.plan(("z", k), do(z_route, k))
 
     def add(dst, *sources):
         total = dst[...].astype(F32)
@@ -200,78 +404,102 @@
             total = total + source[...].astype(F32)
         dst[...] = total.astype(BF)
 
+    def to_core(group):
+        copies.post(("core", group))
+        local(group).start()
+
     def begin():
-        to_core(order[0])
-
-    def cores(k):
-        local(k).wait()
-        copies.got(("core", k))
-        if k:
-            to_core(order[order.index(k) + 1])
+        to_core(groups[0])
+
+    def cores(group):
+        local(group).wait()
+        copies.got(("core", group))
+        at = groups.index(group)
+        if at + 1 < len(groups):
+            to_core(groups[at + 1])
+        for other in (True, False):
+            for h in (0, 1):
+                part = second_part(group, h, other)
+                add(held.at[part], from_core.at[part])
+                if other:
+                    copies.post(("second", group, h))
+
+    def second(group):
+        span = place.span(group)
         for h in (0, 1):
-            for j, mask in ((1, 3), (0, SECOND[h])):
-                q = flip(p, mask)
-                add(held.at[k, q, half(h)], from_core.at[k, q, half(h)])
-                copies.post(
-                    ("second", k, h, j),
-                    lambda h=h, j=j, mask=mask: (
-                        held.at[k, flip(p, mask), half(h)],
-                        from_second.at[k, h, j],
-                        (flip(p, SECOND[h]) * 2 + c, z),
-                    ),
-                )
+            copies.got(("second", group, h))
+            away = 1 - x if h == 0 else 1 - y
+            add(held.at[first_part(group, h)], from_second.at[h, away, span])
+            copies.post(("first", group, h))
+
+    def first(group):
+        span = place.span(group)
         for h in (0, 1):
-            for mask in (0, FIRST[h]):
-                q = flip(p, mask)
-                add(held.at[k, q, half(h)], from_core.at[k, q, half(h)])
-
-    def second(k):
-        for h in (0, 1):
-            copies.got(("second", k, h, 1))
-            add(held.at[k, flip(p, FIRST[h]), half(h)], from_second.at[k, h, 1])
-            copies.post(
-                ("first", k, h),
-                lambda h=h: (
-                    held.at[k, flip(p, FIRST[h]), half(h)],
-                    from_first.at[k, h],
-                    (flip(p, FIRST[h]) * 2 + c, z),
-                ),
-            )
-
-    def first(k):
-        for h in (0, 1):
-            copies.got(("second", k, h, 0))
-            copies.got(("first", k, h))
-            add(held.at[k, p, half(h)], from_second.at[k, h, 0], from_first.at[k, h])
-        if k:
-            copies.post(
-                ("z", k), lambda: (held.at[k, p], from_z.at[k - 1], (p * 2 + c, flip(z, k)))
-            )
+            copies.got(("first", group, h))
+            mine = x if h == 0 else y
+            add(held.at[y, x, span, half(h)], from_second.at[h, mine, span], from_first.at[h, span])
+        for k in group:
+            if k:
+                copies.post(("z", k))
 
     def finish():
-        for k in (3, 2, 1):
+        for k in (1, 2, 3):
             copies.got(("z", k))
-        total = held[0, p].astype(F32)
+        total = held[y, x, z].astype(F32)
         for k in range(3):
             total = total + from_z[k].astype(F32)
         out[...] = total
         copies.sent()
 
-    do = functools.partial
-    plan = [begin, do(cores, 3), do(cores, 2), do(second, 3), do(cores, 1), do(second, 2)]
-    plan += [do(first, 3), do(cores, 0), do(second, 1), do(first, 2), do(second, 0)]
-    return plan + [do(first, 1), do(first, 0), finish]
-
-
-def merge_plans(plans, offset):
-    total = max(len(plan) + offset * g for g, plan in enumerate(plans))
-    merged = []
-    for t in range(total):
-        for g, plan in enumerate(plans):
-            at = t - offset * g
-            if 0 <= at < len(plan):
-                merged.append(plan[at])
-    return merged
+    if whole_first:
+        (group,) = groups
+        return [
+            (0, 0, begin),
+            (7, 1, do(cores, group)),
+            (31, 2, do(second, group)),
+            (43, 3, do(first, group)),
+            (67, 4, finish),
+        ]
+    a, b, d, e = groups
+    return [
+        (0, 0, begin),
+        (2, 1, do(cores, a)),
+        (4, 1.2, do(cores, b)),
+        (6, 2, do(second, a)),
+        (8, 2, do(cores, d)),
+        (12, 3, do(first, a)),
+        (15, 2, do(second, b)),
+        (17, 2, do(cores, e)),
+        (20, 3, do(first, b)),
+        (24, 2, do(second, d)),
+        (29, 3, do(first, d)),
+        (33, 2, do(second, e)),
+        (38, 3, do(first, e)),
+        (42, 4, finish),
+    ]
+
+
+HOP_US = 2.0
+FULL_BLOCK = 128 * 1024
+
+
+def merge_plans(jobs, plans):
+    timed = []
+    start = 0.0
+    for g, (job, plan) in enumerate(zip(jobs, plans)):
+        size = job.rows * job.width / FULL_BLOCK
+        own = 0.0 if job.beside else start
+        at = 0.0
+        for i, (volume, hops, step) in enumerate(plan):
+            ahead = 0.0 if i else min(own, 8.0 * size)
+            at = max(at, own - ahead + volume * size + hops * HOP_US)
+            timed.append((at, g, i, step))
+        if not job.beside:
+            start += 36.0 * size
+        else:
+            start += 9.0 * size
+    timed.sort(key=lambda item: item[:3])
+    return [(item[0], item[3]) for item in timed]
 
 
 ANYWHERE = pl.BlockSpec(memory_space=pl.ANY)
@@ -279,14 +507,17 @@
 
 
 class Gather:
-    def __init__(self, shard):
+    def __init__(self, shard, z_last=False):
         self.array = shard
         self.rows, self.width = shard.shape
-        self.shape = jax.ShapeDtypeStruct((4, 2, 4, self.rows, self.width), BF)
+        self.shape = jax.ShapeDtypeStruct((2, 2, 2, 4, self.rows, self.width), BF)
         self.spec = ANYWHERE
         sems = pltpu.SemaphoreType.DMA((COPIES,))
         self.scratch = [sems, sems, pltpu.SemaphoreType.DMA]
-        self.plan = gather_plan
+        self.beside = z_last
+        self.plan = gather_plan if self.rows >= 64 else gather_small_plan
+        if z_last:
+            self.plan = gather_z_last_plan
 
     def finish(self, out):
         return out.reshape(-1, self.width)
@@ -300,15 +531,16 @@
         devices = lax.axis_size("dp") * lax.axis_size("ffn")
         self.parts = parts
         self.rows, width = parts.shape[0] // devices, parts.shape[1]
+        self.width, self.beside = width, False
         self.shape = jax.ShapeDtypeStruct((self.rows, width), F32)
         self.spec = pl.BlockSpec((self.rows, width), lambda *_: (0, 0))
         sems = pltpu.SemaphoreType.DMA((COPIES,))
         rows = self.rows
         self.scratch = [
-            pltpu.VMEM((4, 4, rows, width), BF),
-            pltpu.VMEM((4, 4, rows, width), BF),
-            pltpu.VMEM((4, 2, 2, rows // 2, width), BF),
-            pltpu.VMEM((4, 2, rows // 2, width), BF),
+            pltpu.VMEM((2, 2, 4, rows, width), BF),
+            pltpu.VMEM((2, 2, 4, rows, width), BF),
+            pltpu.VMEM((2, 2, 4, rows // 2, width), BF),
+            pltpu.VMEM((2, 4, rows // 2, width), BF),
             pltpu.VMEM((3, rows, width), BF),
             sems,
             sems,
@@ -318,7 +550,7 @@
 
     @property
     def array(self):
-        return self.parts.reshape(4, 2, 4, self.rows, self.parts.shape[1])
+        return self.parts.reshape(2, 2, 2, 4, self.rows, self.parts.shape[1])
 
     def finish(self, out):
         return out
@@ -331,10 +563,11 @@
     return lax.axis_size("dp") == 8 and lax.axis_size("ffn") == 4
 
 
-def fused_call(body, steps, ins, outs, scratch, jobs, collective_id, spread=None):
+def fused_call(body, steps, ins, outs, scratch, jobs, collective_id, ticks=1, cost=(0, 1, 0)):
     plainly = not (on_fast_grid() and all(job.rows % 32 == 0 for job in jobs))
     run = [] if plainly else jobs
-    counts = [len(ins), len(run), len(outs), len(run), len(scratch)]
+    held = [i for i, item in enumerate(ins) if item[1] is None]
+    counts = [len(ins), len(run), len(outs), len(run), len(scratch), len(held), len(held)]
 
     def kernel(*refs):
         groups = []
@@ -342,36 +575,73 @@
         for count in counts:
             groups.append(refs[at : at + count])
             at += count
-        own_in, job_in, own_out, job_out, own_scratch = groups
+        own_in, job_in, own_out, job_out, own_scratch, buffers, arrived = groups
+        own_in = list(own_in)
+        loads = []
+        for i, buffer, sem in zip(held, buffers, arrived):
+            loads.append((own_in[i], buffer, sem))
+            own_in[i] = buffer
         t = pl.program_id(0)
+        if loads:
+
+            @pl.when(t == 0)
+            def _():
+                for load in loads:
+                    pltpu.make_async_copy(*load).start()
+
+        here = {}
+        rest = []
         if run:
-            place = coords()
+            place = Place()
             plans = []
             for job, src, dst in zip(run, job_in, job_out):
                 plans.append(job.plan(place, src, dst, *refs[at : at + len(job.scratch)]))
                 at += len(job.scratch)
-            merged = merge_plans(plans, 7)
-            stops = spread or steps
-            for step in range(steps):
-                now = [m for i, m in enumerate(merged[:-1]) if i * stops // len(merged) == step]
-                if step == 0:
-                    now = [greet] + now
-                if now:
-
-                    @pl.when(t == step)
-                    def _(now=now):
+            merged = merge_plans(run, plans)
+            before, each_step, after = cost
+            pace = min(1.0, (before + each_step * steps + after) / merged[-1][0])
+            position = 0
+            for when, step in merged:
+                while position < steps * ticks:
+                    clock = position * each_step / ticks + (before if position else 0)
+                    if clock >= when * pace:
+                        break
+                    position += 1
+                if position < steps * ticks:
+                    here.setdefault(position, []).append(step)
+                else:
+                    rest.append(step)
+            here.setdefault(0, []).insert(0, functools.partial(greet, place))
+
+        def tick(j):
+            for position in sorted(here):
+                if position % ticks == j:
+
+                    @pl.when(t == position // ticks)
+                    def _(now=here[position]):
                         for each in now:
                             each()
 
+        tick(0)
+        if loads:
+
+            @pl.when(t == 0)
+            def _():
+                for load in loads:
+                    pltpu.make_async_copy(*load).wait()
+
         if body is not None:
-            body(t, *own_in, *own_out, *own_scratch)
-        if run:
+            body(t, tick, *own_in, *own_out, *own_scratch)
+        if rest:
 
             @pl.when(t == steps - 1)
             def _():
-                merged[-1]()
+                for each in rest:
+                    each()
 
     all_scratch = list(scratch)
+    all_scratch += [pltpu.VMEM(ins[i][0].shape, ins[i][0].dtype) for i in held]
+    all_scratch += [pltpu.SemaphoreType.DMA] * len(held)
     for job in run:
         all_scratch += job.scratch
     extra = dict(collective_id=collective_id, has_side_effects=True) if run else {}
@@ -379,7 +649,7 @@
         kernel,
         grid=(steps,),
         out_shape=tuple(o[0] for o in outs) + tuple(job.shape for job in run),
-        in_specs=[i[1] for i in ins] + [ANYWHERE] * len(run),
+        in_specs=[i[1] or ANYWHERE for i in ins] + [ANYWHERE] * len(run),
         out_specs=tuple(o[1] for o in outs) + tuple(job.spec for job in run),
         scratch_shapes=all_scratch,
         compiler_params=pltpu.CompilerParams(vmem_limit_bytes=60 * MIB, **extra),
@@ -397,9 +667,23 @@
 
 
 def whole(array):
-    rank = len(array.shape)
-    spec = pl.BlockSpec(array.shape, lambda t: (0,) * rank, pipeline_mode=pl.Buffered(1))
-    return array, spec
+    return array, None
+
+
+def rows_of(array, first, count):
+    if on_fast_grid() and count % 16 == 0 and first % count == 0:
+        shape = (array.shape[0], count, D)
+        at = first // count
+        return array, pl.BlockSpec(shape, lambda t: (0, at, 0), pipeline_mode=pl.Buffered(1))
+    return whole(array[:, first : first + count].reshape(-1, D))
+
+
+def unit_rows(array, count, total):
+    return array, pl.BlockSpec((total // count, count, D), lambda n: (n, 0, 0))
+
+
+def flat(ref):
+    return ref[...].reshape(-1, D)
 
 
 def block(array, shape, at):
@@ -437,7 +721,7 @@
     return jnp.where(at_key <= at_query, scores, masked_score)
 
 
-def attend_body(t, x, vec, wq, wk, wv, head_vec, qkv, mixed, lse, acts):
+def attend_body(t, tick, x, vec, wq, wk, wv, head_vec, qkv, mixed, lse, acts):
     length = x.shape[0]
 
     @pl.when(t == 0)
@@ -455,6 +739,7 @@
     values = projected[:, 2 * HEAD_DIM :] + head_vec[3:4, :]
     qkv[2] = values.astype(BF)
     values_t = values.T.astype(BF)
+    tick(1)
     slope = head_slope(t)
     for start in range(0, length, QUERY_BLOCK):
         rows = start + QUERY_BLOCK
@@ -465,6 +750,8 @@
         mix = dot_nn(values_t[:, :rows], weights.astype(BF)) / totals
         mixed[start:rows, :] = mix.T.astype(BF)
         lse[0, :, start:rows] = highest + jnp.log(totals)
+        if rows < length:
+            tick(2 + start // QUERY_BLOCK)
 
 
 def attend(x, vec, qkv_full, jobs, collective_id):
@@ -492,6 +779,8 @@
         [],
         jobs,
         collective_id,
+        ticks=5,
+        cost=(3, 3.4, 0),
     )
 
 
@@ -501,13 +790,13 @@
     return pre * half, slope
 
 
-def hidden_body(t, x, mixed, out_w, vec, dy, up, bias, residual, acts, hidden, slope, down_t):
+def hidden_body(t, tick, x, mixed, out_w, vec, dy, up, bias, residual, acts, hidden, slope, down_t):
     tokens = x.shape[0]
 
     @pl.when(t == 0)
     def _():
         def enter(rows):
-            attended = dot_nt(mixed[rows, :], out_w[...]) + vec[4:5, :]
+            attended = dot_nt(mixed[rows, :], flat(out_w)) + vec[4:5, :]
             here = x[rows, :].astype(F32) + attended
             residual[rows, :] = here
             acts[rows, :] = layer_norm(here, vec[5:6, :], vec[6:7, :])[0].astype(BF)
@@ -516,26 +805,28 @@
 
     for start in range(0, tokens, 256):
         rows = slice(start, start + 256)
-        pre = dot_nt(acts[rows, :], up[...]) + bias[...]
+        pre = dot_nt(acts[rows, :], flat(up)) + bias[...]
         value, steep = gelu_pair(pre)
         hidden[rows, :] = value.astype(BF)
         slope[rows, :] = steep.astype(BF)
+        tick(1 + start // 256)
     down_t[...] = dot_tn(hidden[...], dy[...]).astype(BF)
 
 
-def hidden_forward(x, mixed, out_full, vec, dy, up_full, bias, jobs, collective_id):
+def hidden_forward(x, mixed, weights, widths, vec, dy, bias, jobs, collective_id):
     tokens = x.shape[0]
-    units = up_full.shape[0]
+    units = bias.shape[1]
+    up_rows, out_rows = widths
     return fused_call(
         hidden_body,
         units // UNITS,
         [
             whole(x),
             whole(mixed),
-            whole(out_full),
+            rows_of(weights, up_rows, out_rows),
             whole(vec),
             whole(dy),
-            block(up_full, (UNITS, D), lambda n: (n, 0)),
+            unit_rows(weights, up_rows, UNITS),
             block(bias, (1, UNITS), lambda n: (0, n)),
         ],
         [
@@ -548,11 +839,14 @@
         [],
         jobs,
         collective_id,
+        ticks=5,
+        cost=(5, 4, 0),
     )
 
 
 def hidden_back_body(
-    t, dy, acts, residual, hidden, slope, down, up, vec, out, up_t, bias_sum, dh, dh_low, sums, total, back, du
+    t, tick, dy, acts, residual, hidden, slope, down, up, vec,
+    out, up_t, bias_sum, dh, dh_low, sums, total, back, du,
 ):
     tokens = dy.shape[0]
     last = pl.num_programs(0) - 1
@@ -566,11 +860,14 @@
         def _():
             into[...] += value
 
-    accumulate(total, dot_nn(hidden[...], down[...]))
-    du[...] = (dot_nt(dy[...], down[...]) * slope[...].astype(F32)).astype(BF)
+    accumulate(total, dot_nn(hidden[...], flat(down)))
+    tick(1)
+    du[...] = (dot_nt(dy[...], flat(down)) * slope[...].astype(F32)).astype(BF)
     bias_sum[...] = jnp.sum(du[...].astype(F32), axis=0, keepdims=True)
+    tick(2)
     up_t[...] = dot_tn(du[...], acts[...]).astype(BF)
-    accumulate(back, dot_nn(du[...], up[...]))
+    tick(3)
+    accumulate(back, dot_nn(du[...], flat(up)))
 
     @pl.when(t == last)
     def _():
@@ -587,19 +884,19 @@
             dh[rows, :] = here
             low = here.astype(BF)
             dh_low[rows, :] = low
-            for row, value in enumerate((jnp.sum(low.astype(F32), axis=0), gain, shift, jnp.sum(upstream, axis=0))):
+            bias = jnp.sum(low.astype(F32), axis=0)
+            for row, value in enumerate((bias, gain, shift, jnp.sum(upstream, axis=0))):
                 sums[4 + row : 5 + row, :] += value[None]
 
         chunks(tokens, CHUNK, leave)
 
 
 def hidden_backward(
-    dy, acts, residual, hidden, slope, down_full, up_full, vec, jobs, collective_id
+    dy, acts, residual, hidden, slope, down_weights, weights, unit_count, vec, jobs, collective_id
 ):
     tokens = dy.shape[0]
-    units = up_full.shape[0]
+    units = hidden.shape[1]
     column = lambda array: block(array, (tokens, UNITS), lambda n: (0, n))
-    rows = lambda array: block(array, (UNITS, D), lambda n: (n, 0))
     return fused_call(
         hidden_back_body,
         units // UNITS,
@@ -609,8 +906,8 @@
             whole(residual),
             column(hidden),
             column(slope),
-            rows(down_full),
-            rows(up_full),
+            unit_rows(down_weights, unit_count, UNITS),
+            unit_rows(weights, unit_count, UNITS),
             whole(vec),
         ],
         [
@@ -628,11 +925,13 @@
         ],
         jobs,
         collective_id,
+        ticks=4,
+        cost=(0, 6.5, 6),
     )
 
 
 def attend_back_body(
-    t, dh_low, out_w, mixed, x, dh, vec, acts, qkv, lse, wq, wk, wv, sums_in,
+    t, tick, dh_low, out_w, mixed, x, dh, vec, acts, qkv, lse, wq, wk, wv, sums_in,
     out_t, qkv_t, grad_in, sums, upstream, grads, dk, dv, back,
 ):
     length = x.shape[0]
@@ -642,7 +941,7 @@
     @pl.when(t == 0)
     def _():
         def enter(rows):
-            value = dot_nn(dh_low[rows, :], out_w[...]).astype(BF)
+            value = dot_nn(dh_low[rows, :], flat(out_w)).astype(BF)
             for head in range(HEADS):
                 upstream[head, rows, :] = value[:, head * HEAD_DIM : (head + 1) * HEAD_DIM]
 
@@ -672,6 +971,7 @@
         else:
             dk[:rows, :] += key_part
             dv[:rows, :] += value_part
+        tick((length - start) // QUERY_BLOCK)
     grads[:, HEAD_DIM : 2 * HEAD_DIM] = (dk[...] * scale).astype(BF)
     grads[:, 2 * HEAD_DIM :] = dv[...].astype(BF)
     totals = jnp.sum(grads[...].astype(F32), axis=0, keepdims=True)
@@ -681,6 +981,7 @@
     weight_grad = dot_tn(grads[...], acts[...]).astype(BF)
     for part in range(3):
         qkv_t[part] = weight_grad[part * HEAD_DIM : (part + 1) * HEAD_DIM, :]
+    tick(length // QUERY_BLOCK + 1)
     weights = jnp.concatenate([wq[...], wk[...], wv[...]], axis=0)
     more = dot_nn(grads[...], weights)
 
@@ -705,7 +1006,7 @@
 
 
 def attend_backward(
-    dh_low, out_full, mixed, x, dh, vec, acts, qkv, lse, qkv_full, sums, jobs, collective_id
+    dh_low, weights, widths, mixed, x, dh, vec, acts, qkv, lse, qkv_full, sums, jobs, collective_id
 ):
     tokens = x.shape[0]
     head_rows = lambda part: block(
@@ -716,7 +1017,7 @@
         HEADS,
         [
             whole(dh_low),
-            whole(out_full),
+            rows_of(weights, *widths),
             whole(mixed),
             whole(x),
             whole(dh),
@@ -744,20 +1045,22 @@
         ],
         jobs,
         collective_id,
+        ticks=6,
+        cost=(9, 6.7, 6),
     )
 
 
 def renew_body(
-    t, own, full, root, n_stat, m_stat, m_root, weight, new_n, new_m, new_w, left, product
+    t, tick, own, full, root, n_stat, m_stat, m_root, weight, new_n, new_m, new_w, left, product
 ):
     last = pl.num_programs(0) - 1
     me = lax.axis_index("dp") * lax.axis_size("ffn") + lax.axis_index("ffn")
     rows_owned = m_stat.shape[0]
     share = 128 // rows_owned
     lanes = pl.ds(pl.multiple_of((me // share) * 128, 128), 128)
-    here = full[...]
+    here = flat(full)
     new_n[...] = decay_rate * n_stat[...] + (1.0 - decay_rate) * dot_nt(own[...], here)
-    left_part = dot_tn(full[:, lanes], here)
+    left_part = dot_tn(full[:, :, lanes].reshape(-1, 128), here)
     product_part = dot_nn(root[...].astype(BF), here)
 
     @pl.when(t == 0)
@@ -774,14 +1077,16 @@
     def _():
         mine = left[pl.ds(pl.multiple_of((me % share) * rows_owned, rows_owned), rows_owned), :]
         new_m[...] = decay_rate * m_stat[...] + (1.0 - decay_rate) * mine
-        step = dot_nt(product[...].astype(BF), m_root[...])
+        step = dot_nt(product[...].astype(BF), flat(m_root))
         new_w[...] = weight[...] - matrix_rate * step
 
 
-def renew(own, full, n_root, n_stat, m_stat, m_root, weight, jobs, collective_id):
-    rows, total = own.shape[0], full.shape[0]
+def renew(own, gathered, at, n_root, n_stat, m_stat, roots, root_at, weight, jobs, collective_id):
+    rows, total = own.shape[0], n_stat.shape[1]
     rows_owned = m_stat.shape[0]
     if not on_fast_grid():
+        full = gathered[:, at : at + rows].reshape(-1, D)
+        m_root = roots[:, root_at : root_at + rows_owned].reshape(-1, D)
         me = lax.axis_index("dp") * lax.axis_size("ffn") + lax.axis_index("ffn")
         new_n = decay_rate * n_stat + (1.0 - decay_rate) * dot_nt(own, full)
         mine = lax.dynamic_slice_in_dim(full, me * rows_owned, rows_owned, 1)
@@ -789,18 +1094,19 @@
         product = dot_nn(n_root.astype(BF), full)
         new_w = weight - matrix_rate * dot_nt(product.astype(BF), m_root)
         return [new_n, new_m, new_w], [job.plainly() for job in jobs]
-    size = 512
+    owners = 16 if rows == 32 else 4
+    size = owners * rows
     column = lambda array: block(array, (rows, size), lambda n: (0, n))
     return fused_call(
         renew_body,
         total // size,
         [
             whole(own),
-            block(full, (size, D), lambda n: (n, 0)),
+            block(gathered, (owners, rows, D), lambda n: (n, at // rows, 0)),
             column(n_root),
             column(n_stat),
             whole(m_stat),
-            whole(m_root),
+            rows_of(roots, root_at, rows_owned),
             whole(weight),
         ],
         [
@@ -811,6 +1117,7 @@
         [pltpu.VMEM((128, D), F32), pltpu.VMEM((rows, D), F32)],
         jobs,
         collective_id,
+        cost=(0, 1.6, 1),
     )
 
 
@@ -867,39 +1174,53 @@
     units = b_up.shape[0]
     qkv_w, out_w, up_w = w_qkv.T, w_out.T, w_up.T
     small = pack_small(vectors[None], b_up[None]).astype(BF)
+    units_rows, qkv_rows, out_rows = units, qkv_w.shape[0], out_w.shape[0]
+    root_rows = qkv_left_root.shape[0]
+
+    def stack(*items):
+        return Gather(jnp.concatenate([item.astype(BF) for item in items], axis=0))
+
+    def by_owner(array):
+        return array.reshape(owners, -1, D)
+
     small_full, qkv_full = transfer([Gather(small), Gather(qkv_w.astype(BF))], 1)
     vector_low, bias_low = unpack_small(small_full, columns, units)
     vector_rows = vector_low.transpose(1, 0, 2).reshape(8, D).astype(F32)
     up_bias = bias_low.reshape(1, -1).astype(F32)
-    (qkv, mixed, lse, acts_one), (out_full, up_full) = attend(
-        block_input, vector_rows, qkv_full, [Gather(out_w.astype(BF)), Gather(up_w.astype(BF))], 2
-    )
-    (residual, acts_two, hidden, slope, down_t), (down_full,) = hidden_forward(
+    (qkv, mixed, lse, acts_one), (up_set,) = attend(
+        block_input, vector_rows, qkv_full, [stack(up_w, out_w, qkv_left_root)], 2
+    )
+    up_set = by_owner(up_set)
+    (residual, acts_two, hidden, slope, down_t), (down_set,) = hidden_forward(
         block_input,
         mixed,
-        out_full,
+        up_set,
+        (units_rows, out_rows),
         vector_rows,
         cotangent,
-        up_full,
         up_bias,
-        [Gather(w_down.astype(BF))],
+        [stack(w_down, out_left_root)],
         3,
     )
-    (block_output, up_t, bias_grad, dh, dh_low, sums), (down_g, qkv_mroot) = hidden_backward(
+    down_set = by_owner(down_set)
+    (block_output, up_t, bias_grad, dh, dh_low, sums), (down_g, down_mroot) = hidden_backward(
         cotangent,
         acts_two,
         residual,
         hidden,
         slope,
-        down_full,
-        up_full,
+        down_set,
+        up_set,
+        units_rows,
         vector_rows,
-        [Reduce(down_t), Gather(qkv_left_root.astype(BF))],
+        [Reduce(down_t), stack(down_right_root)],
         4,
     )
-    (out_t, qkv_t, input_grad, sums), (up_g, out_mroot, up_mroot) = attend_backward(
+    down_low = down_g.astype(BF)
+    (out_t, qkv_t, input_grad, sums), (up_g, down_all) = attend_backward(
         dh_low,
-        out_full,
+        up_set,
+        (units_rows, out_rows),
         mixed,
         block_input,
         dh,
@@ -909,52 +1230,72 @@
         lse,
         qkv_full,
         sums,
-        [Reduce(up_t), Gather(out_left_root.astype(BF)), Gather(up_left_root.astype(BF))],
+        [Reduce(up_t), Gather(down_low)],
         5,
     )
     small_part = pack_small(
         sums.reshape(8, owners, columns).transpose(1, 0, 2), bias_grad.reshape(owners, units)
     ).astype(BF)
-    down_low = down_g.astype(BF)
     up_low = up_g.astype(BF)
-    qkv_g, out_g, small_g, down_all, down_mroot = transfer(
+    (new_down_n, new_down_m, new_w_down), (up_all, qkv_g, out_g, small_g) = renew(
+        down_low,
+        by_owner(down_all),
+        0,
+        down_left_root,
+        down_left,
+        down_right,
+        by_owner(down_mroot),
+        0,
+        w_down,
         [
+            stack(up_low, up_left_root),
             Reduce(qkv_t.reshape(-1, D)),
             Reduce(out_t),
             Reduce(small_part),
-            Gather(down_low),
-            Gather(down_right_root.astype(BF)),
         ],
         6,
     )
     qkv_low, out_low = qkv_g.astype(BF), out_g.astype(BF)
-    (new_down_n, new_down_m, new_w_down), (up_all,) = renew(
-        down_low,
-        down_all,
-        down_left_root,
-        down_left,
-        down_right,
-        down_mroot,
-        w_down,
-        [Gather(up_low)],
-        7,
-    )
-    (new_up_n, new_up_m, new_w_up), (qkv_all, out_all) = renew(
+    up_all = by_owner(up_all)
+    (new_up_n, new_up_m, new_w_up), (last_all,) = renew(
         up_low,
         up_all,
+        0,
         up_right_root,
         up_right,
         up_left,
-        up_mroot,
+        up_all,
+        units_rows,
         up_w,
-        [Gather(qkv_low), Gather(out_low)],
+        [stack(qkv_low, out_low)],
+        7,
+    )
+    last_all = by_owner(last_all)
+    new_qkv_n, new_qkv_m, new_w_qkv = renew(
+        qkv_low,
+        last_all,
+        0,
+        qkv_right_root,
+        qkv_right,
+        qkv_left,
+        up_set,
+        units_rows + out_rows,
+        qkv_w,
+        [],
         8,
-    )
-    new_qkv_n, new_qkv_m, new_w_qkv = renew(
-        qkv_low, qkv_all, qkv_right_root, qkv_right, qkv_left, qkv_mroot, qkv_w, [], 9
     )[0]
     new_out_n, new_out_m, new_w_out = renew(
-        out_low, out_all, out_right_root, out_right, out_left, out_mroot, out_w, [], 9
+        out_low,
+        last_all,
+        qkv_rows,
+        out_right_root,
+        out_right,
+        out_left,
+        down_set,
+        units_rows,
+        out_w,
+        [],
+        8,
     )[0]
     new_m = [new_qkv_m, new_out_m, new_up_m, new_down_m]
     new_n = [new_qkv_n, new_out_n, new_up_n, new_down_n]

time: 655 us -> 558 us (0.85)
  Pallas kernels: 612 us -> 515 us
    pallas_call x10 -> x9, Pallas kernels: 612 us -> 515 us  [fused_call(): pl.pallas_call(kernel, grid=(steps,), out_shape=tuple((o[0] for o in outs...]
    unnamed x63 -> x73, local copies, waits for them, and re-layouts: 16.9 us -> 15.7 us
where the time goes in v3:
time: 558 us; the launch traced here: 549 us
  Pallas kernels  515 us (92%)
  local copies, waits for them, and re-layouts  17.6 us (3%)
  other arithmetic  15.6 us (3%)
    pallas_call x9, Pallas kernels, fused_call(): pl.pallas_call(kernel, grid=(steps,), out_shape=tuple((o[0] for o in outs...  515 us
    unnamed x73, local copies, waits for them, and re-layouts  15.7 us

profile of v3, /device:TPU:0, one launch (start us, length us, event | category | flops | bytes accessed | tf_op | source)
XLA Modules:
  0.0 549.3 jit_solution(7591584870179499097)
XLA Ops:
  0.7 1.8 bitcast_convert_fusion.2.refs_1_
  2.5 0.7 convert.26
  3.1 0.1 reshape_broadcast_in_dim.4
  3.2 0.7 convert_bitcast_fusion
  3.9 0.6 fusion.5
  4.5 42.1 %shard_map.433 = (bf16[2,2,2,4,32,128]{5,4,3,2,1,0:T(8,128)(2,1)}, bf16[2,2,2,4,96,1024]{5,4,3,2,1,0:T(8,128)(2,1)}) custom-call(bf16[32,128]{1,0:T(8,128)(2,1)} %bitcast.81, bf16[96,1024]{1,0:T(8,128)(2,1)} %bitcast_convert_fusion.2.refs_1_), custom_call_target="tpu_custom_call" | custom-call | tf_op jit(solution)/shard_map/pallas_call | solution.py:648
  46.7 1.1 copy.62
  47.8 0.7 reshape.110.refs_1_.refs_5_.refs_3_.refs_7_
  48.6 0.2 copy.55
  48.9 0.8 pad_maximum_fusion.refs_6_
  49.7 65.5 %shard_map.434 = (bf16[3,1024,1024]{2,1,0:T(8,128)(2,1)}, bf16[1024,1024]{1,0:T(8,128)(2,1)}, f32[8,1,1024]{2,1,0:T(1,128)}, bf16[1024,1024]{1,0:T(8,128)(2,1)}, bf16[2,2,2,4,192,1024]{5,4,3,2,1,0:T(8,128)(2,1)}) custom-call(bf16[1024,1024]{1,0:T(8,128)(2,1)} %refs_3_.5, f32[8,1024]{1,0:T(8,128)} %reshape.110.refs_1_.refs_5_.refs_3_.refs_7_, ...), custom_call_target="tpu_custom_call" | custom-call | tf_op jit(solution)/shard_map/pallas_call | solution.py:648
  115.2 0.6 slice_convert_fusion.1
  115.9 0.7 pad_maximum_fusion.1.refs_7_
  116.6 64.1 %shard_map.435 = (f32[1024,1024]{1,0:T(8,128)}, bf16[1024,1024]{1,0:T(8,128)(2,1)}, bf16[1024,4096]{1,0:T(8,128)(2,1)}, bf16[1024,4096]{1,0:T(8,128)(2,1)}, bf16...) custom-call(bf16[1024,1024]{1,0:T(8,128)(2,1)} %refs_3_.5, ...), custom_call_target="tpu_custom_call" | custom-call | tf_op jit(solution)/shard_map/pallas_call | solution.py:648
  180.7 0.6 convert_element_type.75.refs_9_
  181.4 77.4 %shard_map.436 = (bf16[1024,1024]{1,0:T(8,128)(2,1)}, bf16[4096,1024]{1,0:T(8,128)(2,1)}, f32[1,4096]{1,0:T(1,128)}, f32[1024,1024]{1,0:T(8,128)}, bf16[1024,102...) custom-call(bf16[1024,1024]{1,0:T(8,128)(2,1)} %refs_0_.5, ...), custom_call_target="tpu_custom_call" | custom-call | tf_op jit(solution)/shard_map/pallas_call | solution.py:648
  258.8 1.8 convert_element_type.76.refs_14_.refs_0_
  260.6 98.0 %shard_map.437 = (bf16[1024,1024]{1,0:T(8,128)(2,1)}, bf16[3,1024,1024]{2,1,0:T(8,128)(2,1)}, bf16[1024,1024]{1,0:T(8,128)(2,1)}, f32[8,1024]{1,0:T(8,128)}, f32...) custom-call(bf16[1024,1024]{1,0:T(8,128)(2,1)} %get-tuple-element.79.refs_0_, ...), custom_call_target="tpu_custom_call" | custom-call | tf_op jit(solution)/shard_map/pallas_call | solution.py:648
  358.6 0.8 convert.28
  359.3 0.1 reshape.106
  359.5 0.1 reshape.107
  359.7 0.7 copy.60
  360.4 1.1 convert_element_type.77.refs_0_
  361.6 0.8 pad_maximum_fusion.2.refs_7_
  362.3 102.5 %shard_map.438 = (f32[128,4096]{1,0:T(8,128)}, f32[32,1024]{1,0:T(8,128)}, f32[128,1024]{1,0:T(8,128)}, bf16[2,2,2,4,160,1024]{5,4,3,2,1,0:T(8,128)(2,1)}, f32[9...) custom-call(bf16[128,1024]{1,0:T(8,128)(2,1)} %convert_element_type.76.refs_14_.refs_0_, ...), custom_call_target="tpu_custom_call" | custom-call | tf_op jit(solution)/shard_map/pallas_call | solution.py:648
  464.9 1.0 convert_element_type.80.refs_0_
  465.9 1.0 convert_element_type.81.refs_0_
  466.9 0.7 pad_maximum_fusion.3.refs_7_
  467.6 46.3 %shard_map.439 = (f32[128,4096]{1,0:T(8,128)}, f32[32,1024]{1,0:T(8,128)}, f32[128,1024]{1,0:T(8,128)}, bf16[2,2,2,4,128,1024]{5,4,3,2,1,0:T(8,128)(2,1)}) custom-call(bf16[128,1024]{1,0:T(8,128)(2,1)} %copy-done.1, bf16[32,160,1024]{2,1,0:T(8,128)(2,1)} %bitcast.54, f32[128,4096]{1,0:T(8,128)} %refs_2_.5, f32[128,4096]{1,0:T(8,128)} %refs_3_.7, ...), custom_call_target="tpu_custom_call" | custom-call | tf_op jit(solution)/shard_map/pallas_call | solution.py:648
  513.9 6.1 %shard_map.441 = (f32[32,1024]{1,0:T(8,128)}, f32[32,1024]{1,0:T(8,128)}, f32[32,1024]{1,0:T(8,128)}) custom-call(bf16[32,1024]{1,0:T(8,128)(2,1)} %copy-done.11, bf16[32,128,1024]{2,1,0:T(8,128)(2,1)} %bitcast.58, f32[32,1024]{1,0:T(8,128)} %refs_2_.7, f32[32,1024]{1,0:T(8,128)} %refs_3_.9, f32[32,1024]{1,0:T(8,128)} %refs_4_.9, ...), custom_call_target="tpu_custom_call" | custom-call | tf_op jit(solution)/shard_map/pallas_call | solution.py:648
  520.2 12.5 %shard_map.440 = (f32[96,3072]{1,0:T(8,128)}, f32[32,1024]{1,0:T(8,128)}, f32[96,1024]{1,0:T(8,128)}) custom-call(bf16[96,1024]{1,0:T(8,128)(2,1)} %copy-done.9, bf16[32,128,1024]{2,1,0:T(8,128)(2,1)} %bitcast.59, f32[96,3072]{1,0:T(8,128)} %refs_2_.6, f32[96,3072]{1,0:T(8,128)} %refs_3_.8, f32[32,1024]{1,0:T(8,128)} %refs_4_.8, ...), custom_call_target="tpu_custom_call" | custom-call | tf_op jit(solution)/shard_map/pallas_call | solution.py:648
  532.7 1.0 copy.58
  533.7 0.6 slice_reduce_fusion
  534.4 0.6 multiply_subtract_fusion
  535.0 1.1 multiply_subtract_fusion.1
  536.1 1.0 copy.57
  537.1 1.3 copy.73
  538.5 1.0 copy-done.4
  539.5 1.3 copy.74
  540.8 0.7 copy.75
  541.6 0.7 copy.76
  542.2 0.8 copy.77
  543.0 0.7 copy.78
  543.7 1.3 copy.79
  545.0 1.0 copy-done.5
  546.0 1.3 copy.80
  547.4 0.7 copy.81
  548.0 0.8 copy.82
  (69 shorter events, 0.5 us)
Async XLA Ops:
  0.7 47.9 %copy-start.13 = (f32[1024,128]{1,0:T(8,128)S(1)}, f32[1024,128]{1,0:T(8,128)}, u32[]{:S(2)}) copy-start(f32[1024,128]{1,0:T(8,128)} %param.30) | copy-start | bytes 1572868
  0.7 48.2 %copy-start.12 = (f32[1024,32]{0,1:T(8,128)S(1)}, f32[1024,32]{0,1:T(8,128)}, u32[]{:S(2)}) copy-start(f32[1024,32]{0,1:T(8,128)} %param.29) | copy-start | bytes 393220
  0.7 48.2 %copy-start.17 = (f32[32,1024]{1,0:T(8,128)S(1)}, f32[32,1024]{1,0:T(8,128)}, u32[]{:S(2)}) copy-start(f32[32,1024]{1,0:T(8,128)} %param.42) | copy-start | bytes 393220
  48.8 66.4 %copy-start = (f32[1024,128]{0,1:T(8,128)}, f32[1024,128]{0,1:T(8,128)S(1)}, u32[]{:S(2)}) copy-start(f32[1024,128]{0,1:T(8,128)S(1)} %copy.55) | copy-start | bytes 1572868
  49.7 66.1 %copy-start.2 = (f32[128,1024]{1,0:T(8,128)S(1)}, f32[128,1024]{1,0:T(8,128)}, u32[]{:S(2)}) copy-start(f32[128,1024]{1,0:T(8,128)} %refs_6_.1) | copy-start | bytes 1572868
  49.7 66.1 %copy-start.18 = (f32[32,1024]{1,0:T(8,128)S(1)}, f32[32,1024]{1,0:T(8,128)}, u32[]{:S(2)}) copy-start(f32[32,1024]{1,0:T(8,128)} %param.44) | copy-start | bytes 393220
  116.6 64.1 %copy-start.19 = (f32[32,1024]{1,0:T(8,128)S(1)}, f32[32,1024]{1,0:T(8,128)}, u32[]{:S(2)}) copy-start(f32[32,1024]{1,0:T(8,128)} %param.49) | copy-start | bytes 393220
  260.6 99.0 %copy-start.25 = (f32[1,4096]{1,0:T(1,128)S(1)}, f32[1,4096]{1,0:T(1,128)}, u32[]{:S(2)}) copy-start(f32[1,4096]{1,0:T(1,128)} %get-tuple-element.94) | copy-start | bytes 49156
  260.6 100.9 %copy-start.20 = (f32[32,1024]{1,0:T(8,128)S(1)}, f32[32,1024]{1,0:T(8,128)}, u32[]{:S(2)}) copy-start(f32[32,1024]{1,0:T(8,128)} %param.46) | copy-start | bytes 393220
  361.5 103.4 %copy-start.1 = (bf16[128,1024]{1,0:T(8,128)(2,1)}, bf16[128,1024]{1,0:T(8,128)(2,1)S(1)}, u32[]{:S(2)}) copy-start(bf16[128,1024]{1,0:T(8,128)(2,1)S(1)} %convert_element_type.77.refs_0_) | copy-start | bytes 786436
  465.9 48.0 %copy-start.9 = (bf16[96,1024]{1,0:T(8,128)(2,1)}, bf16[96,1024]{1,0:T(8,128)(2,1)S(1)}, u32[]{:S(2)}) copy-start(bf16[96,1024]{1,0:T(8,128)(2,1)S(1)} %convert_element_type.80.refs_0_) | copy-start | bytes 589828
  466.9 47.0 %copy-start.11 = (bf16[32,1024]{1,0:T(8,128)(2,1)}, bf16[32,1024]{1,0:T(8,128)(2,1)S(1)}, u32[]{:S(2)}) copy-start(bf16[32,1024]{1,0:T(8,128)(2,1)S(1)} %convert_element_type.81.refs_0_) | copy-start | bytes 196612
  520.1 12.6 %copy-start.15 = (f32[128,1024]{1,0:T(8,128)S(1)}, f32[128,1024]{1,0:T(8,128)}, u32[]{:S(2)}) copy-start(f32[128,1024]{1,0:T(8,128)} %get-tuple-element.110) | copy-start | bytes 1572868
  520.1 14.3 %copy-start.24 = (f32[8,32]{1,0:T(8,128)S(1)}, f32[8,32]{1,0:T(8,128)}, u32[]{:S(2)}) copy-start(f32[8,32]{1,0:T(8,128)} %param.32) | copy-start | bytes 3076
  520.1 14.3 %copy-start.26 = (f32[8,32]{1,0:T(8,128)S(1)}, f32[8,32]{1,0:T(8,128)}, u32[]{:S(2)}) copy-start(f32[8,32]{1,0:T(8,128)} %param.50) | copy-start | bytes 3076
  520.1 14.9 %copy-start.27 = (f32[128]{0:T(128)S(1)}, f32[128]{0:T(128)}, u32[]{:S(2)}) copy-start(f32[128]{0:T(128)} %param.33) | copy-start | bytes 1540
  520.1 14.9 %copy-start.28 = (f32[128]{0:T(128)S(1)}, f32[128]{0:T(128)}, u32[]{:S(2)}) copy-start(f32[128]{0:T(128)} %param.51) | copy-start | bytes 1540
  520.2 16.0 %copy-start.8 = (f32[128,1024]{1,0:T(8,128)S(1)}, f32[128,1024]{1,0:T(8,128)}, u32[]{:S(2)}) copy-start(f32[128,1024]{1,0:T(8,128)} %get-tuple-element.90) | copy-start | bytes 1572868
  532.7 4.4 copy-start.3
  534.4 4.0 copy-start.23
  537.1 2.3 copy-start.4
  539.5 1.3 copy-start.10
  539.5 2.1 copy-start.16
  539.5 2.7 copy-start.7
  539.5 3.5 copy-start.22
  540.8 2.9 copy-start.6
  543.7 2.3 copy-start.5
  546.0 1.3 copy-start.21
  546.0 2.0 copy-start.14

commit v4 on v3

--- a/solution.py
+++ b/solution.py
@@ -1,4 +1,5 @@
 import functools
+import math
 
 import jax
 import jax.numpy as jnp
@@ -399,6 +400,9 @@
                 copies.plan(("z", k), do(z_route, k))
 
     def add(dst, *sources):
+        if len(sources) == 1:
+            dst[...] += sources[0][...]
+            return
         total = dst[...].astype(F32)
         for source in sources:
             total = total + source[...].astype(F32)
@@ -483,7 +487,7 @@
 FULL_BLOCK = 128 * 1024
 
 
-def merge_plans(jobs, plans):
+def merge_plans(jobs, plans, stagger):
     timed = []
     start = 0.0
     for g, (job, plan) in enumerate(zip(jobs, plans)):
@@ -491,15 +495,15 @@
         own = 0.0 if job.beside else start
         at = 0.0
         for i, (volume, hops, step) in enumerate(plan):
-            ahead = 0.0 if i else min(own, 8.0 * size)
+            ahead = 0.0 if i else min(own, 20.0 * size)
             at = max(at, own - ahead + volume * size + hops * HOP_US)
             timed.append((at, g, i, step))
         if not job.beside:
-            start += 36.0 * size
+            start += stagger * size
         else:
             start += 9.0 * size
     timed.sort(key=lambda item: item[:3])
-    return [(item[0], item[3]) for item in timed]
+    return [(at, step, g, i == len(plans[g]) - 1) for at, g, i, step in timed]
 
 
 ANYWHERE = pl.BlockSpec(memory_space=pl.ANY)
@@ -563,7 +567,20 @@
     return lax.axis_size("dp") == 8 and lax.axis_size("ffn") == 4
 
 
-def fused_call(body, steps, ins, outs, scratch, jobs, collective_id, ticks=1, cost=(0, 1, 0)):
+def fused_call(
+    body,
+    steps,
+    ins,
+    outs,
+    scratch,
+    jobs,
+    collective_id,
+    ticks=1,
+    cost=(0, 1, 0),
+    stagger=28.0,
+    needs=None,
+    timeline=None,
+):
     plainly = not (on_fast_grid() and all(job.rows % 32 == 0 for job in jobs))
     run = [] if plainly else jobs
     held = [i for i, item in enumerate(ins) if item[1] is None]
@@ -597,25 +614,32 @@
             for job, src, dst in zip(run, job_in, job_out):
                 plans.append(job.plan(place, src, dst, *refs[at : at + len(job.scratch)]))
                 at += len(job.scratch)
-            merged = merge_plans(run, plans)
+            merged = merge_plans(run, plans, stagger)
             before, each_step, after = cost
             pace = min(1.0, (before + each_step * steps + after) / merged[-1][0])
+            spans = [(before * (i > 0) + each_step * i, each_step) for i in range(steps)]
+            if timeline:
+                pace = 1.0
+                spans = timeline({g: when for when, _, g, is_last in merged if is_last})
+            clocks = [0.0]
+            for start, length in spans:
+                clocks += [start + length * j / ticks for j in range(ticks)]
+            clocks = [0.0] + clocks[2:]
+            limits = [(needs or {}).get(g, steps) * ticks if is_last else steps * ticks for _, _, g, is_last in merged]
             position = 0
-            for when, step in merged:
-                while position < steps * ticks:
-                    clock = position * each_step / ticks + (before if position else 0)
-                    if clock >= when * pace:
-                        break
+            for i, (when, step, _, _) in enumerate(merged):
+                while position < steps * ticks and clocks[position] < when * pace:
                     position += 1
+                position = min([position] + limits[i:])
                 if position < steps * ticks:
                     here.setdefault(position, []).append(step)
                 else:
                     rest.append(step)
             here.setdefault(0, []).insert(0, functools.partial(greet, place))
 
-        def tick(j):
+        def tick(j, least=0, most=steps):
             for position in sorted(here):
-                if position % ticks == j:
+                if position % ticks == j and least <= position // ticks < most:
 
                     @pl.when(t == position // ticks)
                     def _(now=here[position]):
@@ -631,7 +655,8 @@
                     pltpu.make_async_copy(*load).wait()
 
         if body is not None:
-            body(t, tick, *own_in, *own_out, *own_scratch)
+            shared = [job_out] if needs else []
+            body(t, tick, *shared, *own_in, *own_out, *own_scratch)
         if rest:
 
             @pl.when(t == steps - 1)
@@ -844,40 +869,35 @@
     )
 
 
+def accumulate(t, into, value):
+    @pl.when(t == 0)
+    def _():
+        into[...] = value
+
+    @pl.when(t > 0)
+    def _():
+        into[...] += value
+
+
 def hidden_back_body(
-    t, tick, dy, acts, residual, hidden, slope, down, up, vec,
-    out, up_t, bias_sum, dh, dh_low, sums, total, back, du,
+    t, tick, dy, acts, residual, slope, down, up, vec, up_t, bias_sum, dh, dh_low, sums, back, du
 ):
     tokens = dy.shape[0]
     last = pl.num_programs(0) - 1
-
-    def accumulate(into, value):
-        @pl.when(t == 0)
-        def _():
-            into[...] = value
-
-        @pl.when(t > 0)
-        def _():
-            into[...] += value
-
-    accumulate(total, dot_nn(hidden[...], flat(down)))
-    tick(1)
     du[...] = (dot_nt(dy[...], flat(down)) * slope[...].astype(F32)).astype(BF)
     bias_sum[...] = jnp.sum(du[...].astype(F32), axis=0, keepdims=True)
+    tick(1)
+    up_t[...] = dot_tn(du[...], acts[...]).astype(BF)
     tick(2)
-    up_t[...] = dot_tn(du[...], acts[...]).astype(BF)
-    tick(3)
-    accumulate(back, dot_nn(du[...], flat(up)))
+    accumulate(t, back, dot_nn(du[...], flat(up)))
 
     @pl.when(t == last)
     def _():
         sums[...] = jnp.zeros_like(sums)
 
         def leave(rows):
-            here = residual[rows, :]
-            out[rows, :] = (here + total[rows, :] + vec[7:8, :]).astype(BF)
             grad = back[rows, :]
-            normed, inverse = layer_norm(here, 1.0, 0.0)[1:]
+            normed, inverse = layer_norm(residual[rows, :], 1.0, 0.0)[1:]
             change, gain, shift = norm_backward(grad, normed, inverse, vec[5:6, :])
             upstream = dy[rows, :].astype(F32)
             here = upstream + change
@@ -892,11 +912,10 @@
 
 
 def hidden_backward(
-    dy, acts, residual, hidden, slope, down_weights, weights, unit_count, vec, jobs, collective_id
+    dy, acts, residual, slope, down_weights, weights, unit_count, vec, jobs, collective_id
 ):
     tokens = dy.shape[0]
-    units = hidden.shape[1]
-    column = lambda array: block(array, (tokens, UNITS), lambda n: (0, n))
+    units = slope.shape[1]
     return fused_call(
         hidden_back_body,
         units // UNITS,
@@ -904,39 +923,61 @@
             whole(dy),
             whole(acts),
             whole(residual),
-            column(hidden),
-            column(slope),
+            block(slope, (tokens, UNITS), lambda n: (0, n)),
             unit_rows(down_weights, unit_count, UNITS),
             unit_rows(weights, unit_count, UNITS),
             whole(vec),
         ],
         [
-            result((tokens, D), BF),
             result((units, D), BF, (UNITS, D), lambda n: (n, 0)),
             result((1, units), F32, (1, UNITS), lambda n: (0, n)),
             result((tokens, D), F32),
             result((tokens, D), BF),
             result((8, D), F32),
         ],
-        [
-            pltpu.VMEM((tokens, D), F32),
-            pltpu.VMEM((tokens, D), F32),
-            pltpu.VMEM((tokens, UNITS), BF),
-        ],
+        [pltpu.VMEM((tokens, D), F32), pltpu.VMEM((tokens, UNITS), BF)],
         jobs,
         collective_id,
-        ticks=4,
-        cost=(0, 6.5, 6),
+        ticks=3,
+        cost=(0, 5, 5),
+        stagger=10.0,
     )
 
 
+def output_body(t, tick, hidden, down, residual, vec, out, total):
+    accumulate(t, total, dot_nn(hidden[...], flat(down)))
+
+    @pl.when(t == pl.num_programs(0) - 1)
+    def _():
+        def leave(rows):
+            out[rows, :] = (residual[rows, :] + total[rows, :] + vec[7:8, :]).astype(BF)
+
+        chunks(hidden.shape[0], CHUNK, leave)
+
+
+def output_part(hidden, down_weights, unit_count, residual, vec):
+    tokens = hidden.shape[0]
+    return (
+        output_body,
+        [
+            block(hidden, (tokens, UNITS), lambda n: (0, n)),
+            unit_rows(down_weights, unit_count, UNITS),
+            whole(residual),
+            whole(vec),
+        ],
+        [result((tokens, D), BF)],
+        [pltpu.VMEM((tokens, D), F32)],
+        (0, 1.7, 2),
+    )
+
+
 def attend_back_body(
-    t, tick, dh_low, out_w, mixed, x, dh, vec, acts, qkv, lse, wq, wk, wv, sums_in,
-    out_t, qkv_t, grad_in, sums, upstream, grads, dk, dv, back,
+    t, tick, dh_low, out_w, mixed, acts, qkv, lse, sums_in,
+    out_t, qkv_t, grads_out, sums, upstream, dk, dv,
 ):
-    length = x.shape[0]
-    last = pl.num_programs(0) - 1
+    length = acts.shape[0]
     scale = HEAD_DIM ** (-0.5)
+    grads = grads_out.at[0]
 
     @pl.when(t == 0)
     def _():
@@ -981,37 +1022,10 @@
     weight_grad = dot_tn(grads[...], acts[...]).astype(BF)
     for part in range(3):
         qkv_t[part] = weight_grad[part * HEAD_DIM : (part + 1) * HEAD_DIM, :]
-    tick(length // QUERY_BLOCK + 1)
-    weights = jnp.concatenate([wq[...], wk[...], wv[...]], axis=0)
-    more = dot_nn(grads[...], weights)
-
-    @pl.when(t == 0)
-    def _():
-        back[...] = more
-
-    @pl.when(t > 0)
-    def _():
-        back[...] += more
-
-    @pl.when(t == last)
-    def _():
-        def leave(rows):
-            normed, inverse = layer_norm(x[rows, :].astype(F32), 1.0, 0.0)[1:]
-            change, gain, shift = norm_backward(back[rows, :], normed, inverse, vec[0:1, :])
-            grad_in[rows, :] = (dh[rows, :] + change).astype(BF)
-            sums[0:1, :] += gain[None]
-            sums[1:2, :] += shift[None]
-
-        chunks(length, CHUNK, leave)
-
-
-def attend_backward(
-    dh_low, weights, widths, mixed, x, dh, vec, acts, qkv, lse, qkv_full, sums, jobs, collective_id
-):
-    tokens = x.shape[0]
-    head_rows = lambda part: block(
-        qkv_full, (HEAD_DIM, D), lambda h: (part * HEADS + h, 0)
-    )
+
+
+def attend_backward(dh_low, weights, widths, mixed, acts, qkv, lse, sums, jobs, collective_id):
+    tokens = acts.shape[0]
     return fused_call(
         attend_back_body,
         HEADS,
@@ -1019,34 +1033,230 @@
             whole(dh_low),
             rows_of(weights, *widths),
             whole(mixed),
-            whole(x),
-            whole(dh),
-            whole(vec),
             whole(acts),
             block(qkv, (3, tokens, HEAD_DIM), lambda h: (0, 0, h)),
             block(lse, (1, 1, tokens), lambda h: (h, 0, 0)),
-            head_rows(0),
-            head_rows(1),
-            head_rows(2),
             whole(sums),
         ],
         [
             result((D, D), BF),
             result((3, D, D), BF, (3, HEAD_DIM, D), lambda h: (0, h, 0)),
-            result((tokens, D), BF),
+            result(
+                (HEADS, tokens, 3 * HEAD_DIM), BF, (1, tokens, 3 * HEAD_DIM), lambda h: (h, 0, 0)
+            ),
             result((8, D), F32),
         ],
         [
             pltpu.VMEM((HEADS, tokens, HEAD_DIM), BF),
-            pltpu.VMEM((tokens, 3 * HEAD_DIM), BF),
             pltpu.VMEM((tokens, HEAD_DIM), F32),
             pltpu.VMEM((tokens, HEAD_DIM), F32),
-            pltpu.VMEM((tokens, D), F32),
         ],
         jobs,
         collective_id,
-        ticks=6,
-        cost=(9, 6.7, 6),
+        ticks=5,
+        cost=(7, 5.4, 0),
+        stagger=0.1,
+    )
+
+
+def input_body(t, tick, grads, wq, wk, wv, x, dh, vec, grad_in, sums, back):
+    weights = jnp.concatenate([wq[...], wk[...], wv[...]], axis=0)
+    accumulate(t, back, dot_nn(grads[0], weights))
+
+    @pl.when(t == pl.num_programs(0) - 1)
+    def _():
+        sums[...] = jnp.zeros_like(sums)
+
+        def leave(rows):
+            normed, inverse = layer_norm(x[rows, :].astype(F32), 1.0, 0.0)[1:]
+            change, gain, shift = norm_backward(back[rows, :], normed, inverse, vec[0:1, :])
+            grad_in[rows, :] = (dh[rows, :] + change).astype(BF)
+            sums[0:1, :] += gain[None]
+            sums[1:2, :] += shift[None]
+
+        chunks(x.shape[0], CHUNK, leave)
+
+
+def input_part(grads, qkv_full, x, dh, vec):
+    tokens = x.shape[0]
+    head_rows = lambda part: block(qkv_full, (HEAD_DIM, D), lambda h: (part * HEADS + h, 0))
+    return (
+        input_body,
+        [
+            block(grads, (1, tokens, 3 * HEAD_DIM), lambda h: (h, 0, 0)),
+            head_rows(0),
+            head_rows(1),
+            head_rows(2),
+            whole(x),
+            whole(dh),
+            whole(vec),
+        ],
+        [result((tokens, D), BF), result((8, D), F32)],
+        [pltpu.VMEM((tokens, D), F32)],
+        (0, 2, 6),
+    )
+
+
+def owner_place(owner):
+    return owner // 16, (owner // 8) % 2, (owner // 4) % 2, owner % 4
+
+
+def forward_body(
+    t, tick, gathered, x, dy, qkv, mixed, lse, acts_one, residual, acts, hidden, slope, down_t, vec,
+    small, qkv_w, up_w, out_w, bias, small_sem, qkv_sem, up_sem, out_sem,
+):
+    small_all, qkv_all, up_all, _ = gathered
+    length = x.shape[0]
+    owned = qkv_w.shape[4]
+    up_rows = up_w.shape[2]
+    out_rows = out_w.shape[4]
+
+    def load_up(n):
+        dst = up_w.at[n % 2]
+        src = up_all.at[n // 4, (n // 2) % 2, n % 2, :, pl.ds(0, up_rows)]
+        return pltpu.make_async_copy(src, dst, up_sem.at[n % 2])
+
+    def load_out():
+        return pltpu.make_async_copy(
+            up_all.at[:, :, :, :, pl.ds(up_rows, out_rows)], out_w, out_sem
+        )
+
+    @pl.when(t == 0)
+    def _():
+        weights = pltpu.make_async_copy(qkv_all, qkv_w, qkv_sem)
+        vectors = pltpu.make_async_copy(small_all, small, small_sem)
+        weights.start()
+        vectors.start()
+        vectors.wait()
+        for group in range(8):
+            total = jnp.zeros((8, 128), F32)
+            for z in range(4):
+                part = small[group // 4, (group // 2) % 2, group % 2, z].astype(F32)
+                total = total + part[:8, :]
+                at = (group * 4 + z) * 128
+                bias[:, at : at + 128] = part[8:9, :]
+            vec[:, group * 128 : (group + 1) * 128] = total
+
+        def norm(rows):
+            normed = layer_norm(x[rows, :].astype(F32), vec[0:1, :], vec[1:2, :])[0]
+            acts_one[rows, :] = normed.astype(BF)
+
+        chunks(length, CHUNK, norm)
+        weights.wait()
+
+    @pl.when(t < HEADS)
+    def _():
+        unit = math.gcd(owned, HEAD_DIM)
+        pieces = []
+        for part in range(3):
+            for i in range(HEAD_DIM // unit):
+                index = (part * HEADS + t) * (HEAD_DIM // unit) + i
+                per_owner = owned // unit
+                row = pl.multiple_of((index % per_owner) * unit, unit)
+                pieces.append(qkv_w[(*owner_place(index // per_owner), pl.ds(row, unit))])
+        lanes = pl.ds(pl.multiple_of(t * HEAD_DIM, HEAD_DIM), HEAD_DIM)
+        projected = dot_nt(acts_one[...], jnp.concatenate(pieces, axis=0))
+        qkv[0] = (projected[:, :HEAD_DIM] + vec[2:3, lanes]).astype(BF)
+        qkv[1] = projected[:, HEAD_DIM : 2 * HEAD_DIM].astype(BF)
+        values = projected[:, 2 * HEAD_DIM :] + vec[3:4, lanes]
+        qkv[2] = values.astype(BF)
+        values_t = values.T.astype(BF)
+        tick(1, 0, HEADS)
+        level = head_slope(t)
+        for start in range(0, length, QUERY_BLOCK):
+            rows = start + QUERY_BLOCK
+            scores = scores_t(qkv[0, start:rows, :], qkv[1, :rows, :], level, start, rows)
+            highest = jnp.max(scores, axis=0, keepdims=True)
+            weights = jnp.exp(scores - highest)
+            totals = jnp.sum(weights, axis=0, keepdims=True)
+            mix = dot_nn(values_t[:, :rows], weights.astype(BF)) / totals
+            mixed[start:rows, lanes] = mix.T.astype(BF)
+            lse[0, :, start:rows] = highest + jnp.log(totals)
+            if rows < length:
+                tick(2 + start // QUERY_BLOCK, 0, HEADS)
+
+    @pl.when(t == HEADS)
+    def _():
+        load_out().start()
+        load_up(0).start()
+        load_out().wait()
+
+        def enter(rows):
+            attended = dot_nt(mixed[rows, :], flat(out_w)) + vec[4:5, :]
+            here = x[rows, :].astype(F32) + attended
+            residual[rows, :] = here
+            acts[rows, :] = layer_norm(here, vec[5:6, :], vec[6:7, :])[0].astype(BF)
+
+        chunks(length, 2 * CHUNK, enter)
+
+    @pl.when(t >= HEADS)
+    def _():
+        n = t - HEADS
+        load_up(n).wait()
+
+        @pl.when(t < pl.num_programs(0) - 1)
+        def _():
+            load_up(n + 1).start()
+
+        weights = up_w.at[n % 2]
+        lanes = pl.ds(pl.multiple_of(n * UNITS, UNITS), UNITS)
+        for start in range(0, length, 256):
+            rows = slice(start, start + 256)
+            pre = dot_nt(acts[rows, :], flat(weights)) + bias[:, lanes]
+            value, steep = gelu_pair(pre)
+            hidden[rows, :] = value.astype(BF)
+            slope[rows, :] = steep.astype(BF)
+            tick(1 + start // 256, HEADS)
+        down_t[...] = dot_tn(hidden[...], dy[...]).astype(BF)
+
+
+def forward(x, dy, small, qkv_w, up_set, down_set, units_rows, out_rows, collective_id):
+    tokens = x.shape[0]
+    units = 32 * units_rows
+    steps = HEADS + units // UNITS
+    head = lambda t: jnp.minimum(t, HEADS - 1)
+    unit = lambda t: jnp.maximum(t - HEADS, 0)
+    jobs = [Gather(small), Gather(qkv_w), Gather(up_set), Gather(down_set)]
+
+    def timeline(ends):
+        spans = [(ends[1] + 4 + 3.5 * i, 3.5) for i in range(HEADS)]
+        start = max(ends[1] + 4 + 3.5 * HEADS, ends[2])
+        return spans + [(start + 5 * (i > 0) + 4 * i, 4) for i in range(steps - HEADS)]
+
+    column = result((tokens, units), BF, (tokens, UNITS), lambda t: (0, unit(t)))
+    return fused_call(
+        forward_body,
+        steps,
+        [whole(x), whole(dy)],
+        [
+            result((3, tokens, D), BF, (3, tokens, HEAD_DIM), lambda t: (0, 0, head(t))),
+            result((tokens, D), BF),
+            result((HEADS, 1, tokens), F32, (1, 1, tokens), lambda t: (head(t), 0, 0)),
+            result((tokens, D), BF),
+            result((tokens, D), F32),
+            result((tokens, D), BF),
+            column,
+            column,
+            result((units, D), BF, (UNITS, D), lambda t: (unit(t), 0)),
+            result((8, D), F32),
+        ],
+        [
+            pltpu.VMEM(jobs[0].shape.shape, BF),
+            pltpu.VMEM(jobs[1].shape.shape, BF),
+            pltpu.VMEM((2, 4, units_rows, D), BF),
+            pltpu.VMEM((2, 2, 2, 4, out_rows, D), BF),
+            pltpu.VMEM((1, units), F32),
+            pltpu.SemaphoreType.DMA,
+            pltpu.SemaphoreType.DMA,
+            pltpu.SemaphoreType.DMA((2,)),
+            pltpu.SemaphoreType.DMA,
+        ],
+        jobs,
+        collective_id,
+        ticks=5,
+        stagger=36.0,
+        needs={0: 0, 1: 0, 2: HEADS, 3: steps},
+        timeline=timeline,
     )
 
 
@@ -1081,10 +1291,14 @@
         new_w[...] = weight[...] - matrix_rate * step
 
 
-def renew(own, gathered, at, n_root, n_stat, m_stat, roots, root_at, weight, jobs, collective_id):
+def renew(
+    own, gathered, at, n_root, n_stat, m_stat, roots, root_at, weight, jobs, collective_id, part=None
+):
     rows, total = own.shape[0], n_stat.shape[1]
     rows_owned = m_stat.shape[0]
+    body, ins, outs, scratch, more = part or (None, [], [], [], (0, 0, 0))
     if not on_fast_grid():
+        extra = fused_call(body, 8, ins, outs, scratch, [], collective_id)[0] if part else []
         full = gathered[:, at : at + rows].reshape(-1, D)
         m_root = roots[:, root_at : root_at + rows_owned].reshape(-1, D)
         me = lax.axis_index("dp") * lax.axis_size("ffn") + lax.axis_index("ffn")
@@ -1093,31 +1307,46 @@
         new_m = decay_rate * m_stat + (1.0 - decay_rate) * dot_tn(mine, full)
         product = dot_nn(n_root.astype(BF), full)
         new_w = weight - matrix_rate * dot_nt(product.astype(BF), m_root)
-        return [new_n, new_m, new_w], [job.plainly() for job in jobs]
+        return [new_n, new_m, new_w] + extra, [job.plainly() for job in jobs]
     owners = 16 if rows == 32 else 4
     size = owners * rows
     column = lambda array: block(array, (rows, size), lambda n: (0, n))
+    own_ins = [
+        whole(own),
+        block(gathered, (owners, rows, D), lambda n: (n, at // rows, 0)),
+        column(n_root),
+        column(n_stat),
+        whole(m_stat),
+        rows_of(roots, root_at, rows_owned),
+        whole(weight),
+    ]
+    own_outs = [
+        result((rows, total), F32, (rows, size), lambda n: (0, n)),
+        result((rows_owned, D), F32),
+        result((rows, D), F32),
+    ]
+    own_scratch = [pltpu.VMEM((128, D), F32), pltpu.VMEM((rows, D), F32)]
+    sizes = [len(own_ins), len(ins), len(own_outs), len(outs), len(own_scratch), len(scratch)]
+
+    def both(t, tick, *refs):
+        cuts = [sum(sizes[:i]) for i in range(len(sizes) + 1)]
+        groups = [refs[i:j] for i, j in zip(cuts, cuts[1:])]
+        renew_body(t, tick, *groups[0], *groups[2], *groups[4])
+        if part:
+            tick(1)
+            body(t, tick, *groups[1], *groups[3], *groups[5])
+
     return fused_call(
-        renew_body,
+        both,
         total // size,
-        [
-            whole(own),
-            block(gathered, (owners, rows, D), lambda n: (n, at // rows, 0)),
-            column(n_root),
-            column(n_stat),
-            whole(m_stat),
-            rows_of(roots, root_at, rows_owned),
-            whole(weight),
-        ],
-        [
-            result((rows, total), F32, (rows, size), lambda n: (0, n)),
-            result((rows_owned, D), F32),
-            result((rows, D), F32),
-        ],
-        [pltpu.VMEM((128, D), F32), pltpu.VMEM((rows, D), F32)],
+        own_ins + ins,
+        own_outs + outs,
+        own_scratch + scratch,
         jobs,
         collective_id,
-        cost=(0, 1.6, 1),
+        ticks=2 if part else 1,
+        cost=(0, 1.6 + more[1], 1 + more[2]),
+        stagger=0.1 if len(jobs) > 2 else 36.0,
     )
 
 
@@ -1173,7 +1402,6 @@
     columns = vectors.shape[1]
     units = b_up.shape[0]
     qkv_w, out_w, up_w = w_qkv.T, w_out.T, w_up.T
-    small = pack_small(vectors[None], b_up[None]).astype(BF)
     units_rows, qkv_rows, out_rows = units, qkv_w.shape[0], out_w.shape[0]
     root_rows = qkv_left_root.shape[0]
 
@@ -1183,31 +1411,53 @@
     def by_owner(array):
         return array.reshape(owners, -1, D)
 
-    small_full, qkv_full = transfer([Gather(small), Gather(qkv_w.astype(BF))], 1)
-    vector_low, bias_low = unpack_small(small_full, columns, units)
-    vector_rows = vector_low.transpose(1, 0, 2).reshape(8, D).astype(F32)
-    up_bias = bias_low.reshape(1, -1).astype(F32)
-    (qkv, mixed, lse, acts_one), (up_set,) = attend(
-        block_input, vector_rows, qkv_full, [stack(up_w, out_w, qkv_left_root)], 2
-    )
-    up_set = by_owner(up_set)
-    (residual, acts_two, hidden, slope, down_t), (down_set,) = hidden_forward(
-        block_input,
-        mixed,
-        up_set,
-        (units_rows, out_rows),
-        vector_rows,
-        cotangent,
-        up_bias,
-        [stack(w_down, out_left_root)],
-        3,
-    )
-    down_set = by_owner(down_set)
-    (block_output, up_t, bias_grad, dh, dh_low, sums), (down_g, down_mroot) = hidden_backward(
+    up_block = [up_w, out_w]
+    down_block = [w_down, out_left_root, qkv_left_root]
+    if on_fast_grid():
+        lane = (lax.axis_index("ffn") * columns).astype(jnp.int32)
+        small = jnp.zeros((SMALL_ROWS, SMALL_WIDTH), BF)
+        small = lax.dynamic_update_slice(small, vectors.astype(BF), (0, lane))
+        small = lax.dynamic_update_slice(small, b_up.astype(BF)[None], (8, 0))
+        results, gathered = forward(
+            block_input,
+            cotangent,
+            small,
+            qkv_w.astype(BF),
+            stack(*up_block).array,
+            stack(*down_block).array,
+            units_rows,
+            out_rows,
+            1,
+        )
+        qkv, mixed, logsum, acts_one, residual, acts_two, hidden, slope, down_t, vector_rows = results
+        _, qkv_full, up_set, down_set = gathered
+        up_set, down_set = by_owner(up_set), by_owner(down_set)
+    else:
+        small = pack_small(vectors[None], b_up[None]).astype(BF)
+        small_full, qkv_full = transfer([Gather(small), Gather(qkv_w.astype(BF))], 1)
+        vector_low, bias_low = unpack_small(small_full, columns, units)
+        vector_rows = vector_low.transpose(1, 0, 2).reshape(8, D).astype(F32)
+        up_bias = bias_low.reshape(1, -1).astype(F32)
+        (qkv, mixed, logsum, acts_one), (up_set,) = attend(
+            block_input, vector_rows, qkv_full, [stack(*up_block)], 2
+        )
+        up_set = by_owner(up_set)
+        (residual, acts_two, hidden, slope, down_t), (down_set,) = hidden_forward(
+            block_input,
+            mixed,
+            up_set,
+            (units_rows, out_rows),
+            vector_rows,
+            cotangent,
+            up_bias,
+            [stack(*down_block)],
+            3,
+        )
+        down_set = by_owner(down_set)
+    (up_t, bias_grad, dh, dh_low, sums), (down_g, down_mroot) = hidden_backward(
         cotangent,
         acts_two,
         residual,
-        hidden,
         slope,
         down_set,
         up_set,
@@ -1217,27 +1467,20 @@
         4,
     )
     down_low = down_g.astype(BF)
-    (out_t, qkv_t, input_grad, sums), (up_g, down_all) = attend_backward(
+    (out_t, qkv_t, qkv_grads, sums), (up_g, down_all) = attend_backward(
         dh_low,
         up_set,
         (units_rows, out_rows),
         mixed,
-        block_input,
-        dh,
-        vector_rows,
         acts_one,
         qkv,
-        lse,
-        qkv_full,
+        logsum,
         sums,
         [Reduce(up_t), Gather(down_low)],
         5,
     )
-    small_part = pack_small(
-        sums.reshape(8, owners, columns).transpose(1, 0, 2), bias_grad.reshape(owners, units)
-    ).astype(BF)
     up_low = up_g.astype(BF)
-    (new_down_n, new_down_m, new_w_down), (up_all, qkv_g, out_g, small_g) = renew(
+    (new_down_n, new_down_m, new_w_down, input_grad, first_sums), (up_all, qkv_g, out_g) = renew(
         down_low,
         by_owner(down_all),
         0,
@@ -1247,17 +1490,17 @@
         by_owner(down_mroot),
         0,
         w_down,
-        [
-            stack(up_low, up_left_root),
-            Reduce(qkv_t.reshape(-1, D)),
-            Reduce(out_t),
-            Reduce(small_part),
-        ],
+        [stack(up_low, up_left_root), Reduce(qkv_t.reshape(-1, D)), Reduce(out_t)],
         6,
+        input_part(qkv_grads, qkv_full, block_input, dh, vector_rows),
     )
+    small_part = pack_small(
+        (sums + first_sums).reshape(8, owners, columns).transpose(1, 0, 2),
+        bias_grad.reshape(owners, units),
+    ).astype(BF)
     qkv_low, out_low = qkv_g.astype(BF), out_g.astype(BF)
     up_all = by_owner(up_all)
-    (new_up_n, new_up_m, new_w_up), (last_all,) = renew(
+    (new_up_n, new_up_m, new_w_up, block_output), (last_all, small_g) = renew(
         up_low,
         up_all,
         0,
@@ -1267,8 +1510,9 @@
         up_all,
         units_rows,
         up_w,
-        [stack(qkv_low, out_low)],
+        [stack(qkv_low, out_low), Reduce(small_part)],
         7,
+        output_part(hidden, down_set, units_rows, residual, vector_rows),
     )
     last_all = by_owner(last_all)
     new_qkv_n, new_qkv_m, new_w_qkv = renew(
@@ -1278,8 +1522,8 @@
         qkv_right_root,
         qkv_right,
         qkv_left,
-        up_set,
-        units_rows + out_rows,
+        down_set,
+        units_rows + root_rows,
         qkv_w,
         [],
         8,

time: 558 us -> 521 us (0.934); the launches traced: 549 us -> 520 us
  Pallas kernels: 515 us -> 487 us
    pallas_call x9 -> x7, Pallas kernels: 515 us -> 487 us  [fused_call(): pl.pallas_call(kernel, grid=(steps,), out_shape=tuple((o[0] for o in outs...]
    unnamed x73 -> x74, local copies, waits for them, and re-layouts: 15.7 us -> 15.8 us
where the time goes in v4:
time: 521 us; the launch traced here: 520 us
  Pallas kernels  487 us (93%)
  local copies, waits for them, and re-layouts  17 us (3%)
  other arithmetic  14.3 us (3%)
    pallas_call x7, Pallas kernels, fused_call(): pl.pallas_call(kernel, grid=(steps,), out_shape=tuple((o[0] for o in outs...  487 us
    unnamed x74, local copies, waits for them, and re-layouts  15.8 us

profile of v4, /device:TPU:0, one launch (start us, length us, event | category | flops | bytes accessed | tf_op | source)
XLA Modules:
  0.0 519.9 jit_solution(16289433918125469737)
XLA Ops:
  0.7 0.0 copy-start.2
  0.7 0.8 convert_element_type.49
  1.5 0.2 dynamic_update_slice.6
  1.7 0.7 convert_bitcast_fusion
  2.4 1.3 copy.50
  3.7 1.1 bitcast_convert_fusion
  4.8 0.7 pad_maximum_fusion.1.refs_4_
  5.6 0.8 pad_maximum_fusion.refs_5_
  6.4 0.7 bitcast_convert_fusion.2.refs_3_
  7.1 162.4 %shard_map.433 = (bf16[3,1024,1024]{2,1,0:T(8,128)(2,1)}, bf16[1024,1024]{1,0:T(8,128)(2,1)}, f32[8,1,1024]{2,1,0:T(1,128)}, bf16[1024,1024]{1,0:T(8,128)(2,1)},...) custom-call(bf16[1024,1024]{1,0:T(8,128)(2,1)} %refs_11_.1, ...), custom_call_target="tpu_custom_call" | custom-call | tf_op jit(solution)/shard_map/pallas_call | solution.py:673
  169.5 0.6 convert_element_type.57.refs_8_
  170.2 68.6 %shard_map.434 = (bf16[4096,1024]{1,0:T(8,128)(2,1)}, f32[1,4096]{1,0:T(1,128)}, f32[1024,1024]{1,0:T(8,128)}, bf16[1024,1024]{1,0:T(8,128)(2,1)}, f32[8,1024]{1...) custom-call(bf16[1024,1024]{1,0:T(8,128)(2,1)} %refs_0_.3, ...), custom_call_target="tpu_custom_call" | custom-call | tf_op jit(solution)/shard_map/pallas_call | solution.py:673
  238.8 1.8 convert_element_type.58.refs_8_.refs_0_
  240.5 84.1 %shard_map.435 = (bf16[1024,1024]{1,0:T(8,128)(2,1)}, bf16[3,1024,1024]{2,1,0:T(8,128)(2,1)}, bf16[8,1024,384]{2,1,0:T(8,128)(2,1)}, f32[8,1024]{1,0:T(8,128)}, ...) custom-call(bf16[1024,1024]{1,0:T(8,128)(2,1)} %get-tuple-element.77.refs_0_, ...), custom_call_target="tpu_custom_call" | custom-call | tf_op jit(solution)/shard_map/pallas_call | solution.py:673
  324.7 1.1 convert_element_type.59.refs_0_
  325.7 0.0 copy-start.1
  325.8 0.8 pad_maximum_fusion.2.refs_14_
  326.6 100.0 %shard_map.436 = (f32[128,4096]{1,0:T(8,128)}, f32[32,1024]{1,0:T(8,128)}, f32[128,1024]{1,0:T(8,128)}, bf16[1024,1024]{1,0:T(8,128)(2,1)}, f32[8,1024]{1,0:T(8,...) custom-call(bf16[128,1024]{1,0:T(8,128)(2,1)} %convert_element_type.58.refs_8_.refs_0_, ...), custom_call_target="tpu_custom_call" | custom-call | tf_op jit(solution)/shard_map/pallas_call | solution.py:673
  426.5 0.8 add_convert_fusion
  427.3 0.1 reshape.83
  427.5 0.1 reshape.84
  427.6 0.1 convert_reduce_fusion
  427.7 0.7 copy.54
  428.4 1.0 convert_element_type.61.refs_0_
  429.4 0.0 copy-start.9
  429.4 1.0 convert_element_type.62.refs_0_
  430.4 0.7 pad_maximum_fusion.3.refs_11_
  431.1 53.8 %shard_map.437 = (f32[128,4096]{1,0:T(8,128)}, f32[32,1024]{1,0:T(8,128)}, f32[128,1024]{1,0:T(8,128)}, bf16[1024,1024]{1,0:T(8,128)(2,1)}, bf16[2,2,2,4,128,102...) custom-call(bf16[128,1024]{1,0:T(8,128)(2,1)} %copy-done.1, bf16[32,160,1024]{2,1,0:T(8,128)(2,1)} %bitcast.44, ...), custom_call_target="tpu_custom_call" | custom-call | tf_op jit(solution)/shard_map/pallas_call | solution.py:673
  484.9 6.1 %shard_map.439 = (f32[32,1024]{1,0:T(8,128)}, f32[32,1024]{1,0:T(8,128)}, f32[32,1024]{1,0:T(8,128)}) custom-call(bf16[32,1024]{1,0:T(8,128)(2,1)} %copy-done.12, bf16[32,128,1024]{2,1,0:T(8,128)(2,1)} %bitcast.46, f32[32,1024]{1,0:T(8,128)} %refs_2_.7, f32[32,1024]{1,0:T(8,128)} %refs_3_.7, f32[32,1024]{1,0:T(8,128)} %refs_4_.7, ...), custom_call_target="tpu_custom_call" | custom-call | tf_op jit(solution)/shard_map/pallas_call | solution.py:673
  491.2 12.5 %shard_map.438 = (f32[96,3072]{1,0:T(8,128)}, f32[32,1024]{1,0:T(8,128)}, f32[96,1024]{1,0:T(8,128)}) custom-call(bf16[96,1024]{1,0:T(8,128)(2,1)} %copy-done.9, bf16[32,128,1024]{2,1,0:T(8,128)(2,1)} %bitcast.47, f32[96,3072]{1,0:T(8,128)} %refs_2_.6, f32[96,3072]{1,0:T(8,128)} %refs_3_.6, f32[32,1024]{1,0:T(8,128)} %refs_4_.6, ...), custom_call_target="tpu_custom_call" | custom-call | tf_op jit(solution)/shard_map/pallas_call | solution.py:673
  503.7 1.0 copy.53
  504.7 0.7 slice_reduce_fusion
  505.4 0.1 squeeze_reshape.3
  505.5 0.6 multiply_subtract_fusion
  506.1 1.1 multiply_subtract_fusion.1
  507.2 1.0 copy.52
  508.2 1.3 copy.67
  509.5 1.0 copy-done.4
  510.5 1.3 copy.68
  511.9 0.7 copy.69
  512.6 0.7 copy.70
  513.3 0.8 copy.71
  514.1 0.7 copy.72
  514.7 1.3 copy.73
  516.1 1.0 copy-done.3
  517.1 1.3 copy.74
  518.4 0.7 copy.75
  519.1 0.8 copy.76
  (64 shorter events, 0.3 us)
Async XLA Ops:
  0.7 4.9 copy-start.2
  0.7 4.9 copy-start.16
  0.7 4.9 copy-start.17
  2.4 4.0 copy-start.22
  2.4 4.0 copy-start.11
  3.7 3.4 copy-start
  7.1 162.4 %copy-start.18 = (f32[32,1024]{1,0:T(8,128)S(1)}, f32[32,1024]{1,0:T(8,128)}, u32[]{:S(2)}) copy-start(f32[32,1024]{1,0:T(8,128)} %param.49) | copy-start | bytes 393220
  240.5 85.2 %copy-start.19 = (f32[32,1024]{1,0:T(8,128)S(1)}, f32[32,1024]{1,0:T(8,128)}, u32[]{:S(2)}) copy-start(f32[32,1024]{1,0:T(8,128)} %param.46) | copy-start | bytes 393220
  325.7 100.8 %copy-start.1 = (bf16[128,1024]{1,0:T(8,128)(2,1)}, bf16[128,1024]{1,0:T(8,128)(2,1)S(1)}, u32[]{:S(2)}) copy-start(bf16[128,1024]{1,0:T(8,128)(2,1)S(1)} %convert_element_type.59.refs_0_) | copy-start | bytes 786436
  326.6 100.0 %copy-start.23 = (f32[8,1024]{1,0:T(8,128)S(1)}, f32[8,1024]{1,0:T(8,128)}, u32[]{:S(2)}) copy-start(f32[8,1024]{1,0:T(8,128)} %get-tuple-element.97) | copy-start | bytes 98308
  326.6 101.0 %copy-start.26 = (f32[1,4096]{1,0:T(1,128)S(1)}, f32[1,4096]{1,0:T(1,128)}, u32[]{:S(2)}) copy-start(f32[1,4096]{1,0:T(1,128)} %get-tuple-element.99) | copy-start | bytes 49156
  429.4 55.5 %copy-start.9 = (bf16[96,1024]{1,0:T(8,128)(2,1)}, bf16[96,1024]{1,0:T(8,128)(2,1)S(1)}, u32[]{:S(2)}) copy-start(bf16[96,1024]{1,0:T(8,128)(2,1)S(1)} %convert_element_type.61.refs_0_) | copy-start | bytes 589828
  430.4 54.5 %copy-start.12 = (bf16[32,1024]{1,0:T(8,128)(2,1)}, bf16[32,1024]{1,0:T(8,128)(2,1)S(1)}, u32[]{:S(2)}) copy-start(bf16[32,1024]{1,0:T(8,128)(2,1)S(1)} %convert_element_type.62.refs_0_) | copy-start | bytes 196612
  491.1 12.6 %copy-start.14 = (f32[128,1024]{1,0:T(8,128)S(1)}, f32[128,1024]{1,0:T(8,128)}, u32[]{:S(2)}) copy-start(f32[128,1024]{1,0:T(8,128)} %get-tuple-element.114) | copy-start | bytes 1572868
  491.1 14.4 %copy-start.25 = (f32[8,32]{1,0:T(8,128)S(1)}, f32[8,32]{1,0:T(8,128)}, u32[]{:S(2)}) copy-start(f32[8,32]{1,0:T(8,128)} %param.32) | copy-start | bytes 3076
  491.1 14.4 %copy-start.27 = (f32[8,32]{1,0:T(8,128)S(1)}, f32[8,32]{1,0:T(8,128)}, u32[]{:S(2)}) copy-start(f32[8,32]{1,0:T(8,128)} %param.50) | copy-start | bytes 3076
  491.1 15.0 %copy-start.28 = (f32[128]{0:T(128)S(1)}, f32[128]{0:T(128)}, u32[]{:S(2)}) copy-start(f32[128]{0:T(128)} %param.33) | copy-start | bytes 1540
  491.1 15.0 %copy-start.29 = (f32[128]{0:T(128)S(1)}, f32[128]{0:T(128)}, u32[]{:S(2)}) copy-start(f32[128]{0:T(128)} %param.51) | copy-start | bytes 1540
  491.1 16.1 %copy-start.8 = (f32[128,1024]{1,0:T(8,128)S(1)}, f32[128,1024]{1,0:T(8,128)}, u32[]{:S(2)}) copy-start(f32[128,1024]{1,0:T(8,128)} %get-tuple-element.85) | copy-start | bytes 1572868
  503.7 4.5 copy-start.6
  505.5 4.0 copy-start.24
  508.2 2.3 copy-start.4
  510.5 1.3 copy-start.10
  510.5 2.1 copy-start.15
  510.5 2.7 copy-start.7
  510.5 3.5 copy-start.21
  511.9 2.9 copy-start.5
  514.7 2.3 copy-start.3
  517.1 1.3 copy-start.20
  517.1 2.0 copy-start.13

commit v5 on v4

--- a/solution.py
+++ b/solution.py
@@ -1308,7 +1308,7 @@
         product = dot_nn(n_root.astype(BF), full)
         new_w = weight - matrix_rate * dot_nt(product.astype(BF), m_root)
         return [new_n, new_m, new_w] + extra, [job.plainly() for job in jobs]
-    owners = 16 if rows == 32 else 4
+    owners = {32: 32, 96: 8}.get(rows, 4)
     size = owners * rows
     column = lambda array: block(array, (rows, size), lambda n: (0, n))
     own_ins = [

time: 521 us -> 527 us (1.012); the launches traced: 520 us -> 519 us
  no operation moved by 1% of the time
where the time goes in v5:
time: 527 us; the launch traced here: 519 us
  Pallas kernels  486 us (92%)
  local copies, waits for them, and re-layouts  17 us (3%)
  other arithmetic  14.3 us (3%)
    pallas_call x7, Pallas kernels, fused_call(): pl.pallas_call(kernel, grid=(steps,), out_shape=tuple((o[0] for o in outs...  486 us
    unnamed x74, local copies, waits for them, and re-layouts  15.8 us

profile of v5, /device:TPU:0, one launch (start us, length us, event | category | flops | bytes accessed | tf_op | source)
XLA Modules:
  0.0 518.5 jit_solution(10929292399644584630)
XLA Ops:
  0.7 0.8 convert_element_type.49
  1.5 0.2 dynamic_update_slice.6
  1.7 0.7 convert_bitcast_fusion
  2.4 1.3 copy.50
  3.7 0.0 copy-start
  3.7 1.1 bitcast_convert_fusion
  4.8 0.7 pad_maximum_fusion.1.refs_4_
  5.6 0.8 pad_maximum_fusion.refs_5_
  6.4 0.7 bitcast_convert_fusion.2.refs_3_
  7.1 162.4 %shard_map.433 = (bf16[3,1024,1024]{2,1,0:T(8,128)(2,1)}, bf16[1024,1024]{1,0:T(8,128)(2,1)}, f32[8,1,1024]{2,1,0:T(1,128)}, bf16[1024,1024]{1,0:T(8,128)(2,1)},...) custom-call(bf16[1024,1024]{1,0:T(8,128)(2,1)} %refs_11_.1, ...), custom_call_target="tpu_custom_call" | custom-call | tf_op jit(solution)/shard_map/pallas_call | solution.py:673
  169.5 0.6 convert_element_type.57.refs_8_
  170.2 68.8 %shard_map.434 = (bf16[4096,1024]{1,0:T(8,128)(2,1)}, f32[1,4096]{1,0:T(1,128)}, f32[1024,1024]{1,0:T(8,128)}, bf16[1024,1024]{1,0:T(8,128)(2,1)}, f32[8,1024]{1...) custom-call(bf16[1024,1024]{1,0:T(8,128)(2,1)} %refs_0_.3, ...), custom_call_target="tpu_custom_call" | custom-call | tf_op jit(solution)/shard_map/pallas_call | solution.py:673
  238.9 1.8 convert_element_type.58.refs_8_.refs_0_
  240.7 84.2 %shard_map.435 = (bf16[1024,1024]{1,0:T(8,128)(2,1)}, bf16[3,1024,1024]{2,1,0:T(8,128)(2,1)}, bf16[8,1024,384]{2,1,0:T(8,128)(2,1)}, f32[8,1024]{1,0:T(8,128)}, ...) custom-call(bf16[1024,1024]{1,0:T(8,128)(2,1)} %get-tuple-element.77.refs_0_, ...), custom_call_target="tpu_custom_call" | custom-call | tf_op jit(solution)/shard_map/pallas_call | solution.py:673
  325.0 1.1 convert_element_type.59.refs_0_
  326.1 0.0 copy-start.1
  326.1 0.8 pad_maximum_fusion.2.refs_14_
  326.9 100.0 %shard_map.436 = (f32[128,4096]{1,0:T(8,128)}, f32[32,1024]{1,0:T(8,128)}, f32[128,1024]{1,0:T(8,128)}, bf16[1024,1024]{1,0:T(8,128)(2,1)}, f32[8,1024]{1,0:T(8,...) custom-call(bf16[128,1024]{1,0:T(8,128)(2,1)} %convert_element_type.58.refs_8_.refs_0_, ...), custom_call_target="tpu_custom_call" | custom-call | tf_op jit(solution)/shard_map/pallas_call | solution.py:673
  426.9 0.8 add_convert_fusion
  427.6 0.1 reshape.83
  427.8 0.1 reshape.84
  427.9 0.1 convert_reduce_fusion
  428.0 0.7 copy.54
  428.7 1.0 convert_element_type.61.refs_0_
  429.8 1.0 convert_element_type.62.refs_0_
  430.8 0.7 pad_maximum_fusion.3.refs_11_
  431.5 53.8 %shard_map.437 = (f32[128,4096]{1,0:T(8,128)}, f32[32,1024]{1,0:T(8,128)}, f32[128,1024]{1,0:T(8,128)}, bf16[1024,1024]{1,0:T(8,128)(2,1)}, bf16[2,2,2,4,128,102...) custom-call(bf16[128,1024]{1,0:T(8,128)(2,1)} %copy-done.1, bf16[32,160,1024]{2,1,0:T(8,128)(2,1)} %bitcast.44, ...), custom_call_target="tpu_custom_call" | custom-call | tf_op jit(solution)/shard_map/pallas_call | solution.py:673
  485.3 6.0 %shard_map.439 = (f32[32,1024]{1,0:T(8,128)}, f32[32,1024]{1,0:T(8,128)}, f32[32,1024]{1,0:T(8,128)}) custom-call(bf16[32,1024]{1,0:T(8,128)(2,1)} %copy-done.12, bf16[32,128,1024]{2,1,0:T(8,128)(2,1)} %bitcast.46, f32[32,1024]{1,0:T(8,128)} %refs_2_.7, f32[32,1024]{1,0:T(8,128)} %refs_3_.7, f32[32,1024]{1,0:T(8,128)} %refs_4_.7, ...), custom_call_target="tpu_custom_call" | custom-call | tf_op jit(solution)/shard_map/pallas_call | solution.py:673
  491.3 0.0 copy-start.27
  491.4 10.5 %shard_map.438 = (f32[96,3072]{1,0:T(8,128)}, f32[32,1024]{1,0:T(8,128)}, f32[96,1024]{1,0:T(8,128)}) custom-call(bf16[96,1024]{1,0:T(8,128)(2,1)} %copy-done.9, bf16[32,128,1024]{2,1,0:T(8,128)(2,1)} %bitcast.47, f32[96,3072]{1,0:T(8,128)} %refs_2_.6, f32[96,3072]{1,0:T(8,128)} %refs_3_.6, f32[32,1024]{1,0:T(8,128)} %refs_4_.6, ...), custom_call_target="tpu_custom_call" | custom-call | tf_op jit(solution)/shard_map/pallas_call | solution.py:673
  501.9 1.0 copy.53
  502.9 0.7 slice_reduce_fusion
  503.6 0.1 squeeze_reshape.3
  503.7 0.6 multiply_subtract_fusion
  504.3 1.1 multiply_subtract_fusion.1
  505.4 1.0 copy.52
  506.4 1.3 copy.67
  507.7 1.0 copy-done.4
  508.8 1.3 copy.68
  510.1 0.7 copy.69
  510.8 0.7 copy.70
  511.5 0.8 copy.71
  512.3 0.7 copy.72
  513.0 1.3 copy.73
  514.3 1.0 copy-done.3
  515.3 1.3 copy.74
  516.6 0.7 copy.75
  517.3 0.8 copy.76
  (64 shorter events, 0.3 us)
Async XLA Ops:
  0.7 4.9 copy-start.2
  0.7 4.9 copy-start.16
  0.7 4.9 copy-start.17
  2.4 4.0 copy-start.22
  2.4 4.0 copy-start.11
  3.7 3.4 copy-start
  7.1 162.4 %copy-start.18 = (f32[32,1024]{1,0:T(8,128)S(1)}, f32[32,1024]{1,0:T(8,128)}, u32[]{:S(2)}) copy-start(f32[32,1024]{1,0:T(8,128)} %param.49) | copy-start | bytes 393220
  240.7 85.3 %copy-start.19 = (f32[32,1024]{1,0:T(8,128)S(1)}, f32[32,1024]{1,0:T(8,128)}, u32[]{:S(2)}) copy-start(f32[32,1024]{1,0:T(8,128)} %param.46) | copy-start | bytes 393220
  326.1 100.8 %copy-start.1 = (bf16[128,1024]{1,0:T(8,128)(2,1)}, bf16[128,1024]{1,0:T(8,128)(2,1)S(1)}, u32[]{:S(2)}) copy-start(bf16[128,1024]{1,0:T(8,128)(2,1)S(1)} %convert_element_type.59.refs_0_) | copy-start | bytes 786436
  326.9 100.0 %copy-start.23 = (f32[8,1024]{1,0:T(8,128)S(1)}, f32[8,1024]{1,0:T(8,128)}, u32[]{:S(2)}) copy-start(f32[8,1024]{1,0:T(8,128)} %get-tuple-element.97) | copy-start | bytes 98308
  326.9 101.0 %copy-start.26 = (f32[1,4096]{1,0:T(1,128)S(1)}, f32[1,4096]{1,0:T(1,128)}, u32[]{:S(2)}) copy-start(f32[1,4096]{1,0:T(1,128)} %get-tuple-element.99) | copy-start | bytes 49156
  429.8 55.5 %copy-start.9 = (bf16[96,1024]{1,0:T(8,128)(2,1)}, bf16[96,1024]{1,0:T(8,128)(2,1)S(1)}, u32[]{:S(2)}) copy-start(bf16[96,1024]{1,0:T(8,128)(2,1)S(1)} %convert_element_type.61.refs_0_) | copy-start | bytes 589828
  430.8 54.5 %copy-start.12 = (bf16[32,1024]{1,0:T(8,128)(2,1)}, bf16[32,1024]{1,0:T(8,128)(2,1)S(1)}, u32[]{:S(2)}) copy-start(bf16[32,1024]{1,0:T(8,128)(2,1)S(1)} %convert_element_type.62.refs_0_) | copy-start | bytes 196612
  491.3 10.6 %copy-start.14 = (f32[128,1024]{1,0:T(8,128)S(1)}, f32[128,1024]{1,0:T(8,128)}, u32[]{:S(2)}) copy-start(f32[128,1024]{1,0:T(8,128)} %get-tuple-element.114) | copy-start | bytes 1572868
  491.3 12.4 %copy-start.25 = (f32[8,32]{1,0:T(8,128)S(1)}, f32[8,32]{1,0:T(8,128)}, u32[]{:S(2)}) copy-start(f32[8,32]{1,0:T(8,128)} %param.32) | copy-start | bytes 3076
  491.3 12.4 %copy-start.27 = (f32[8,32]{1,0:T(8,128)S(1)}, f32[8,32]{1,0:T(8,128)}, u32[]{:S(2)}) copy-start(f32[8,32]{1,0:T(8,128)} %param.50) | copy-start | bytes 3076
  491.3 13.0 %copy-start.28 = (f32[128]{0:T(128)S(1)}, f32[128]{0:T(128)}, u32[]{:S(2)}) copy-start(f32[128]{0:T(128)} %param.33) | copy-start | bytes 1540
  491.4 13.0 %copy-start.29 = (f32[128]{0:T(128)S(1)}, f32[128]{0:T(128)}, u32[]{:S(2)}) copy-start(f32[128]{0:T(128)} %param.51) | copy-start | bytes 1540
  491.4 14.0 %copy-start.8 = (f32[128,1024]{1,0:T(8,128)S(1)}, f32[128,1024]{1,0:T(8,128)}, u32[]{:S(2)}) copy-start(f32[128,1024]{1,0:T(8,128)} %get-tuple-element.85) | copy-start | bytes 1572868
  501.9 4.5 copy-start.6
  503.7 4.0 copy-start.24
  506.4 2.3 copy-start.4
  508.8 1.3 copy-start.10
  508.8 2.1 copy-start.15
  508.8 2.7 copy-start.7
  508.8 3.5 copy-start.21
  510.1 2.9 copy-start.5
  513.0 2.3 copy-start.3
  515.3 1.3 copy-start.20
  515.3 2.0 copy-start.13

commit v6 on v4

--- a/solution.py
+++ b/solution.py
@@ -1346,7 +1346,7 @@
         collective_id,
         ticks=2 if part else 1,
         cost=(0, 1.6 + more[1], 1 + more[2]),
-        stagger=0.1 if len(jobs) > 2 else 36.0,
+        stagger=0.1 if len(jobs) > 2 else 14.0,
     )
 
 

time: 521 us -> 520 us (level)
  no operation moved by 1% of the time
where the time goes in v6:
time: 520 us; the launch traced here: 519 us
  Pallas kernels  487 us (94%)
  local copies, waits for them, and re-layouts  17 us (3%)
  other arithmetic  14.3 us (3%)
    pallas_call x7, Pallas kernels, fused_call(): pl.pallas_call(kernel, grid=(steps,), out_shape=tuple((o[0] for o in outs...  487 us
    unnamed x74, local copies, waits for them, and re-layouts  15.8 us

profile of v6, /device:TPU:0, one launch (start us, length us, event | category | flops | bytes accessed | tf_op | source)
XLA Modules:
  0.0 519.0 jit_solution(12502790137550298462)
XLA Ops:
  0.7 0.0 copy-start.2
  0.7 0.8 convert_element_type.49
  1.5 0.2 dynamic_update_slice.6
  1.7 0.7 convert_bitcast_fusion
  2.4 1.3 copy.50
  3.7 0.0 copy-start
  3.7 1.1 bitcast_convert_fusion
  4.8 0.7 pad_maximum_fusion.1.refs_4_
  5.6 0.8 pad_maximum_fusion.refs_5_
  6.4 0.7 bitcast_convert_fusion.2.refs_3_
  7.1 162.4 %shard_map.433 = (bf16[3,1024,1024]{2,1,0:T(8,128)(2,1)}, bf16[1024,1024]{1,0:T(8,128)(2,1)}, f32[8,1,1024]{2,1,0:T(1,128)}, bf16[1024,1024]{1,0:T(8,128)(2,1)},...) custom-call(bf16[1024,1024]{1,0:T(8,128)(2,1)} %refs_11_.1, ...), custom_call_target="tpu_custom_call" | custom-call | tf_op jit(solution)/shard_map/pallas_call | solution.py:673
  169.5 0.6 convert_element_type.57.refs_8_
  170.2 68.6 %shard_map.434 = (bf16[4096,1024]{1,0:T(8,128)(2,1)}, f32[1,4096]{1,0:T(1,128)}, f32[1024,1024]{1,0:T(8,128)}, bf16[1024,1024]{1,0:T(8,128)(2,1)}, f32[8,1024]{1...) custom-call(bf16[1024,1024]{1,0:T(8,128)(2,1)} %refs_0_.3, ...), custom_call_target="tpu_custom_call" | custom-call | tf_op jit(solution)/shard_map/pallas_call | solution.py:673
  238.8 1.8 convert_element_type.58.refs_8_.refs_0_
  240.5 84.1 %shard_map.435 = (bf16[1024,1024]{1,0:T(8,128)(2,1)}, bf16[3,1024,1024]{2,1,0:T(8,128)(2,1)}, bf16[8,1024,384]{2,1,0:T(8,128)(2,1)}, f32[8,1024]{1,0:T(8,128)}, ...) custom-call(bf16[1024,1024]{1,0:T(8,128)(2,1)} %get-tuple-element.77.refs_0_, ...), custom_call_target="tpu_custom_call" | custom-call | tf_op jit(solution)/shard_map/pallas_call | solution.py:673
  324.7 1.1 convert_element_type.59.refs_0_
  325.8 0.8 pad_maximum_fusion.2.refs_14_
  326.6 100.0 %shard_map.436 = (f32[128,4096]{1,0:T(8,128)}, f32[32,1024]{1,0:T(8,128)}, f32[128,1024]{1,0:T(8,128)}, bf16[1024,1024]{1,0:T(8,128)(2,1)}, f32[8,1024]{1,0:T(8,...) custom-call(bf16[128,1024]{1,0:T(8,128)(2,1)} %convert_element_type.58.refs_8_.refs_0_, ...), custom_call_target="tpu_custom_call" | custom-call | tf_op jit(solution)/shard_map/pallas_call | solution.py:673
  426.5 0.8 add_convert_fusion
  427.3 0.1 reshape.83
  427.5 0.1 reshape.84
  427.6 0.1 convert_reduce_fusion
  427.7 0.7 copy.54
  428.4 1.0 convert_element_type.61.refs_0_
  429.4 1.0 convert_element_type.62.refs_0_
  430.4 0.7 pad_maximum_fusion.3.refs_11_
  431.1 52.8 %shard_map.437 = (f32[128,4096]{1,0:T(8,128)}, f32[32,1024]{1,0:T(8,128)}, f32[128,1024]{1,0:T(8,128)}, bf16[1024,1024]{1,0:T(8,128)(2,1)}, bf16[2,2,2,4,128,102...) custom-call(bf16[128,1024]{1,0:T(8,128)(2,1)} %copy-done.1, bf16[32,160,1024]{2,1,0:T(8,128)(2,1)} %bitcast.44, ...), custom_call_target="tpu_custom_call" | custom-call | tf_op jit(solution)/shard_map/pallas_call | solution.py:673
  484.0 6.2 %shard_map.439 = (f32[32,1024]{1,0:T(8,128)}, f32[32,1024]{1,0:T(8,128)}, f32[32,1024]{1,0:T(8,128)}) custom-call(bf16[32,1024]{1,0:T(8,128)(2,1)} %copy-done.12, bf16[32,128,1024]{2,1,0:T(8,128)(2,1)} %bitcast.46, f32[32,1024]{1,0:T(8,128)} %refs_2_.7, f32[32,1024]{1,0:T(8,128)} %refs_3_.7, f32[32,1024]{1,0:T(8,128)} %refs_4_.7, ...), custom_call_target="tpu_custom_call" | custom-call | tf_op jit(solution)/shard_map/pallas_call | solution.py:673
  490.2 0.0 copy-start.27
  490.3 12.5 %shard_map.438 = (f32[96,3072]{1,0:T(8,128)}, f32[32,1024]{1,0:T(8,128)}, f32[96,1024]{1,0:T(8,128)}) custom-call(bf16[96,1024]{1,0:T(8,128)(2,1)} %copy-done.9, bf16[32,128,1024]{2,1,0:T(8,128)(2,1)} %bitcast.47, f32[96,3072]{1,0:T(8,128)} %refs_2_.6, f32[96,3072]{1,0:T(8,128)} %refs_3_.6, f32[32,1024]{1,0:T(8,128)} %refs_4_.6, ...), custom_call_target="tpu_custom_call" | custom-call | tf_op jit(solution)/shard_map/pallas_call | solution.py:673
  502.8 1.0 copy.53
  503.8 0.7 slice_reduce_fusion
  504.5 0.1 squeeze_reshape.3
  504.6 0.6 multiply_subtract_fusion
  505.2 1.1 multiply_subtract_fusion.1
  506.3 1.0 copy.52
  507.3 1.3 copy.67
  508.6 1.0 copy-done.4
  509.7 1.3 copy.68
  511.0 0.7 copy.69
  511.7 0.7 copy.70
  512.4 0.8 copy.71
  513.2 0.7 copy.72
  513.8 1.3 copy.73
  515.2 1.0 copy-done.3
  516.2 1.3 copy.74
  517.5 0.7 copy.75
  518.2 0.8 copy.76
  (64 shorter events, 0.3 us)
Async XLA Ops:
  0.7 4.9 copy-start.2
  0.7 4.9 copy-start.16
  0.7 4.9 copy-start.17
  2.4 4.0 copy-start.22
  2.4 4.0 copy-start.11
  3.7 3.4 copy-start
  7.1 162.4 %copy-start.18 = (f32[32,1024]{1,0:T(8,128)S(1)}, f32[32,1024]{1,0:T(8,128)}, u32[]{:S(2)}) copy-start(f32[32,1024]{1,0:T(8,128)} %param.49) | copy-start | bytes 393220
  240.5 85.2 %copy-start.19 = (f32[32,1024]{1,0:T(8,128)S(1)}, f32[32,1024]{1,0:T(8,128)}, u32[]{:S(2)}) copy-start(f32[32,1024]{1,0:T(8,128)} %param.46) | copy-start | bytes 393220
  325.7 100.8 %copy-start.1 = (bf16[128,1024]{1,0:T(8,128)(2,1)}, bf16[128,1024]{1,0:T(8,128)(2,1)S(1)}, u32[]{:S(2)}) copy-start(bf16[128,1024]{1,0:T(8,128)(2,1)S(1)} %convert_element_type.59.refs_0_) | copy-start | bytes 786436
  326.6 100.0 %copy-start.23 = (f32[8,1024]{1,0:T(8,128)S(1)}, f32[8,1024]{1,0:T(8,128)}, u32[]{:S(2)}) copy-start(f32[8,1024]{1,0:T(8,128)} %get-tuple-element.97) | copy-start | bytes 98308
  326.6 101.0 %copy-start.26 = (f32[1,4096]{1,0:T(1,128)S(1)}, f32[1,4096]{1,0:T(1,128)}, u32[]{:S(2)}) copy-start(f32[1,4096]{1,0:T(1,128)} %get-tuple-element.99) | copy-start | bytes 49156
  429.4 54.6 %copy-start.9 = (bf16[96,1024]{1,0:T(8,128)(2,1)}, bf16[96,1024]{1,0:T(8,128)(2,1)S(1)}, u32[]{:S(2)}) copy-start(bf16[96,1024]{1,0:T(8,128)(2,1)S(1)} %convert_element_type.61.refs_0_) | copy-start | bytes 589828
  430.4 53.6 %copy-start.12 = (bf16[32,1024]{1,0:T(8,128)(2,1)}, bf16[32,1024]{1,0:T(8,128)(2,1)S(1)}, u32[]{:S(2)}) copy-start(bf16[32,1024]{1,0:T(8,128)(2,1)S(1)} %convert_element_type.62.refs_0_) | copy-start | bytes 196612
  490.2 12.6 %copy-start.14 = (f32[128,1024]{1,0:T(8,128)S(1)}, f32[128,1024]{1,0:T(8,128)}, u32[]{:S(2)}) copy-start(f32[128,1024]{1,0:T(8,128)} %get-tuple-element.114) | copy-start | bytes 1572868
  490.2 14.4 %copy-start.25 = (f32[8,32]{1,0:T(8,128)S(1)}, f32[8,32]{1,0:T(8,128)}, u32[]{:S(2)}) copy-start(f32[8,32]{1,0:T(8,128)} %param.32) | copy-start | bytes 3076
  490.2 14.4 %copy-start.27 = (f32[8,32]{1,0:T(8,128)S(1)}, f32[8,32]{1,0:T(8,128)}, u32[]{:S(2)}) copy-start(f32[8,32]{1,0:T(8,128)} %param.50) | copy-start | bytes 3076
  490.2 15.0 %copy-start.28 = (f32[128]{0:T(128)S(1)}, f32[128]{0:T(128)}, u32[]{:S(2)}) copy-start(f32[128]{0:T(128)} %param.33) | copy-start | bytes 1540
  490.2 15.0 %copy-start.29 = (f32[128]{0:T(128)S(1)}, f32[128]{0:T(128)}, u32[]{:S(2)}) copy-start(f32[128]{0:T(128)} %param.51) | copy-start | bytes 1540
  490.2 16.1 %copy-start.8 = (f32[128,1024]{1,0:T(8,128)S(1)}, f32[128,1024]{1,0:T(8,128)}, u32[]{:S(2)}) copy-start(f32[128,1024]{1,0:T(8,128)} %get-tuple-element.85) | copy-start | bytes 1572868
  502.8 4.5 copy-start.6
  504.6 4.0 copy-start.24
  507.3 2.3 copy-start.4
  509.6 1.3 copy-start.10
  509.6 2.1 copy-start.15
  509.6 2.7 copy-start.7
  509.7 3.5 copy-start.21
  511.0 2.9 copy-start.5
  513.8 2.3 copy-start.3
  516.2 1.3 copy-start.20
  516.2 2.0 copy-start.13
